TPU v7x, 1024 devices: a whole 4x4x32 slice. The times are simulated.
1024 devices in a mesh: dp: 16 (over x, z_hi, core), tensor: 64 (over y, z_lo).
Axes of the slice: x: 4, y: 4, z: 32 (z_hi: 2, z_lo: 16; z = z_hi * 16 + z_lo), core: 2. Of those that a mesh axis runs over, the one named last changes fastest.
Arguments:
- activations: bfloat16 [2048, 29696], P('dp', 'tensor'), may hold values from -6 to 6
- weight_codes: bfloat16 [29696, 7424], P('tensor'), may hold values from -127 to 127, as said below
- channel_scale: float32 [7424], replicated, may hold values from 0.0013130644 to 0.013130643
- output_grads: bfloat16 [2048, 7424], P('dp', 'tensor'), may hold values from -0.375 to 0.375
Outputs:
- input_grads: float32 [2048, 29696], P('dp', 'tensor')
- weight_grads: float32 [29696, 7424], P('tensor', 'dp')
Inputs may be any that keep to these rules, and one draw needn't show every extreme that they name: weight_codes holds whole numbers.
All inputs are finite; a program needn't handle non-finite values.
Results may differ from a plain program's by a relative error of at most 0.0029.
Values may be sent and summed in bfloat16 or wider, within the bound.
No kernel may reach another device: no remote copies, remote signals or barrier semaphores. Data moves between devices by JAX's collectives and lax.ppermute only.
A program may use at most 64 MiB of HBM per device.

v0:
```python
import jax
import jax.numpy as jnp
from jax import lax
from jax.sharding import PartitionSpec as P


def per_device(activations, weight_codes, channel_scale, output_grads):
    full_rows = lax.all_gather(output_grads, "tensor", axis=1, tiled=True)
    scaled = (full_rows.astype(jnp.float32) * channel_scale).astype(jnp.bfloat16)
    input_grads = lax.dot_general(
        scaled, weight_codes, (((1,), (1,)), ((), ())), preferred_element_type=jnp.float32
    )
    grad_columns = lax.all_to_all(full_rows, "dp", split_axis=1, concat_axis=0, tiled=True)
    weight_grads = lax.dot_general(
        lax.all_gather(activations, "dp", axis=0, tiled=True),
        grad_columns,
        (((0,), (0,)), ((), ())),
        preferred_element_type=jnp.float32,
    )
    return (input_grads, weight_grads)


def solution(mesh):
    placed = (P("dp", "tensor"), P("tensor", None), P(), P("dp", "tensor"))
    return jax.shard_map(
        per_device,
        mesh=mesh,
        in_specs=placed,
        out_specs=(P("dp", "tensor"), P("tensor", "dp")),
        check_vma=False,
    )
```

profile of v0, /device:TPU:1, one launch (start us, length us, event | category | flops | bytes accessed | tf_op | source)
XLA Modules:
  0.0 1048.8 jit_solution(18111356878201526585)
XLA Ops:
  8.0 0.0 all-gather.6.cloned.1.call-start
  8.0 0.7 all-gather.6.cloned.1.call-update
  8.7 676.6 %all-gather.6.cloned.1.call-done = bf16[64,116,128]{2,1,0:T(8,128)(2,1)} async-done(((bf16[1,116,128]{2,1,0:T(8,128)(2,1)}), bf16[64,116,128]{2,1,0:T(8,128)(2,1)}) %all-gather.6.cloned.1.call-update) | async-done | bytes 1900560 | tf_op jit(solution)/shard_map/all_gather | solution.py:8
  685.3 3.7 reshape.9
  689.0 0.0 copy-start
  689.0 203.1 %all-to-all-start = ((bf16[128,16,464]{0,2,1:T(8,128)(2,1)}), bf16[128,16,464]{0,2,1:T(8,128)(2,1)S(1)}, u32[]{:S(2)}, u32[]{:S(2)}) async-start(bf16[128,16,464]{0,2,1:T(8,128)(2,1)} %bitcast.3), calls=%async_computation | async-start | bytes 3801088 | tf_op jit(solution)/shard_map/all_to_all | solution.py:13
  892.1 0.0 all-gather.4.cloned.1.call-start
  892.1 0.5 all-gather.4.cloned.1.call-update
  892.7 0.0 copy-done
  892.7 6.2 fusion
  898.9 138.8 %all-gather.4.cloned.1.call-done = bf16[2048,464]{0,1:T(8,128)(2,1)} async-done(((bf16[128,464]{0,1:T(8,128)(2,1)}), bf16[2048,464]{0,1:T(8,128)(2,1)}) %all-gather.4.cloned.1.call-update) | async-done | bytes 1900560 | tf_op jit(solution)/shard_map/all_gather | solution.py:15
  1037.7 0.0 all-to-all-done
  1037.7 3.6 fusion.1
Async XLA Ops:
  8.0 677.3 %all-gather.6.cloned.1.call-start = ((), (), s32[]{:S(2)}) async-start(), calls=%async_computation.2 | async-start | bytes 1996800 | tf_op jit(solution)/shard_map/all_gather | solution.py:8
  689.0 203.7 %copy-start = (f32[7424]{0:T(1024)S(1)}, f32[7424]{0:T(1024)}, u32[]{:S(2)}) copy-start(f32[7424]{0:T(1024)} %param.6) | copy-start | bytes 89092
  689.0 348.7 %all-to-all-start = ((bf16[128,16,464]{0,2,1:T(8,128)(2,1)}), bf16[128,16,464]{0,2,1:T(8,128)(2,1)S(1)}, u32[]{:S(2)}, u32[]{:S(2)}) async-start(bf16[128,16,464]{0,2,1:T(8,128)(2,1)} %bitcast.3), calls=%async_computation | async-start | bytes 3801088 | tf_op jit(solution)/shard_map/all_to_all | solution.py:13
  892.1 145.6 %all-gather.4.cloned.1.call-start = ((), (), s32[]{:S(2)}) async-start(), calls=%async_computation.1 | async-start | bytes 2019328 | tf_op jit(solution)/shard_map/all_gather | solution.py:15
Sparse Core Ops, SparseCore 0:
  11.5 673.7 all-gather.5
Sparse Core Ops, SparseCore 1:
  896.9 140.8 all-gather.3
where the time goes:
time: 1050 us
  waiting for transfers between devices  817 us (78%)
  starting transfers between devices  203 us (19%)
  between operations  15.5 us (1%)
    all_gather x1, waiting for transfers between devices, per_device(): full_rows = lax.all_gather(output_grads, 'tensor', axis=1, tiled=True)  677 us
    all_to_all x1, starting transfers between devices, per_device(): lax.all_to_all(full_rows, 'dp', split_axis=1, concat_axis=0, tiled=True)  203 us
    all_gather x1, waiting for transfers between devices, per_device(): lax.all_gather(activations, 'dp', axis=0, tiled=True)  139 us
  transfers between devices with their start and end apart: 3, of which 2 were waited for; matrix products, arithmetic and copies ran while one was open for 1% of the time, Pallas kernels for 0%

commit v1 on v0

v1 whole, which is shorter than its diff:
```python
import itertools

import jax
import jax.numpy as jnp
import numpy as np
from jax import lax
from jax.sharding import Mesh, PartitionSpec as P

AXES = ("x", "zh", "c", "y", "za", "zb")
SIZES = (4, 2, 2, 4, 4, 4)
DP = ("x", "zh", "c")
TENSOR = ("y", "za", "zb")


def permute(value, axes, target):
    sizes = [SIZES[AXES.index(a)] for a in axes]
    pairs = []
    for place in itertools.product(*map(range, sizes)):
        to = target(*place)
        pairs.append((int(np.ravel_multi_index(place, sizes)), int(np.ravel_multi_index(to, sizes))))
    return lax.ppermute(value, axes, pairs)


def spread(value, axis):
    n = SIZES[AXES.index(axis)]
    copies = jnp.broadcast_to(value[None], (n,) + value.shape)
    return lax.all_to_all(copies, axis, 0, 0, tiled=True)


def per_device(activations, weight_codes, channel_scale, output_grads):
    a = activations.T
    g = output_grads.T
    units, tokens = a.shape
    cols = g.shape[0]

    other = permute(a, ("zh",), lambda h: (1 - h,))
    moved = permute(g, AXES, lambda x, zh, c, y, za, zb: (y, za // 2, za % 2, x, zb, 2 * zh + c))

    me = lax.axis_index(TENSOR)
    scale = lax.dynamic_slice(channel_scale, (me * cols,), (cols,))
    scaled = (g.astype(jnp.float32) * scale[:, None]).astype(jnp.bfloat16)

    both = spread(jnp.stack([scaled, moved]), "za")
    rows = both[:, 0].reshape(4 * cols, tokens)
    part = both[:, 1].reshape(4 * cols, tokens)
    both = spread(jnp.concatenate([rows, part]), "zb")
    rows = both[:, : 4 * cols].reshape(4, 4, cols, tokens).transpose(1, 0, 2, 3).reshape(16 * cols, tokens)
    part = both[:, 4 * cols :].reshape(16 * cols, tokens)
    both = spread(jnp.concatenate([rows, part]), "y")
    rows = both[:, : 16 * cols].reshape(64 * cols, tokens)
    part = both[:, 16 * cols :].reshape(16, 4 * cols, tokens)

    input_grads = lax.dot_general(weight_codes, rows, (((1,), (0,)), ((), ())), preferred_element_type=jnp.float32)

    first = lax.axis_index("zh") == 0
    pair = jnp.where(first, jnp.stack([a, other]), jnp.stack([other, a]))
    acts = spread(spread(pair, "x"), "c").transpose(1, 2, 0, 3, 4).reshape(16, units, tokens)
    weight_grads = lax.dot_general(acts, part, (((0, 2), (0, 2)), ((), ())), preferred_element_type=jnp.float32)
    return input_grads.T, weight_grads


def solution(mesh):
    fine = Mesh(mesh.devices.reshape(SIZES), AXES)
    placed = (P(DP, TENSOR), P(TENSOR, None), P(), P(DP, TENSOR))
    return jax.shard_map(
        per_device,
        mesh=fine,
        in_specs=placed,
        out_specs=(P(DP, TENSOR), P(TENSOR, DP)),
        check_vma=False,
    )
```

time: 1050 us -> 208 us (0.20)
  waiting for transfers between devices: 817 us -> 60.2 us
  starting transfers between devices: 203 us -> 69.9 us
  blocking collectives: 0 us -> 49.7 us
  between operations: 15.5 us -> 0.77 us
    all_gather x2 -> x0, waiting for transfers between devices: 815 us -> none  [the longest x1 677 us: per_device(): full_rows = lax.all_gather(output_grads, 'tensor', axis=1, tiled=True)]
    all_to_all x1 -> x4, starting transfers between devices: 203 us -> 41 us  [spread(): return lax.all_to_all(copies, axis, 0, 0, tiled=True)]
    all_to_all x1 -> x4, waiting for transfers between devices: 0.01 us -> 51 us  [spread(): return lax.all_to_all(copies, axis, 0, 0, tiled=True)]
    all_to_all x0 -> x1, blocking collectives: none -> 49.7 us  [spread(): return lax.all_to_all(copies, axis, 0, 0, tiled=True)]
    ppermute x0 -> x2, starting transfers between devices: none -> 29 us  [permute(): return lax.ppermute(value, axes, pairs)]
  transfers between devices with their start and end apart: 3 -> 6, of which waited for: 2 -> 5; matrix products, arithmetic and copies ran while one was open for 1% -> 4% of each run, Pallas kernels for 0% -> 0%
where the time goes in v1:
time: 208 us; the launch traced here: 204 us
  starting transfers between devices  69.9 us (34%)
  waiting for transfers between devices  60.2 us (29%)
  blocking collectives  49.7 us (24%)
  local copies, waits for them, and re-layouts  12.9 us (6%)
  matrix products  7.72 us (4%)
  other arithmetic  2.95 us (1%)
    all_to_all x4, waiting for transfers between devices, spread(): return lax.all_to_all(copies, axis, 0, 0, tiled=True)  51 us
    all_to_all x1, blocking collectives, spread(): return lax.all_to_all(copies, axis, 0, 0, tiled=True)  49.7 us
    all_to_all x4, starting transfers between devices, spread(): return lax.all_to_all(copies, axis, 0, 0, tiled=True)  41 us
    ppermute x2, starting transfers between devices, permute(): return lax.ppermute(value, axes, pairs)  29 us
    ppermute x2, waiting for transfers between devices, permute(): return lax.ppermute(value, axes, pairs)  9.22 us
    broadcast_in_dim x5, local copies, waits for them, and re-layouts, spread(): copies = jnp.broadcast_to(value[None], (n,) + value.shape)  5.88 us
    dot_general x1, matrix products, per_device(): lax.dot_general(weight_codes, rows, (((1,), (0,)), ((), ())), preferred_e...  5.61 us
  transfers between devices with their start and end apart: 6, of which 5 were waited for; matrix products, arithmetic and copies ran while one was open for 4% of the time, Pallas kernels for 0%

profile of v1, /device:TPU:1, one launch (start us, length us, event | category | flops | bytes accessed | tf_op | source)
XLA Modules:
  0.0 204.2 jit_solution(9789271310109038670)
XLA Ops:
  0.6 4.9 %collective-permute-start = (bf16[116,128]{1,0:T(8,128)(2,1)}, bf16[116,128]{1,0:T(8,128)(2,1)S(1)}, u32[]{:S(2)}, u32[]{:S(2)}) collective-permute-start(bf16[116,128]{1,0:T(8,128)(2,1)} %bitcast.30), channel_id=1, source_target_pairs={{0,0},{1,4},{2,8},{3,12},{4,64},{5,68},{6,72},{7,76},{8,128},{9,13... | collective-permute-start | bytes 89096 | tf_op jit(solution)/shard_map/ppermute | solution.py:21
  5.6 0.8 dynamic_slice.3
  6.4 0.8 fusion
  7.2 5.4 %collective-permute-done = bf16[116,128]{1,0:T(8,128)(2,1)S(1)} collective-permute-done((bf16[116,128]{1,0:T(8,128)(2,1)}, bf16[116,128]{1,0:T(8,128)(2,1)S(1)}, u32[]{:S(2)}, u32[]{:S(2)}) %collective-permute-start) | collective-permute-done | bytes 29728 | tf_op jit(solution)/shard_map/ppermute | solution.py:21
  12.7 0.8 broadcast_in_dim.10
  13.5 21.8 %all-to-all-start = ((bf16[4,2,116,128]{3,1,2,0:T(2,128)(2,1)}), bf16[4,2,116,128]{3,1,2,0:T(2,128)(2,1)S(1)}, u32[]{:S(2)}, u32[]{:S(2)}) async-start(bf16[4,2,116,128]{3,1,2,0:T(2,128)(2,1)} %broadcast_in_dim.10), calls=%async_computation | async-start | bytes 475136 | tf_op jit(solution)/shard_map/all_to_all | solution.py:27
  35.3 24.0 %collective-permute-start.1 = (bf16[464,128]{1,0:T(8,128)(2,1)}, bf16[464,128]{1,0:T(8,128)(2,1)S(1)}, u32[]{:S(2)}, u32[]{:S(2)}) collective-permute-start(bf16[464,128]{1,0:T(8,128)(2,1)} %bitcast.27), channel_id=1, source_target_pairs={{0,128},{128,0},{1,129},{129,1},{2,130},{130,2},{3,131},{131,3},{4... | collective-permute-start | bytes 356360 | tf_op jit(solution)/shard_map/ppermute | solution.py:21
  59.3 3.8 %collective-permute-done.1 = bf16[464,128]{1,0:T(8,128)(2,1)S(1)} collective-permute-done((bf16[464,128]{1,0:T(8,128)(2,1)}, bf16[464,128]{1,0:T(8,128)(2,1)S(1)}, u32[]{:S(2)}, u32[]{:S(2)}) %collective-permute-start.1) | collective-permute-done | bytes 118816 | tf_op jit(solution)/shard_map/ppermute | solution.py:21
  63.1 1.0 maximum_select_fusion
  64.1 0.0 all-to-all-done
  64.1 1.1 broadcast_in_dim.13
  65.2 8.7 %all-to-all-start.3 = ((bf16[4,2,464,128]{3,2,1,0:T(8,128)(2,1)}), bf16[4,2,464,128]{3,2,1,0:T(8,128)(2,1)S(1)}, u32[]{:S(2)}, u32[]{:S(2)}) async-start(bf16[4,2,464,128]{3,2,1,0:T(8,128)(2,1)} %broadcast_in_dim.13), calls=%async_computation.3 | async-start | bytes 1900544 | tf_op jit(solution)/shard_map/all_to_all | solution.py:27
  73.9 1.2 slice_reduce_fusion.1
  75.2 7.9 %all-to-all-done.3 = bf16[4,2,464,128]{3,2,1,0:T(8,128)(2,1)S(1)} async-done(((bf16[4,2,464,128]{3,2,1,0:T(8,128)(2,1)}), bf16[4,2,464,128]{3,2,1,0:T(8,128)(2,1)S(1)}, u32[]{:S(2)}, u32[]{:S(2)}) %all-to-all-start.3) | async-done | bytes 950304 | tf_op jit(solution)/shard_map/all_to_all | solution.py:27
  83.1 0.1 broadcast_in_dim.11
  83.2 49.7 %all_to_all.25 = bf16[4,928,128]{2,1,0:T(8,128)(2,1)S(1)} all-to-all(bf16[4,928,128]{2,1,0:T(8,128)(2,1)S(1)} %broadcast_in_dim.11), channel_id=1, replica_groups=mesh['x'=4,'zh'=2,'c'=2,'y'=4,'za'=4,'zb'=4] {'zb'}, dimensions={0} | all-to-all | bytes 1900544 | tf_op jit(solution)/shard_map/all_to_all | solution.py:27
  132.9 1.5 broadcast_in_dim.14
  134.4 5.7 %all-to-all-start.4 = ((bf16[2,4,2,464,128]{4,3,2,1,0:T(8,128)(2,1)}), bf16[2,4,2,464,128]{4,3,2,1,0:T(8,128)(2,1)S(1)}, u32[]{:S(2)}, u32[]{:S(2)}) async-start(bf16[2,4,2,464,128]{4,3,2,1,0:T(8,128)(2,1)} %broadcast_in_dim.14), calls=%async_computation.4 | async-start | bytes 3801088 | tf_op jit(solution)/shard_map/all_to_all | solution.py:27
  140.2 0.8 fusion.2
  141.0 0.1 reshape.60
  141.1 0.1 reshape.61
  141.2 1.1 pad_maximum_fusion
  142.3 0.2 all-to-all-done.4
  142.5 2.4 %broadcast_in_dim.12 = bf16[4,3712,128]{2,1,0:T(8,128)(2,1)} broadcast(bf16[3712,128]{1,0:T(8,128)(2,1)S(1)} %pad_maximum_fusion), dimensions={1,2} | broadcast | bytes 4751360 | tf_op jit(solution)/shard_map/broadcast_in_dim | solution.py:26
  144.9 4.8 %all-to-all-start.2 = ((bf16[4,3712,128]{2,1,0:T(8,128)(2,1)}), bf16[4,3712,128]{2,1,0:T(8,128)(2,1)}, u32[]{:S(2)}, u32[]{:S(2)}) async-start(bf16[4,3712,128]{2,1,0:T(8,128)(2,1)} %broadcast_in_dim.12), calls=%async_computation.2 | async-start | bytes 7602176 | tf_op jit(solution)/shard_map/all_to_all | solution.py:27
  149.7 1.5 copy.10
  151.1 0.0 copy-start
  151.1 42.9 %all-to-all-done.2 = bf16[4,3712,128]{2,1,0:T(8,128)(2,1)} async-done(((bf16[4,3712,128]{2,1,0:T(8,128)(2,1)}), bf16[4,3712,128]{2,1,0:T(8,128)(2,1)}, u32[]{:S(2)}, u32[]{:S(2)}) %all-to-all-start.2) | async-done | bytes 3801120 | tf_op jit(solution)/shard_map/all_to_all | solution.py:27
  194.1 2.4 %fusion.1 = (bf16[4,1856,128]{2,1,0:T(8,128)(2,1)S(1)}, bf16[4,1856,128]{2,1,0:T(8,128)(2,1)S(1)}) fusion(bf16[4,3712,128]{2,1,0:T(8,128)(2,1)} %all-to-all-done.2), kind=kLoop, calls=%fused_computation.9 | loop fusion | bytes 7602176 | tf_op jit(solution)/shard_map/slice | solution.py:51
  196.4 0.0 copy-done
  196.5 2.1 %convolution_bitcast_fusion = f32[464,464]{1,0:T(8,128)} fusion(bf16[16,464,128]{2,1,0:T(8,128)(2,1)S(1)} %bitcast.23, bf16[16,464,128]{2,1,0:T(8,128)(2,1)S(1)} %bitcast.25), kind=kOutput, calls=%fused_computation | convolution fusion | flops 881852416 | bytes 4662272 | tf_op jit(solution)/shard_map/dot_general | solution.py:58
  198.6 5.6 %fusion.3 = f32[128,464]{0,1:T(8,128)} fusion(bf16[464,7424]{1,0:T(8,128)(2,1)} %param.5, bf16[7424,128]{1,0:T(8,128)(2,1)S(1)} %bitcast.24), kind=kOutput, calls=%fused_computation.11 | convolution fusion | flops 881852416 | bytes 9027584 | tf_op jit(solution)/shard_map/dot_general | solution.py:53
  (6 shorter events, 0.2 us)
Async XLA Ops:
  0.6 12.0 %collective-permute-start = (bf16[116,128]{1,0:T(8,128)(2,1)}, bf16[116,128]{1,0:T(8,128)(2,1)S(1)}, u32[]{:S(2)}, u32[]{:S(2)}) collective-permute-start(bf16[116,128]{1,0:T(8,128)(2,1)} %bitcast.30), channel_id=1, source_target_pairs={{0,0},{1,4},{2,8},{3,12},{4,64},{5,68},{6,72},{7,76},{8,128},{9,13... | collective-permute-start | bytes 89096 | tf_op jit(solution)/shard_map/ppermute | solution.py:21
  13.5 50.6 %all-to-all-start = ((bf16[4,2,116,128]{3,1,2,0:T(2,128)(2,1)}), bf16[4,2,116,128]{3,1,2,0:T(2,128)(2,1)S(1)}, u32[]{:S(2)}, u32[]{:S(2)}) async-start(bf16[4,2,116,128]{3,1,2,0:T(2,128)(2,1)} %broadcast_in_dim.10), calls=%async_computation | async-start | bytes 475136 | tf_op jit(solution)/shard_map/all_to_all | solution.py:27
  35.3 27.9 %collective-permute-start.1 = (bf16[464,128]{1,0:T(8,128)(2,1)}, bf16[464,128]{1,0:T(8,128)(2,1)S(1)}, u32[]{:S(2)}, u32[]{:S(2)}) collective-permute-start(bf16[464,128]{1,0:T(8,128)(2,1)} %bitcast.27), channel_id=1, source_target_pairs={{0,128},{128,0},{1,129},{129,1},{2,130},{130,2},{3,131},{131,3},{4... | collective-permute-start | bytes 356360 | tf_op jit(solution)/shard_map/ppermute | solution.py:21
  65.2 17.9 %all-to-all-start.3 = ((bf16[4,2,464,128]{3,2,1,0:T(8,128)(2,1)}), bf16[4,2,464,128]{3,2,1,0:T(8,128)(2,1)S(1)}, u32[]{:S(2)}, u32[]{:S(2)}) async-start(bf16[4,2,464,128]{3,2,1,0:T(8,128)(2,1)} %broadcast_in_dim.13), calls=%async_computation.3 | async-start | bytes 1900544 | tf_op jit(solution)/shard_map/all_to_all | solution.py:27
  134.4 8.1 %all-to-all-start.4 = ((bf16[2,4,2,464,128]{4,3,2,1,0:T(8,128)(2,1)}), bf16[2,4,2,464,128]{4,3,2,1,0:T(8,128)(2,1)S(1)}, u32[]{:S(2)}, u32[]{:S(2)}) async-start(bf16[2,4,2,464,128]{4,3,2,1,0:T(8,128)(2,1)} %broadcast_in_dim.14), calls=%async_computation.4 | async-start | bytes 3801088 | tf_op jit(solution)/shard_map/all_to_all | solution.py:27
  144.9 49.2 %all-to-all-start.2 = ((bf16[4,3712,128]{2,1,0:T(8,128)(2,1)}), bf16[4,3712,128]{2,1,0:T(8,128)(2,1)}, u32[]{:S(2)}, u32[]{:S(2)}) async-start(bf16[4,3712,128]{2,1,0:T(8,128)(2,1)} %broadcast_in_dim.12), calls=%async_computation.2 | async-start | bytes 7602176 | tf_op jit(solution)/shard_map/all_to_all | solution.py:27
  151.1 45.3 %copy-start = (bf16[4,2,2,464,128]{4,3,2,1,0:T(8,128)(2,1)S(1)}, bf16[4,2,2,464,128]{4,3,2,1,0:T(8,128)(2,1)}, u32[]{:S(2)}) copy-start(bf16[4,2,2,464,128]{4,3,2,1,0:T(8,128)(2,1)} %copy.10) | copy-start | bytes 5701636

commit v2 on v1

v2 whole, which is shorter than its diff:
```python
import itertools

import jax
import jax.numpy as jnp
import numpy as np
from jax import lax
from jax.sharding import Mesh, PartitionSpec as P

AXES = ("x", "zh", "c", "y", "za", "zb")
SIZES = (4, 2, 2, 4, 4, 4)
DP = ("x", "zh", "c")
TENSOR = ("y", "za", "zb")


def permute(value, axes, target):
    sizes = [SIZES[AXES.index(a)] for a in axes]
    pairs = []
    for place in itertools.product(*map(range, sizes)):
        to = target(*place)
        pairs.append((int(np.ravel_multi_index(place, sizes)), int(np.ravel_multi_index(to, sizes))))
    return lax.ppermute(value, axes, pairs)


def along_z(value, step):
    def target(zh, za, zb):
        z = (zh * 16 + za * 4 + zb + step) % 32
        return (z // 16, z % 16 // 4, z % 4)

    return permute(value, ("zh", "za", "zb"), target)


def along_y(value, step):
    return permute(value, ("y",), lambda y: ((y + step) % 4,))


def spread(value, axis):
    n = SIZES[AXES.index(axis)]
    copies = jnp.broadcast_to(value[None], (n,) + value.shape)
    return lax.all_to_all(copies, axis, 0, 0, tiled=True)


def around(own, ahead, opposite, behind):
    y = lax.axis_index("y")
    ring = jnp.broadcast_to(own[None], (4,) + own.shape)
    for k, block in ((1, ahead), (2, opposite), (3, behind)):
        ring = lax.dynamic_update_slice(ring, block[None], ((y + k) % 4, 0, 0))
    return ring


sync = lax.optimization_barrier


def per_device(activations, weight_codes, channel_scale, output_grads):
    a = activations.T
    g = output_grads.T
    units, tokens = a.shape
    cols = g.shape[0]
    cut = units // 2 // 16 * 16
    half = 8 * cols

    me = lax.axis_index(TENSOR)
    scale = lax.dynamic_slice(channel_scale, (me * cols,), (cols,))
    scaled = (g.astype(jnp.float32) * scale[:, None]).astype(jnp.bfloat16)

    part = permute(g, AXES, lambda x, zh, c, y, za, zb: (y, za // 2, za % 2, x, zb, 2 * zh + c))
    rows = spread(scaled, "za").reshape(4 * cols, tokens)
    low = along_z(a[:cut], -1)
    part, rows, low = sync((part, rows, low))

    rows = spread(rows, "zb")
    part = spread(part, "za").reshape(4 * cols, tokens)
    other = jnp.concatenate([along_z(low, -15), along_z(a[cut:], 16)])
    acts = spread(a, "x")
    rows = rows.reshape(4, 4, cols, tokens).transpose(1, 0, 2, 3).reshape(16 * cols, tokens)
    rows, part, other, acts = sync((rows, part, other, acts))

    rows_b, rows_a = along_y(rows, 1), along_y(rows, -1)
    part = spread(part, "zb").reshape(16 * cols, tokens)
    rows_b, rows_a, part, other = sync((rows_b, rows_a, part, other))

    up = along_y(jnp.concatenate([rows_b[:half], part]), 1)
    down = along_y(jnp.concatenate([rows_a[half:], part]), -1)
    acts_o = spread(other, "x")
    up, down, acts_o = sync((up, down, acts_o))
    rows_o = jnp.concatenate([up[:half], down[:half]])
    part_b, part_a = up[half:], down[half:]

    part_o = jnp.concatenate([along_y(part_b[:half], 1), along_y(part_a[half:], -1)])
    first = lax.axis_index("zh") == 0
    acts = jnp.where(first, jnp.stack([acts, acts_o], 1), jnp.stack([acts_o, acts], 1))
    acts_c = permute(acts, ("c",), lambda c: (1 - c,))
    first = lax.axis_index("c") == 0
    acts = jnp.where(first, jnp.stack([acts, acts_c], 2), jnp.stack([acts_c, acts], 2)).reshape(16, units, tokens)

    rows = around(rows, rows_a, rows_o, rows_b).reshape(64 * cols, tokens)
    input_grads = lax.dot_general(weight_codes, rows, (((1,), (0,)), ((), ())), preferred_element_type=jnp.float32)
    part = around(part, part_a, part_o, part_b).reshape(16, 4 * cols, tokens)
    weight_grads = lax.dot_general(acts, part, (((0, 2), (0, 2)), ((), ())), preferred_element_type=jnp.float32)
    return input_grads.T, weight_grads


def solution(mesh):
    fine = Mesh(mesh.devices.reshape(SIZES), AXES)
    placed = (P(DP, TENSOR), P(TENSOR, None), P(), P(DP, TENSOR))
    return jax.shard_map(
        per_device,
        mesh=fine,
        in_specs=placed,
        out_specs=(P(DP, TENSOR), P(TENSOR, DP)),
        check_vma=False,
    )
```

time: 208 us -> 221 us (1.062); the launches traced: 204 us -> 220 us
  starting transfers between devices: 69.9 us -> 108 us
  waiting for transfers between devices: 60.2 us -> 45 us
  blocking collectives: 49.7 us -> 44.1 us
    all_to_all x4, waiting for transfers between devices: 51 us -> 5.02 us  [spread(): return lax.all_to_all(copies, axis, 0, 0, tiled=True)]
    ppermute x2 -> x11, starting transfers between devices: 29 us -> 65.6 us  [permute(): return lax.ppermute(value, axes, pairs)]
    ppermute x2 -> x11, waiting for transfers between devices: 9.22 us -> 39.9 us  [permute(): return lax.ppermute(value, axes, pairs)]
    all_to_all x1 -> x2, blocking collectives: 49.7 us -> 44.1 us  [spread(): return lax.all_to_all(copies, axis, 0, 0, tiled=True)]
    dynamic_update_slice x0 -> x4, local copies, waits for them, and re-layouts: none -> 2.79 us  [around(): ring = lax.dynamic_update_slice(ring, block[None], ((y + k) % 4, 0, 0))]
    broadcast_in_dim x5 -> x6, local copies, waits for them, and re-layouts: 5.88 us -> 3.25 us  [spread(): copies = jnp.broadcast_to(value[None], (n,) + value.shape)]
    slice x3 -> x6, local copies, waits for them, and re-layouts: 4.44 us -> 1.98 us  [the longest x1 1.09 us: per_device(): part_a[half:]]
  transfers between devices with their start and end apart: 6 -> 15, of which waited for: 5 -> 8; matrix products, arithmetic and copies ran while one was open for 4% -> 6% of each run, Pallas kernels for 0% -> 0%
where the time goes in v2:
time: 221 us; the launch traced here: 220 us
  starting transfers between devices  108 us (49%)
  waiting for transfers between devices  45 us (20%)
  blocking collectives  44.1 us (20%)
  local copies, waits for them, and re-layouts  10.9 us (5%)
  matrix products  8.22 us (4%)
  other arithmetic  3.47 us (2%)
    ppermute x11, starting transfers between devices, permute(): return lax.ppermute(value, axes, pairs)  65.6 us
    all_to_all x2, blocking collectives, spread(): return lax.all_to_all(copies, axis, 0, 0, tiled=True)  44.1 us
    all_to_all x4, starting transfers between devices, spread(): return lax.all_to_all(copies, axis, 0, 0, tiled=True)  42 us
    ppermute x11, waiting for transfers between devices, permute(): return lax.ppermute(value, axes, pairs)  39.9 us
    dot_general x1, matrix products, per_device(): lax.dot_general(weight_codes, rows, (((1,), (0,)), ((), ())), preferred_e...  6.11 us
    all_to_all x4, waiting for transfers between devices, spread(): return lax.all_to_all(copies, axis, 0, 0, tiled=True)  5.02 us
  transfers between devices with their start and end apart: 15, of which 8 were waited for; matrix products, arithmetic and copies ran while one was open for 6% of the time, Pallas kernels for 0%

profile of v2, /device:TPU:1, one launch (start us, length us, event | category | flops | bytes accessed | tf_op | source)
XLA Modules:
  0.0 220.1 jit_solution(1754075971643264906)
XLA Ops:
  0.6 0.0 copy-start.2
  0.7 0.8 dynamic_slice.3
  1.5 0.8 multiply_convert_fusion
  2.3 0.7 broadcast_in_dim.28
  3.0 22.3 %all-to-all-start = ((bf16[4,116,128]{2,1,0:T(8,128)(2,1)}), bf16[4,116,128]{2,1,0:T(8,128)(2,1)S(1)}, u32[]{:S(2)}, u32[]{:S(2)}) async-start(bf16[4,116,128]{2,1,0:T(8,128)(2,1)} %broadcast_in_dim.28), calls=%async_computation | async-start | bytes 245760 | tf_op jit(solution)/shard_map/all_to_all | solution.py:39
  25.2 0.8 slice.42
  26.0 13.2 %collective-permute-start.1 = (bf16[224,128]{1,0:T(8,128)(2,1)S(1)}, bf16[224,128]{1,0:T(8,128)(2,1)S(1)}, u32[]{:S(2)}, u32[]{:S(2)}) collective-permute-start(bf16[224,128]{1,0:T(8,128)(2,1)S(1)} %slice.42), channel_id=1, source_target_pairs={{0,143},{1,0},{2,1},{3,2},{4,3},{5,4},{6,5},{7,6},{8,7},{9,8},{10,... | collective-permute-start | bytes 172040 | tf_op jit(solution)/shard_map/ppermute | solution.py:21
  39.3 1.9 collective-permute-start
  41.2 0.7 all-to-all-done
  41.9 6.7 %collective-permute-done = bf16[116,128]{1,0:T(8,128)(2,1)S(1)} collective-permute-done((bf16[116,128]{1,0:T(8,128)(2,1)}, bf16[116,128]{1,0:T(8,128)(2,1)S(1)}, u32[]{:S(2)}, u32[]{:S(2)}) %collective-permute-start) | collective-permute-done | bytes 29728 | tf_op jit(solution)/shard_map/ppermute | solution.py:21
  48.7 0.0 collective-permute-done.1
  48.7 25.9 %all_to_all.30 = bf16[4,116,128]{2,1,0:T(8,128)(2,1)S(1)} all-to-all(bf16[4,116,128]{2,1,0:T(8,128)(2,1)S(1)} %broadcast_in_dim.30), channel_id=1, replica_groups=mesh['x'=4,'zh'=2,'c'=2,'y'=4,'za'=4,'zb'=4] {'za'}, dimensions={0} | all-to-all | bytes 237568 | tf_op jit(solution)/shard_map/all_to_all | solution.py:39
  74.6 0.1 broadcast_in_dim.29
  74.6 18.2 %all_to_all.31 = bf16[4,464,128]{2,1,0:T(8,128)(2,1)S(1)} all-to-all(bf16[4,464,128]{2,1,0:T(8,128)(2,1)S(1)} %broadcast_in_dim.29), channel_id=1, replica_groups=mesh['x'=4,'zh'=2,'c'=2,'y'=4,'za'=4,'zb'=4] {'zb'}, dimensions={0} | all-to-all | bytes 950272 | tf_op jit(solution)/shard_map/all_to_all | solution.py:39
  92.8 0.0 copy-done.2
  92.8 0.8 broadcast_in_dim.31
  93.7 7.9 %all-to-all-start.3 = ((bf16[4,464,128]{2,1,0:T(8,128)(2,1)}), bf16[4,464,128]{2,1,0:T(8,128)(2,1)S(1)}, u32[]{:S(2)}, u32[]{:S(2)}) async-start(bf16[4,464,128]{2,1,0:T(8,128)(2,1)} %broadcast_in_dim.31), calls=%async_computation.3 | async-start | bytes 950272 | tf_op jit(solution)/shard_map/all_to_all | solution.py:39
  101.6 15.6 %collective-permute-start.3 = (bf16[240,128]{1,0:T(8,128)(2,1)S(1)}, bf16[240,128]{1,0:T(8,128)(2,1)S(1)}, u32[]{:S(2)}, u32[]{:S(2)}) collective-permute-start(bf16[240,128]{1,0:T(8,128)(2,1)S(1)} %slice.43), channel_id=1, source_target_pairs={{0,128},{1,129},{2,130},{3,131},{4,132},{5,133},{6,134},{7,135},{8... | collective-permute-start | bytes 184328 | tf_op jit(solution)/shard_map/ppermute | solution.py:21
  117.2 7.0 %collective-permute-start.2 = (bf16[224,128]{1,0:T(8,128)(2,1)S(1)}, bf16[224,128]{1,0:T(8,128)(2,1)S(1)}, u32[]{:S(2)}, u32[]{:S(2)}) collective-permute-start(bf16[224,128]{1,0:T(8,128)(2,1)S(1)} %collective-permute-done.1), channel_id=1, source_target_pairs={{0,129},{1,130},{2,131},{3,132},{4,133},{5,134},{6,135},{7,136},{8... | collective-permute-start | bytes 172040 | tf_op jit(solution)/shard_map/ppermute | solution.py:21
  124.2 0.8 collective-permute-done.3
  125.0 21.5 %collective-permute-done.2 = bf16[224,128]{1,0:T(8,128)(2,1)S(1)} collective-permute-done((bf16[224,128]{1,0:T(8,128)(2,1)S(1)}, bf16[224,128]{1,0:T(8,128)(2,1)S(1)}, u32[]{:S(2)}, u32[]{:S(2)}) %collective-permute-start.2) | collective-permute-done | bytes 57376 | tf_op jit(solution)/shard_map/ppermute | solution.py:21
  146.5 0.1 reshape.107
  146.7 0.1 reshape.108
  146.8 0.0 all-to-all-done.3
  146.8 0.8 broadcast_in_dim.33
  147.6 8.4 %all-to-all-start.4 = ((bf16[4,464,128]{2,1,0:T(8,128)(2,1)}), bf16[4,464,128]{2,1,0:T(8,128)(2,1)S(1)}, u32[]{:S(2)}, u32[]{:S(2)}) async-start(bf16[4,464,128]{2,1,0:T(8,128)(2,1)} %broadcast_in_dim.33), calls=%async_computation.4 | async-start | bytes 950272 | tf_op jit(solution)/shard_map/all_to_all | solution.py:39
  156.0 5.5 %collective-permute-start.4 = (bf16[1856,128]{1,0:T(8,128)(2,1)S(1)}, bf16[1856,128]{1,0:T(8,128)(2,1)S(1)}, u32[]{:S(2)}, u32[]{:S(2)}) collective-permute-start(bf16[1856,128]{1,0:T(8,128)(2,1)S(1)} %reshape.108), channel_id=1, source_target_pairs={{0,16},{16,32},{32,48},{48,0},{1,17},{17,33},{33,49},{49,1},{2,18}... | collective-permute-start | bytes 1425416 | tf_op jit(solution)/shard_map/ppermute | solution.py:21
  161.5 1.9 collective-permute-start.5
  163.4 6.1 %collective-permute-done.4 = bf16[1856,128]{1,0:T(8,128)(2,1)S(1)} collective-permute-done((bf16[1856,128]{1,0:T(8,128)(2,1)S(1)}, bf16[1856,128]{1,0:T(8,128)(2,1)S(1)}, u32[]{:S(2)}, u32[]{:S(2)}) %collective-permute-start.4) | collective-permute-done | bytes 475168 | tf_op jit(solution)/shard_map/ppermute | solution.py:21
  169.5 3.8 %collective-permute-done.5 = bf16[1856,128]{1,0:T(8,128)(2,1)S(1)} collective-permute-done((bf16[1856,128]{1,0:T(8,128)(2,1)S(1)}, bf16[1856,128]{1,0:T(8,128)(2,1)S(1)}, u32[]{:S(2)}, u32[]{:S(2)}) %collective-permute-start.5) | collective-permute-done | bytes 475168 | tf_op jit(solution)/shard_map/ppermute | solution.py:21
  173.3 0.0 copy-start
  173.3 0.0 all-to-all-done.4
  173.4 1.2 pad_maximum_fusion.2
  174.6 1.9 collective-permute-start.6
  176.5 4.6 %collective-permute-start.7 = (bf16[2784,128]{1,0:T(8,128)(2,1)}, bf16[2784,128]{1,0:T(8,128)(2,1)}, u32[]{:S(2)}, u32[]{:S(2)}) collective-permute-start(bf16[2784,128]{1,0:T(8,128)(2,1)} %get-tuple-element.36), channel_id=1, source_target_pairs={{0,48},{16,0},{32,16},{48,32},{1,49},{17,1},{33,17},{49,33},{2,50}... | collective-permute-start | bytes 2138120 | tf_op jit(solution)/shard_map/ppermute | solution.py:21
  181.1 0.8 broadcast_in_dim.35
  182.0 0.0 copy-done
  182.0 3.5 %all-to-all-start.5 = ((bf16[4,464,128]{2,1,0:T(8,128)(2,1)}), bf16[4,464,128]{2,1,0:T(8,128)(2,1)S(1)}, u32[]{:S(2)}, u32[]{:S(2)}) async-start(bf16[4,464,128]{2,1,0:T(8,128)(2,1)} %broadcast_in_dim.35), calls=%async_computation.5 | async-start | bytes 950272 | tf_op jit(solution)/shard_map/all_to_all | solution.py:39
  185.5 0.0 copy-start.1
  185.5 1.5 broadcast_in_dim.32
  187.0 0.0 copy-done.1
  187.0 0.8 bitcast_dynamic-update-slice_fusion.3
  187.8 4.3 %all-to-all-done.5 = bf16[4,464,128]{2,1,0:T(8,128)(2,1)S(1)} async-done(((bf16[4,464,128]{2,1,0:T(8,128)(2,1)}), bf16[4,464,128]{2,1,0:T(8,128)(2,1)S(1)}, u32[]{:S(2)}, u32[]{:S(2)}) %all-to-all-start.5) | async-done | bytes 475168 | tf_op jit(solution)/shard_map/all_to_all | solution.py:39
  192.1 0.0 collective-permute-done.6
  192.1 1.0 collective-permute-done.7
  193.1 1.1 fusion.3
  194.1 0.2 broadcast_in_dim.38
  194.4 1.1 bitcast_dynamic-update-slice_fusion.1
  195.5 5.3 %collective-permute-start.10 = (bf16[928,128]{1,0:T(8,128)(2,1)S(1)}, bf16[928,128]{1,0:T(8,128)(2,1)S(1)}, u32[]{:S(2)}, u32[]{:S(2)}) collective-permute-start(bf16[928,128]{1,0:T(8,128)(2,1)S(1)} %get-tuple-element.34), channel_id=1, source_target_pairs={{0,48},{16,0},{32,16},{48,32},{1,49},{17,1},{33,17},{49,33},{2,50}... | collective-permute-start | bytes 712712 | tf_op jit(solution)/shard_map/ppermute | solution.py:21
  200.9 1.9 collective-permute-start.9
  202.8 0.1 maximum_select_fusion.1
  202.9 6.7 %collective-permute-start.8 = (bf16[4,2,464,128]{3,2,1,0:T(8,128)(2,1)S(1)}, bf16[4,2,464,128]{3,2,1,0:T(8,128)(2,1)S(1)}, u32[]{:S(2)}, u32[]{:S(2)}) collective-permute-start(bf16[4,2,464,128]{3,2,1,0:T(8,128)(2,1)S(1)} %maximum_select_fusion.1), channel_id=1, source_target_pairs={{0,64},{64,0},{1,65},{65,1},{2,66},{66,2},{3,67},{67,3},{4,68},{68... | collective-permute-start | bytes 2850824 | tf_op jit(solution)/shard_map/ppermute | solution.py:21
  209.6 0.2 pad_maximum_fusion
  209.8 0.8 fusion
  210.6 0.8 bitcast_dynamic-update-slice_fusion.2
  211.4 6.1 %fusion.4 = f32[128,464]{0,1:T(8,128)} fusion(bf16[464,7424]{1,0:T(8,128)(2,1)} %param.5, bf16[7424,128]{1,0:T(8,128)(2,1)} %bitcast.7), kind=kOutput, calls=%fused_computation.20 | convolution fusion | flops 881852416 | bytes 9027584 | tf_op jit(solution)/shard_map/dot_general | solution.py:96
  217.5 0.1 copy_select_fusion
  217.6 0.0 collective-permute-done.10
  217.7 0.0 collective-permute-done.9
  217.7 0.1 fusion.1
  217.7 0.1 bitcast_dynamic-update-slice_fusion
  217.8 0.0 collective-permute-done.8
  217.8 0.2 maximum_select_fusion
  218.0 2.1 convolution_bitcast_fusion
  (9 shorter events, 0.2 us)
Async XLA Ops:
  0.6 92.2 %copy-start.2 = (bf16[128,464]{0,1:T(8,128)(2,1)S(1)}, bf16[128,464]{0,1:T(8,128)(2,1)}, u32[]{:S(2)}) copy-start(bf16[128,464]{0,1:T(8,128)(2,1)} %param.4) | copy-start | bytes 356356
  3.0 39.0 %all-to-all-start = ((bf16[4,116,128]{2,1,0:T(8,128)(2,1)}), bf16[4,116,128]{2,1,0:T(8,128)(2,1)S(1)}, u32[]{:S(2)}, u32[]{:S(2)}) async-start(bf16[4,116,128]{2,1,0:T(8,128)(2,1)} %broadcast_in_dim.28), calls=%async_computation | async-start | bytes 245760 | tf_op jit(solution)/shard_map/all_to_all | solution.py:39
  26.0 22.7 %collective-permute-start.1 = (bf16[224,128]{1,0:T(8,128)(2,1)S(1)}, bf16[224,128]{1,0:T(8,128)(2,1)S(1)}, u32[]{:S(2)}, u32[]{:S(2)}) collective-permute-start(bf16[224,128]{1,0:T(8,128)(2,1)S(1)} %slice.42), channel_id=1, source_target_pairs={{0,143},{1,0},{2,1},{3,2},{4,3},{5,4},{6,5},{7,6},{8,7},{9,8},{10,... | collective-permute-start | bytes 172040 | tf_op jit(solution)/shard_map/ppermute | solution.py:21
  39.3 9.4 %collective-permute-start = (bf16[116,128]{1,0:T(8,128)(2,1)}, bf16[116,128]{1,0:T(8,128)(2,1)S(1)}, u32[]{:S(2)}, u32[]{:S(2)}) collective-permute-start(bf16[116,128]{1,0:T(8,128)(2,1)} %bitcast.48), channel_id=1, source_target_pairs={{0,0},{1,4},{2,8},{3,12},{4,64},{5,68},{6,72},{7,76},{8,128},{9,13... | collective-permute-start | bytes 89096 | tf_op jit(solution)/shard_map/ppermute | solution.py:21
  93.7 53.1 %all-to-all-start.3 = ((bf16[4,464,128]{2,1,0:T(8,128)(2,1)}), bf16[4,464,128]{2,1,0:T(8,128)(2,1)S(1)}, u32[]{:S(2)}, u32[]{:S(2)}) async-start(bf16[4,464,128]{2,1,0:T(8,128)(2,1)} %broadcast_in_dim.31), calls=%async_computation.3 | async-start | bytes 950272 | tf_op jit(solution)/shard_map/all_to_all | solution.py:39
  101.6 23.4 %collective-permute-start.3 = (bf16[240,128]{1,0:T(8,128)(2,1)S(1)}, bf16[240,128]{1,0:T(8,128)(2,1)S(1)}, u32[]{:S(2)}, u32[]{:S(2)}) collective-permute-start(bf16[240,128]{1,0:T(8,128)(2,1)S(1)} %slice.43), channel_id=1, source_target_pairs={{0,128},{1,129},{2,130},{3,131},{4,132},{5,133},{6,134},{7,135},{8... | collective-permute-start | bytes 184328 | tf_op jit(solution)/shard_map/ppermute | solution.py:21
  117.2 29.3 %collective-permute-start.2 = (bf16[224,128]{1,0:T(8,128)(2,1)S(1)}, bf16[224,128]{1,0:T(8,128)(2,1)S(1)}, u32[]{:S(2)}, u32[]{:S(2)}) collective-permute-start(bf16[224,128]{1,0:T(8,128)(2,1)S(1)} %collective-permute-done.1), channel_id=1, source_target_pairs={{0,129},{1,130},{2,131},{3,132},{4,133},{5,134},{6,135},{7,136},{8... | collective-permute-start | bytes 172040 | tf_op jit(solution)/shard_map/ppermute | solution.py:21
  147.6 25.7 %all-to-all-start.4 = ((bf16[4,464,128]{2,1,0:T(8,128)(2,1)}), bf16[4,464,128]{2,1,0:T(8,128)(2,1)S(1)}, u32[]{:S(2)}, u32[]{:S(2)}) async-start(bf16[4,464,128]{2,1,0:T(8,128)(2,1)} %broadcast_in_dim.33), calls=%async_computation.4 | async-start | bytes 950272 | tf_op jit(solution)/shard_map/all_to_all | solution.py:39
  156.0 13.5 %collective-permute-start.4 = (bf16[1856,128]{1,0:T(8,128)(2,1)S(1)}, bf16[1856,128]{1,0:T(8,128)(2,1)S(1)}, u32[]{:S(2)}, u32[]{:S(2)}) collective-permute-start(bf16[1856,128]{1,0:T(8,128)(2,1)S(1)} %reshape.108), channel_id=1, source_target_pairs={{0,16},{16,32},{32,48},{48,0},{1,17},{17,33},{33,49},{49,1},{2,18}... | collective-permute-start | bytes 1425416 | tf_op jit(solution)/shard_map/ppermute | solution.py:21
  161.5 11.9 %collective-permute-start.5 = (bf16[1856,128]{1,0:T(8,128)(2,1)S(1)}, bf16[1856,128]{1,0:T(8,128)(2,1)S(1)}, u32[]{:S(2)}, u32[]{:S(2)}) collective-permute-start(bf16[1856,128]{1,0:T(8,128)(2,1)S(1)} %reshape.108), channel_id=1, source_target_pairs={{0,48},{16,0},{32,16},{48,32},{1,49},{17,1},{33,17},{49,33},{2,50}... | collective-permute-start | bytes 1425416 | tf_op jit(solution)/shard_map/ppermute | solution.py:21
  173.3 8.6 %copy-start = (bf16[1856,128]{1,0:T(8,128)(2,1)}, bf16[1856,128]{1,0:T(8,128)(2,1)S(1)}, u32[]{:S(2)}) copy-start(bf16[1856,128]{1,0:T(8,128)(2,1)S(1)} %collective-permute-done.5) | copy-start | bytes 1425412
  174.6 17.5 %collective-permute-start.6 = (bf16[2784,128]{1,0:T(8,128)(2,1)}, bf16[2784,128]{1,0:T(8,128)(2,1)S(1)}, u32[]{:S(2)}, u32[]{:S(2)}) collective-permute-start(bf16[2784,128]{1,0:T(8,128)(2,1)} %get-tuple-element.37), channel_id=1, source_target_pairs={{0,16},{16,32},{32,48},{48,0},{1,17},{17,33},{33,49},{49,1},{2,18}... | collective-permute-start | bytes 2138120 | tf_op jit(solution)/shard_map/ppermute | solution.py:21
  176.5 16.5 %collective-permute-start.7 = (bf16[2784,128]{1,0:T(8,128)(2,1)}, bf16[2784,128]{1,0:T(8,128)(2,1)}, u32[]{:S(2)}, u32[]{:S(2)}) collective-permute-start(bf16[2784,128]{1,0:T(8,128)(2,1)} %get-tuple-element.36), channel_id=1, source_target_pairs={{0,48},{16,0},{32,16},{48,32},{1,49},{17,1},{33,17},{49,33},{2,50}... | collective-permute-start | bytes 2138120 | tf_op jit(solution)/shard_map/ppermute | solution.py:21
  182.0 10.1 %all-to-all-start.5 = ((bf16[4,464,128]{2,1,0:T(8,128)(2,1)}), bf16[4,464,128]{2,1,0:T(8,128)(2,1)S(1)}, u32[]{:S(2)}, u32[]{:S(2)}) async-start(bf16[4,464,128]{2,1,0:T(8,128)(2,1)} %broadcast_in_dim.35), calls=%async_computation.5 | async-start | bytes 950272 | tf_op jit(solution)/shard_map/all_to_all | solution.py:39
  185.5 1.5 copy-start.1
  195.5 22.2 %collective-permute-start.10 = (bf16[928,128]{1,0:T(8,128)(2,1)S(1)}, bf16[928,128]{1,0:T(8,128)(2,1)S(1)}, u32[]{:S(2)}, u32[]{:S(2)}) collective-permute-start(bf16[928,128]{1,0:T(8,128)(2,1)S(1)} %get-tuple-element.34), channel_id=1, source_target_pairs={{0,48},{16,0},{32,16},{48,32},{1,49},{17,1},{33,17},{49,33},{2,50}... | collective-permute-start | bytes 712712 | tf_op jit(solution)/shard_map/ppermute | solution.py:21
  200.9 16.8 %collective-permute-start.9 = (bf16[928,128]{1,0:T(8,128)(2,1)S(1)}, bf16[928,128]{1,0:T(8,128)(2,1)S(1)}, u32[]{:S(2)}, u32[]{:S(2)}) collective-permute-start(bf16[928,128]{1,0:T(8,128)(2,1)S(1)} %get-tuple-element.32), channel_id=1, source_target_pairs={{0,16},{16,32},{32,48},{48,0},{1,17},{17,33},{33,49},{49,1},{2,18}... | collective-permute-start | bytes 712712 | tf_op jit(solution)/shard_map/ppermute | solution.py:21
  202.9 14.9 %collective-permute-start.8 = (bf16[4,2,464,128]{3,2,1,0:T(8,128)(2,1)S(1)}, bf16[4,2,464,128]{3,2,1,0:T(8,128)(2,1)S(1)}, u32[]{:S(2)}, u32[]{:S(2)}) collective-permute-start(bf16[4,2,464,128]{3,2,1,0:T(8,128)(2,1)S(1)} %maximum_select_fusion.1), channel_id=1, source_target_pairs={{0,64},{64,0},{1,65},{65,1},{2,66},{66,2},{3,67},{67,3},{4,68},{68... | collective-permute-start | bytes 2850824 | tf_op jit(solution)/shard_map/ppermute | solution.py:21

commit v3 on v2

v3 whole, which is shorter than its diff:
```python
import itertools

import jax
import jax.numpy as jnp
import numpy as np
from jax import lax
from jax.sharding import Mesh, PartitionSpec as P

AXES = ("x", "zh", "c", "y", "za", "zb")
SIZES = (4, 2, 2, 4, 4, 4)
DP = ("x", "zh", "c")
TENSOR = ("y", "za", "zb")


def permute(value, axes, target):
    sizes = [SIZES[AXES.index(a)] for a in axes]
    pairs = []
    for place in itertools.product(*map(range, sizes)):
        to = target(*place)
        pairs.append((int(np.ravel_multi_index(place, sizes)), int(np.ravel_multi_index(to, sizes))))
    return lax.ppermute(value, axes, pairs)


def along_y(value, step):
    return permute(value, ("y",), lambda y: ((y + step) % 4,))


def spread(value, axis):
    n = SIZES[AXES.index(axis)]
    copies = jnp.broadcast_to(value[None], (n,) + value.shape)
    return lax.all_to_all(copies, axis, 0, 0, tiled=True)


def along_zb(value, step):
    return permute(value, ("zb",), lambda zb: ((zb + step) % 4,))


def ordered(axis, blocks):
    me = lax.axis_index(axis)
    ring = jnp.broadcast_to(blocks[0][None], (4,) + blocks[0].shape)
    for k, block in enumerate(blocks[1:], 1):
        ring = lax.dynamic_update_slice(ring, block[None], ((me + k) % 4, 0, 0))
    return ring


sync = lax.optimization_barrier


def per_device(activations, weight_codes, channel_scale, output_grads):
    a = activations.T
    g = output_grads.T
    units, tokens = a.shape
    cols = g.shape[0]
    half = 8 * cols

    me = lax.axis_index(TENSOR)
    scale = lax.dynamic_slice(channel_scale, (me * cols,), (cols,))
    scaled = (g.astype(jnp.float32) * scale[:, None]).astype(jnp.bfloat16)

    part = permute(g, AXES, lambda x, zh, c, y, za, zb: (y, za // 2, za % 2, x, zb, 2 * zh + c))
    other = permute(a, ("zh",), lambda h: (1 - h,))
    rows = spread(scaled, "za").reshape(4 * cols, tokens)
    part, rows, other = sync((part, rows, other))

    part = spread(part, "za").reshape(4 * cols, tokens)
    rows = ordered("zb", [rows] + [along_zb(rows, -k) for k in (1, 2, 3)])
    rows = rows.reshape(4, 4, cols, tokens).transpose(1, 0, 2, 3).reshape(16 * cols, tokens)
    rows, part = sync((rows, part))

    rows_b, rows_a = along_y(rows, 1), along_y(rows, -1)
    part = spread(part, "zb").reshape(16 * cols, tokens)
    rows_b, rows_a, part, other = sync((rows_b, rows_a, part, other))

    up = along_y(jnp.concatenate([rows_b[:half], part]), 1)
    down = along_y(jnp.concatenate([rows_a[half:], part]), -1)
    first = lax.axis_index("zh") == 0
    acts = spread(jnp.where(first, jnp.stack([a, other]), jnp.stack([other, a])), "x")
    up, down, acts = sync((up, down, acts))
    rows_o = jnp.concatenate([up[:half], down[:half]])
    part_b, part_a = up[half:], down[half:]

    part_o = jnp.concatenate([along_y(part_b[:half], 1), along_y(part_a[half:], -1)])
    acts_c = permute(acts, ("c",), lambda c: (1 - c,))
    first = lax.axis_index("c") == 0
    acts = jnp.where(first, jnp.stack([acts, acts_c], 2), jnp.stack([acts_c, acts], 2)).reshape(16, units, tokens)

    rows = ordered("y", [rows, rows_a, rows_o, rows_b]).reshape(64 * cols, tokens)
    input_grads = lax.dot_general(weight_codes, rows, (((1,), (0,)), ((), ())), preferred_element_type=jnp.float32)
    part = ordered("y", [part, part_a, part_o, part_b]).reshape(16, 4 * cols, tokens)
    weight_grads = lax.dot_general(acts, part, (((0, 2), (0, 2)), ((), ())), preferred_element_type=jnp.float32)
    return input_grads.T, weight_grads


def solution(mesh):
    fine = Mesh(mesh.devices.reshape(SIZES), AXES)
    placed = (P(DP, TENSOR), P(TENSOR, None), P(), P(DP, TENSOR))
    return jax.shard_map(
        per_device,
        mesh=fine,
        in_specs=placed,
        out_specs=(P(DP, TENSOR), P(TENSOR, DP)),
        check_vma=False,
    )
```

time: 221 us -> 182 us (0.82)
  blocking collectives: 44.1 us -> 0 us
  starting transfers between devices: 108 us -> 124 us
  waiting for transfers between devices: 45 us -> 36.4 us
    all_to_all x2 -> x0, blocking collectives: 44.1 us -> none  [spread(): return lax.all_to_all(copies, axis, 0, 0, tiled=True)]
    all_to_all x4, starting transfers between devices: 42 us -> 56.2 us  [spread(): return lax.all_to_all(copies, axis, 0, 0, tiled=True)]
    ppermute x11 -> x12, waiting for transfers between devices: 39.9 us -> 30.5 us  [permute(): return lax.ppermute(value, axes, pairs)]
    ppermute x11 -> x12, starting transfers between devices: 65.6 us -> 67.8 us  [permute(): return lax.ppermute(value, axes, pairs)]
  transfers between devices with their start and end apart: 15 -> 16, of which waited for: 8 -> 8; matrix products, arithmetic and copies ran while one was open for 6% -> 6% of each run, Pallas kernels for 0% -> 0%
where the time goes in v3:
time: 182 us; the launch traced here: 181 us
  starting transfers between devices  124 us (68%)
  waiting for transfers between devices  36.4 us (20%)
  local copies, waits for them, and re-layouts  9.48 us (5%)
  matrix products  7.69 us (4%)
  other arithmetic  2.15 us (1%)
    ppermute x12, starting transfers between devices, permute(): return lax.ppermute(value, axes, pairs)  67.8 us
    all_to_all x4, starting transfers between devices, spread(): return lax.all_to_all(copies, axis, 0, 0, tiled=True)  56.2 us
    ppermute x12, waiting for transfers between devices, permute(): return lax.ppermute(value, axes, pairs)  30.5 us
    all_to_all x4, waiting for transfers between devices, spread(): return lax.all_to_all(copies, axis, 0, 0, tiled=True)  5.83 us
    dot_general x1, matrix products, per_device(): lax.dot_general(weight_codes, rows, (((1,), (0,)), ((), ())), preferred_e...  5.59 us
  transfers between devices with their start and end apart: 16, of which 8 were waited for; matrix products, arithmetic and copies ran while one was open for 6% of the time, Pallas kernels for 0%

profile of v3, /device:TPU:1, one launch (start us, length us, event | category | flops | bytes accessed | tf_op | source)
XLA Modules:
  0.0 180.7 jit_solution(12875166005007112430)
XLA Ops:
  0.6 0.8 dynamic_slice.3
  1.4 0.8 multiply_convert_fusion
  2.3 0.7 broadcast_in_dim.32
  2.9 22.3 %all-to-all-start = ((bf16[4,116,128]{2,1,0:T(8,128)(2,1)}), bf16[4,116,128]{2,1,0:T(8,128)(2,1)S(1)}, u32[]{:S(2)}, u32[]{:S(2)}) async-start(bf16[4,116,128]{2,1,0:T(8,128)(2,1)} %broadcast_in_dim.32), calls=%async_computation | async-start | bytes 245760 | tf_op jit(solution)/shard_map/all_to_all | solution.py:31
  25.2 14.3 %collective-permute-start.1 = (bf16[464,128]{1,0:T(8,128)(2,1)}, bf16[464,128]{1,0:T(8,128)(2,1)S(1)}, u32[]{:S(2)}, u32[]{:S(2)}) collective-permute-start(bf16[464,128]{1,0:T(8,128)(2,1)} %bitcast.49), channel_id=1, source_target_pairs={{0,128},{128,0},{1,129},{129,1},{2,130},{130,2},{3,131},{131,3},{4... | collective-permute-start | bytes 356360 | tf_op jit(solution)/shard_map/ppermute | solution.py:21
  39.5 3.8 %collective-permute-start = (bf16[116,128]{1,0:T(8,128)(2,1)}, bf16[116,128]{1,0:T(8,128)(2,1)S(1)}, u32[]{:S(2)}, u32[]{:S(2)}) collective-permute-start(bf16[116,128]{1,0:T(8,128)(2,1)} %bitcast.52), channel_id=1, source_target_pairs={{0,0},{1,4},{2,8},{3,12},{4,64},{5,68},{6,72},{7,76},{8,128},{9,13... | collective-permute-start | bytes 89096 | tf_op jit(solution)/shard_map/ppermute | solution.py:21
  43.2 0.0 all-to-all-done
  43.3 15.3 %collective-permute-done = bf16[116,128]{1,0:T(8,128)(2,1)S(1)} collective-permute-done((bf16[116,128]{1,0:T(8,128)(2,1)}, bf16[116,128]{1,0:T(8,128)(2,1)S(1)}, u32[]{:S(2)}, u32[]{:S(2)}) %collective-permute-start) | collective-permute-done | bytes 29728 | tf_op jit(solution)/shard_map/ppermute | solution.py:21
  58.6 0.0 collective-permute-done.1
  58.6 6.0 %collective-permute-start.2 = (bf16[464,128]{1,0:T(8,128)(2,1)S(1)}, bf16[464,128]{1,0:T(8,128)(2,1)S(1)}, u32[]{:S(2)}, u32[]{:S(2)}) collective-permute-start(bf16[464,128]{1,0:T(8,128)(2,1)S(1)} %reshape.78), channel_id=1, source_target_pairs={{0,3},{1,0},{2,1},{3,2},{4,7},{5,4},{6,5},{7,6},{8,11},{9,8},{10,9... | collective-permute-start | bytes 356360 | tf_op jit(solution)/shard_map/ppermute | solution.py:21
  64.6 0.7 broadcast_in_dim.37
  65.2 20.9 %all-to-all-start.1 = ((bf16[4,116,128]{2,1,0:T(8,128)(2,1)}), bf16[4,116,128]{2,1,0:T(8,128)(2,1)S(1)}, u32[]{:S(2)}, u32[]{:S(2)}) async-start(bf16[4,116,128]{2,1,0:T(8,128)(2,1)} %broadcast_in_dim.37), calls=%async_computation.1 | async-start | bytes 245760 | tf_op jit(solution)/shard_map/all_to_all | solution.py:31
  86.2 6.1 %collective-permute-start.3 = (bf16[464,128]{1,0:T(8,128)(2,1)S(1)}, bf16[464,128]{1,0:T(8,128)(2,1)S(1)}, u32[]{:S(2)}, u32[]{:S(2)}) collective-permute-start(bf16[464,128]{1,0:T(8,128)(2,1)S(1)} %reshape.78), channel_id=1, source_target_pairs={{0,2},{1,3},{2,0},{3,1},{4,6},{5,7},{6,4},{7,5},{8,10},{9,11},{10,... | collective-permute-start | bytes 356360 | tf_op jit(solution)/shard_map/ppermute | solution.py:21
  92.3 3.4 %collective-permute-start.4 = (bf16[464,128]{1,0:T(8,128)(2,1)S(1)}, bf16[464,128]{1,0:T(8,128)(2,1)S(1)}, u32[]{:S(2)}, u32[]{:S(2)}) collective-permute-start(bf16[464,128]{1,0:T(8,128)(2,1)S(1)} %reshape.78), channel_id=1, source_target_pairs={{0,1},{1,2},{2,3},{3,0},{4,5},{5,6},{6,7},{7,4},{8,9},{9,10},{10,1... | collective-permute-start | bytes 356360 | tf_op jit(solution)/shard_map/ppermute | solution.py:21
  95.6 0.0 collective-permute-done.2
  95.7 0.1 broadcast_in_dim.33
  95.8 6.5 %collective-permute-done.3 = bf16[464,128]{1,0:T(8,128)(2,1)S(1)} collective-permute-done((bf16[464,128]{1,0:T(8,128)(2,1)S(1)}, bf16[464,128]{1,0:T(8,128)(2,1)S(1)}, u32[]{:S(2)}, u32[]{:S(2)}) %collective-permute-start.3) | collective-permute-done | bytes 118816 | tf_op jit(solution)/shard_map/ppermute | solution.py:21
  102.3 0.0 collective-permute-done.4
  102.3 0.1 reshape.79
  102.5 0.1 reshape.80
  102.6 0.1 all-to-all-done.1
  102.7 0.8 broadcast_in_dim.77
  103.5 9.0 %all-to-all-start.2 = ((bf16[4,464,128]{2,1,0:T(8,128)(2,1)}), bf16[4,464,128]{2,1,0:T(8,128)(2,1)S(1)}, u32[]{:S(2)}, u32[]{:S(2)}) async-start(bf16[4,464,128]{2,1,0:T(8,128)(2,1)} %broadcast_in_dim.77), calls=%async_computation.2 | async-start | bytes 950272 | tf_op jit(solution)/shard_map/all_to_all | solution.py:31
  112.5 0.0 copy-start.4
  112.5 2.0 %collective-permute-start.5 = (bf16[1856,128]{1,0:T(8,128)(2,1)S(1)}, bf16[1856,128]{1,0:T(8,128)(2,1)S(1)}, u32[]{:S(2)}, u32[]{:S(2)}) collective-permute-start(bf16[1856,128]{1,0:T(8,128)(2,1)S(1)} %reshape.80), channel_id=1, source_target_pairs={{0,16},{16,32},{32,48},{48,0},{1,17},{17,33},{33,49},{49,1},{2,18}... | collective-permute-start | bytes 1425416 | tf_op jit(solution)/shard_map/ppermute | solution.py:21
  114.5 4.6 %collective-permute-start.6 = (bf16[1856,128]{1,0:T(8,128)(2,1)S(1)}, bf16[1856,128]{1,0:T(8,128)(2,1)S(1)}, u32[]{:S(2)}, u32[]{:S(2)}) collective-permute-start(bf16[1856,128]{1,0:T(8,128)(2,1)S(1)} %reshape.80), channel_id=1, source_target_pairs={{0,48},{16,0},{32,16},{48,32},{1,49},{17,1},{33,17},{49,33},{2,50}... | collective-permute-start | bytes 1425416 | tf_op jit(solution)/shard_map/ppermute | solution.py:21
  119.1 4.1 %collective-permute-done.5 = bf16[1856,128]{1,0:T(8,128)(2,1)S(1)} collective-permute-done((bf16[1856,128]{1,0:T(8,128)(2,1)S(1)}, bf16[1856,128]{1,0:T(8,128)(2,1)S(1)}, u32[]{:S(2)}, u32[]{:S(2)}) %collective-permute-start.5) | collective-permute-done | bytes 475168 | tf_op jit(solution)/shard_map/ppermute | solution.py:21
  123.2 0.0 copy-start.2
  123.2 1.5 collective-permute-done.6
  124.7 0.0 all-to-all-done.2
  124.7 0.9 pad_maximum_fusion
  125.7 1.9 %collective-permute-start.7 = (bf16[2784,128]{1,0:T(8,128)(2,1)}, bf16[2784,128]{1,0:T(8,128)(2,1)}, u32[]{:S(2)}, u32[]{:S(2)}) collective-permute-start(bf16[2784,128]{1,0:T(8,128)(2,1)} %get-tuple-element.31), channel_id=1, source_target_pairs={{0,16},{16,32},{32,48},{48,0},{1,17},{17,33},{33,49},{49,1},{2,18}... | collective-permute-start | bytes 2138120 | tf_op jit(solution)/shard_map/ppermute | solution.py:21
  127.6 5.0 %collective-permute-start.8 = (bf16[2784,128]{1,0:T(8,128)(2,1)S(1)}, bf16[2784,128]{1,0:T(8,128)(2,1)}, u32[]{:S(2)}, u32[]{:S(2)}) collective-permute-start(bf16[2784,128]{1,0:T(8,128)(2,1)S(1)} %get-tuple-element.30), channel_id=1, source_target_pairs={{0,48},{16,0},{32,16},{48,32},{1,49},{17,1},{33,17},{49,33},{2,50}... | collective-permute-start | bytes 2138120 | tf_op jit(solution)/shard_map/ppermute | solution.py:21
  132.6 0.0 copy-done.4
  132.7 0.0 copy-done.2
  132.7 1.1 broadcast_in_dim.79
  133.7 4.1 %all-to-all-start.3 = ((bf16[4,2,464,128]{3,2,1,0:T(8,128)(2,1)}), bf16[4,2,464,128]{3,2,1,0:T(8,128)(2,1)S(1)}, u32[]{:S(2)}, u32[]{:S(2)}) async-start(bf16[4,2,464,128]{3,2,1,0:T(8,128)(2,1)} %broadcast_in_dim.79), calls=%async_computation.3 | async-start | bytes 1900544 | tf_op jit(solution)/shard_map/all_to_all | solution.py:31
  137.8 0.2 broadcast_in_dim.76
  138.1 0.1 bitcast_dynamic-update-slice_fusion.3
  138.2 0.0 copy-start
  138.2 1.4 collective-permute-done.7
  139.6 0.0 copy-done
  139.6 1.7 collective-permute-done.8
  141.3 0.0 copy-start.1
  141.3 5.7 %all-to-all-done.3 = bf16[4,2,464,128]{3,2,1,0:T(8,128)(2,1)S(1)} async-done(((bf16[4,2,464,128]{3,2,1,0:T(8,128)(2,1)}), bf16[4,2,464,128]{3,2,1,0:T(8,128)(2,1)S(1)}, u32[]{:S(2)}, u32[]{:S(2)}) %all-to-all-start.3) | async-done | bytes 950304 | tf_op jit(solution)/shard_map/all_to_all | solution.py:31
  147.1 1.1 fusion.2
  148.2 2.3 %collective-permute-start.10 = (bf16[928,128]{1,0:T(8,128)(2,1)S(1)}, bf16[928,128]{1,0:T(8,128)(2,1)S(1)}, u32[]{:S(2)}, u32[]{:S(2)}) collective-permute-start(bf16[928,128]{1,0:T(8,128)(2,1)S(1)} %get-tuple-element.26), channel_id=1, source_target_pairs={{0,16},{16,32},{32,48},{48,0},{1,17},{17,33},{33,49},{49,1},{2,18}... | collective-permute-start | bytes 712712 | tf_op jit(solution)/shard_map/ppermute | solution.py:21
  150.5 1.1 fusion.3
  151.6 4.2 %collective-permute-start.11 = (bf16[928,128]{1,0:T(8,128)(2,1)S(1)}, bf16[928,128]{1,0:T(8,128)(2,1)S(1)}, u32[]{:S(2)}, u32[]{:S(2)}) collective-permute-start(bf16[928,128]{1,0:T(8,128)(2,1)S(1)} %get-tuple-element.28), channel_id=1, source_target_pairs={{0,48},{16,0},{32,16},{48,32},{1,49},{17,1},{33,17},{49,33},{2,50}... | collective-permute-start | bytes 712712 | tf_op jit(solution)/shard_map/ppermute | solution.py:21
  155.8 14.3 %collective-permute-start.9 = (bf16[4,2,464,128]{3,2,1,0:T(8,128)(2,1)S(1)}, bf16[4,2,464,128]{3,2,1,0:T(8,128)(2,1)S(1)}, u32[]{:S(2)}, u32[]{:S(2)}) collective-permute-start(bf16[4,2,464,128]{3,2,1,0:T(8,128)(2,1)S(1)} %all-to-all-done.3), channel_id=1, source_target_pairs={{0,64},{64,0},{1,65},{65,1},{2,66},{66,2},{3,67},{67,3},{4,68},{68... | collective-permute-start | bytes 2850824 | tf_op jit(solution)/shard_map/ppermute | solution.py:21
  170.1 0.0 copy-done.1
  170.1 0.1 fusion
  170.2 0.0 copy-done.3
  170.2 0.1 bitcast_dynamic-update-slice_fusion.2
  170.3 5.6 %fusion.4 = f32[128,464]{0,1:T(8,128)} fusion(bf16[464,7424]{1,0:T(8,128)(2,1)} %param.5, bf16[7424,128]{1,0:T(8,128)(2,1)S(1)} %bitcast.47), kind=kOutput, calls=%fused_computation.19 | convolution fusion | flops 881852416 | bytes 9027584 | tf_op jit(solution)/shard_map/dot_general | solution.py:88
  175.9 0.2 broadcast_in_dim.82
  176.1 1.1 bitcast_dynamic-update-slice_fusion.1
  177.2 0.0 collective-permute-done.10
  177.2 0.0 collective-permute-done.11
  177.2 0.1 fusion.1
  177.3 1.1 bitcast_dynamic-update-slice_fusion
  178.4 0.0 collective-permute-done.9
  178.4 0.2 maximum_select_fusion
  178.6 2.1 %convolution_bitcast_fusion = f32[464,464]{1,0:T(8,128)} fusion(bf16[16,464,128]{2,1,0:T(8,128)(2,1)S(1)} %bitcast.45, bf16[16,464,128]{2,1,0:T(8,128)(2,1)S(1)} %bitcast.46), kind=kOutput, calls=%fused_computation.1 | convolution fusion | flops 881852416 | bytes 4662272 | tf_op jit(solution)/shard_map/dot_general | solution.py:90
  (10 shorter events, 0.2 us)
Async XLA Ops:
  2.9 40.3 %all-to-all-start = ((bf16[4,116,128]{2,1,0:T(8,128)(2,1)}), bf16[4,116,128]{2,1,0:T(8,128)(2,1)S(1)}, u32[]{:S(2)}, u32[]{:S(2)}) async-start(bf16[4,116,128]{2,1,0:T(8,128)(2,1)} %broadcast_in_dim.32), calls=%async_computation | async-start | bytes 245760 | tf_op jit(solution)/shard_map/all_to_all | solution.py:31
  25.2 33.4 %collective-permute-start.1 = (bf16[464,128]{1,0:T(8,128)(2,1)}, bf16[464,128]{1,0:T(8,128)(2,1)S(1)}, u32[]{:S(2)}, u32[]{:S(2)}) collective-permute-start(bf16[464,128]{1,0:T(8,128)(2,1)} %bitcast.49), channel_id=1, source_target_pairs={{0,128},{128,0},{1,129},{129,1},{2,130},{130,2},{3,131},{131,3},{4... | collective-permute-start | bytes 356360 | tf_op jit(solution)/shard_map/ppermute | solution.py:21
  39.5 19.1 %collective-permute-start = (bf16[116,128]{1,0:T(8,128)(2,1)}, bf16[116,128]{1,0:T(8,128)(2,1)S(1)}, u32[]{:S(2)}, u32[]{:S(2)}) collective-permute-start(bf16[116,128]{1,0:T(8,128)(2,1)} %bitcast.52), channel_id=1, source_target_pairs={{0,0},{1,4},{2,8},{3,12},{4,64},{5,68},{6,72},{7,76},{8,128},{9,13... | collective-permute-start | bytes 89096 | tf_op jit(solution)/shard_map/ppermute | solution.py:21
  58.6 37.1 %collective-permute-start.2 = (bf16[464,128]{1,0:T(8,128)(2,1)S(1)}, bf16[464,128]{1,0:T(8,128)(2,1)S(1)}, u32[]{:S(2)}, u32[]{:S(2)}) collective-permute-start(bf16[464,128]{1,0:T(8,128)(2,1)S(1)} %reshape.78), channel_id=1, source_target_pairs={{0,3},{1,0},{2,1},{3,2},{4,7},{5,4},{6,5},{7,6},{8,11},{9,8},{10,9... | collective-permute-start | bytes 356360 | tf_op jit(solution)/shard_map/ppermute | solution.py:21
  65.2 37.4 %all-to-all-start.1 = ((bf16[4,116,128]{2,1,0:T(8,128)(2,1)}), bf16[4,116,128]{2,1,0:T(8,128)(2,1)S(1)}, u32[]{:S(2)}, u32[]{:S(2)}) async-start(bf16[4,116,128]{2,1,0:T(8,128)(2,1)} %broadcast_in_dim.37), calls=%async_computation.1 | async-start | bytes 245760 | tf_op jit(solution)/shard_map/all_to_all | solution.py:31
  86.2 16.1 %collective-permute-start.3 = (bf16[464,128]{1,0:T(8,128)(2,1)S(1)}, bf16[464,128]{1,0:T(8,128)(2,1)S(1)}, u32[]{:S(2)}, u32[]{:S(2)}) collective-permute-start(bf16[464,128]{1,0:T(8,128)(2,1)S(1)} %reshape.78), channel_id=1, source_target_pairs={{0,2},{1,3},{2,0},{3,1},{4,6},{5,7},{6,4},{7,5},{8,10},{9,11},{10,... | collective-permute-start | bytes 356360 | tf_op jit(solution)/shard_map/ppermute | solution.py:21
  92.3 10.0 %collective-permute-start.4 = (bf16[464,128]{1,0:T(8,128)(2,1)S(1)}, bf16[464,128]{1,0:T(8,128)(2,1)S(1)}, u32[]{:S(2)}, u32[]{:S(2)}) collective-permute-start(bf16[464,128]{1,0:T(8,128)(2,1)S(1)} %reshape.78), channel_id=1, source_target_pairs={{0,1},{1,2},{2,3},{3,0},{4,5},{5,6},{6,7},{7,4},{8,9},{9,10},{10,1... | collective-permute-start | bytes 356360 | tf_op jit(solution)/shard_map/ppermute | solution.py:21
  103.5 21.2 %all-to-all-start.2 = ((bf16[4,464,128]{2,1,0:T(8,128)(2,1)}), bf16[4,464,128]{2,1,0:T(8,128)(2,1)S(1)}, u32[]{:S(2)}, u32[]{:S(2)}) async-start(bf16[4,464,128]{2,1,0:T(8,128)(2,1)} %broadcast_in_dim.77), calls=%async_computation.2 | async-start | bytes 950272 | tf_op jit(solution)/shard_map/all_to_all | solution.py:31
  112.5 20.2 %copy-start.4 = (bf16[128,464]{0,1:T(8,128)(2,1)S(1)}, bf16[128,464]{0,1:T(8,128)(2,1)}, u32[]{:S(2)}) copy-start(bf16[128,464]{0,1:T(8,128)(2,1)} %param.4) | copy-start | bytes 356356
  112.5 10.7 %collective-permute-start.5 = (bf16[1856,128]{1,0:T(8,128)(2,1)S(1)}, bf16[1856,128]{1,0:T(8,128)(2,1)S(1)}, u32[]{:S(2)}, u32[]{:S(2)}) collective-permute-start(bf16[1856,128]{1,0:T(8,128)(2,1)S(1)} %reshape.80), channel_id=1, source_target_pairs={{0,16},{16,32},{32,48},{48,0},{1,17},{17,33},{33,49},{49,1},{2,18}... | collective-permute-start | bytes 1425416 | tf_op jit(solution)/shard_map/ppermute | solution.py:21
  114.5 10.2 %collective-permute-start.6 = (bf16[1856,128]{1,0:T(8,128)(2,1)S(1)}, bf16[1856,128]{1,0:T(8,128)(2,1)S(1)}, u32[]{:S(2)}, u32[]{:S(2)}) collective-permute-start(bf16[1856,128]{1,0:T(8,128)(2,1)S(1)} %reshape.80), channel_id=1, source_target_pairs={{0,48},{16,0},{32,16},{48,32},{1,49},{17,1},{33,17},{49,33},{2,50}... | collective-permute-start | bytes 1425416 | tf_op jit(solution)/shard_map/ppermute | solution.py:21
  123.2 9.5 %copy-start.2 = (bf16[1856,128]{1,0:T(8,128)(2,1)}, bf16[1856,128]{1,0:T(8,128)(2,1)S(1)}, u32[]{:S(2)}) copy-start(bf16[1856,128]{1,0:T(8,128)(2,1)S(1)} %collective-permute-done.5) | copy-start | bytes 1425412
  125.7 13.9 %collective-permute-start.7 = (bf16[2784,128]{1,0:T(8,128)(2,1)}, bf16[2784,128]{1,0:T(8,128)(2,1)}, u32[]{:S(2)}, u32[]{:S(2)}) collective-permute-start(bf16[2784,128]{1,0:T(8,128)(2,1)} %get-tuple-element.31), channel_id=1, source_target_pairs={{0,16},{16,32},{32,48},{48,0},{1,17},{17,33},{33,49},{49,1},{2,18}... | collective-permute-start | bytes 2138120 | tf_op jit(solution)/shard_map/ppermute | solution.py:21
  127.6 13.7 %collective-permute-start.8 = (bf16[2784,128]{1,0:T(8,128)(2,1)S(1)}, bf16[2784,128]{1,0:T(8,128)(2,1)}, u32[]{:S(2)}, u32[]{:S(2)}) collective-permute-start(bf16[2784,128]{1,0:T(8,128)(2,1)S(1)} %get-tuple-element.30), channel_id=1, source_target_pairs={{0,48},{16,0},{32,16},{48,32},{1,49},{17,1},{33,17},{49,33},{2,50}... | collective-permute-start | bytes 2138120 | tf_op jit(solution)/shard_map/ppermute | solution.py:21
  133.7 13.3 %all-to-all-start.3 = ((bf16[4,2,464,128]{3,2,1,0:T(8,128)(2,1)}), bf16[4,2,464,128]{3,2,1,0:T(8,128)(2,1)S(1)}, u32[]{:S(2)}, u32[]{:S(2)}) async-start(bf16[4,2,464,128]{3,2,1,0:T(8,128)(2,1)} %broadcast_in_dim.79), calls=%async_computation.3 | async-start | bytes 1900544 | tf_op jit(solution)/shard_map/all_to_all | solution.py:31
  138.2 1.4 copy-start
  141.3 28.8 %copy-start.1 = (bf16[4,1856,128]{2,1,0:T(8,128)(2,1)S(1)}, bf16[4,1856,128]{2,1,0:T(8,128)(2,1)}, u32[]{:S(2)}) copy-start(bf16[4,1856,128]{2,1,0:T(8,128)(2,1)} %copy-done) | copy-start | bytes 5701636
  147.1 23.1 %copy-start.3 = (bf16[1856,128]{1,0:T(8,128)(2,1)S(1)}, bf16[1856,128]{1,0:T(8,128)(2,1)}, u32[]{:S(2)}) copy-start(bf16[1856,128]{1,0:T(8,128)(2,1)} %copy-done.2) | copy-start | bytes 1425412
  148.2 29.0 %collective-permute-start.10 = (bf16[928,128]{1,0:T(8,128)(2,1)S(1)}, bf16[928,128]{1,0:T(8,128)(2,1)S(1)}, u32[]{:S(2)}, u32[]{:S(2)}) collective-permute-start(bf16[928,128]{1,0:T(8,128)(2,1)S(1)} %get-tuple-element.26), channel_id=1, source_target_pairs={{0,16},{16,32},{32,48},{48,0},{1,17},{17,33},{33,49},{49,1},{2,18}... | collective-permute-start | bytes 712712 | tf_op jit(solution)/shard_map/ppermute | solution.py:21
  151.6 25.6 %collective-permute-start.11 = (bf16[928,128]{1,0:T(8,128)(2,1)S(1)}, bf16[928,128]{1,0:T(8,128)(2,1)S(1)}, u32[]{:S(2)}, u32[]{:S(2)}) collective-permute-start(bf16[928,128]{1,0:T(8,128)(2,1)S(1)} %get-tuple-element.28), channel_id=1, source_target_pairs={{0,48},{16,0},{32,16},{48,32},{1,49},{17,1},{33,17},{49,33},{2,50}... | collective-permute-start | bytes 712712 | tf_op jit(solution)/shard_map/ppermute | solution.py:21
  155.8 22.6 %collective-permute-start.9 = (bf16[4,2,464,128]{3,2,1,0:T(8,128)(2,1)S(1)}, bf16[4,2,464,128]{3,2,1,0:T(8,128)(2,1)S(1)}, u32[]{:S(2)}, u32[]{:S(2)}) collective-permute-start(bf16[4,2,464,128]{3,2,1,0:T(8,128)(2,1)S(1)} %all-to-all-done.3), channel_id=1, source_target_pairs={{0,64},{64,0},{1,65},{65,1},{2,66},{66,2},{3,67},{67,3},{4,68},{68... | collective-permute-start | bytes 2850824 | tf_op jit(solution)/shard_map/ppermute | solution.py:21

commit v4 on v3

--- a/solution.py
+++ b/solution.py
@@ -58,36 +58,44 @@
     scaled = (g.astype(jnp.float32) * scale[:, None]).astype(jnp.bfloat16)
 
     part = permute(g, AXES, lambda x, zh, c, y, za, zb: (y, za // 2, za % 2, x, zb, 2 * zh + c))
-    other = permute(a, ("zh",), lambda h: (1 - h,))
     rows = spread(scaled, "za").reshape(4 * cols, tokens)
-    part, rows, other = sync((part, rows, other))
+    part, rows, a = sync((part, rows, a))
 
     part = spread(part, "za").reshape(4 * cols, tokens)
     rows = ordered("zb", [rows] + [along_zb(rows, -k) for k in (1, 2, 3)])
     rows = rows.reshape(4, 4, cols, tokens).transpose(1, 0, 2, 3).reshape(16 * cols, tokens)
-    rows, part = sync((rows, part))
+    rows, part, a = sync((rows, part, a))
 
     rows_b, rows_a = along_y(rows, 1), along_y(rows, -1)
-    part = spread(part, "zb").reshape(16 * cols, tokens)
-    rows_b, rows_a, part, other = sync((rows_b, rows_a, part, other))
+    part = spread(part, "zb").reshape(2, 2, 4 * cols, tokens)
+    part = jnp.where(lax.axis_index("c") == 0, part, part[:, ::-1])
+    part = jnp.where(lax.axis_index("zh") == 0, part, part[::-1])
+    part = part.transpose(1, 0, 2, 3).reshape(16 * cols, tokens)
+    rows_b, rows_a, part, a = sync((rows_b, rows_a, part, a))
 
     up = along_y(jnp.concatenate([rows_b[:half], part]), 1)
     down = along_y(jnp.concatenate([rows_a[half:], part]), -1)
-    first = lax.axis_index("zh") == 0
-    acts = spread(jnp.where(first, jnp.stack([a, other]), jnp.stack([other, a])), "x")
-    up, down, acts = sync((up, down, acts))
+    other = permute(a, ("zh",), lambda h: (1 - h,))
+    up, down, a, other = sync((up, down, a, other))
     rows_o = jnp.concatenate([up[:half], down[:half]])
     part_b, part_a = up[half:], down[half:]
 
-    part_o = jnp.concatenate([along_y(part_b[:half], 1), along_y(part_a[half:], -1)])
-    acts_c = permute(acts, ("c",), lambda c: (1 - c,))
-    first = lax.axis_index("c") == 0
-    acts = jnp.where(first, jnp.stack([acts, acts_c], 2), jnp.stack([acts_c, acts], 2)).reshape(16, units, tokens)
-
+    part_o, part_oc = along_y(part_b[:half], 1), along_y(part_a[half:], -1)
+    acts = spread(jnp.stack([a, other]), "x")
+    part_o, part_oc, acts = sync((part_o, part_oc, acts))
     rows = ordered("y", [rows, rows_a, rows_o, rows_b]).reshape(64 * cols, tokens)
     input_grads = lax.dot_general(weight_codes, rows, (((1,), (0,)), ((), ())), preferred_element_type=jnp.float32)
-    part = ordered("y", [part, part_a, part_o, part_b]).reshape(16, 4 * cols, tokens)
-    weight_grads = lax.dot_general(acts, part, (((0, 2), (0, 2)), ((), ())), preferred_element_type=jnp.float32)
+
+    acts_c = permute(acts, ("c",), lambda c: (1 - c,))
+    weight_grads = 0.0
+    for mine, blocks in (
+        (acts, [part[:half], part_a[:half], part_o, part_b[:half]]),
+        (acts_c, [part[half:], part_a[half:], part_oc, part_b[half:]]),
+    ):
+        blocks = ordered("y", blocks).reshape(8, 4 * cols, tokens)
+        weight_grads += lax.dot_general(
+            mine.reshape(8, units, tokens), blocks, (((0, 2), (0, 2)), ((), ())), preferred_element_type=jnp.float32
+        )
     return input_grads.T, weight_grads
 
 

time: 182 us -> 195 us (1.071)
  the two profiles are of different devices: /device:TPU:1 before, /device:TPU:225 now
where the time goes in v4:
time: 195 us; the launch traced here: 194 us
  starting transfers between devices  101 us (52%)
  waiting for transfers between devices  70 us (36%)
  local copies, waits for them, and re-layouts  11 us (6%)
  matrix products  8.47 us (4%)
  other arithmetic  2.32 us (1%)
    ppermute x12, starting transfers between devices, permute(): return lax.ppermute(value, axes, pairs)  59.7 us
    ppermute x12, waiting for transfers between devices, permute(): return lax.ppermute(value, axes, pairs)  56 us
    all_to_all x4, starting transfers between devices, spread(): return lax.all_to_all(copies, axis, 0, 0, tiled=True)  41 us
    all_to_all x4, waiting for transfers between devices, spread(): return lax.all_to_all(copies, axis, 0, 0, tiled=True)  14 us
    dot_general x1, matrix products, per_device(): lax.dot_general(weight_codes, rows, (((1,), (0,)), ((), ())), preferred_e...  6.18 us
  transfers between devices with their start and end apart: 16, of which 9 were waited for; matrix products, arithmetic and copies ran while one was open for 6% of the time, Pallas kernels for 0%

profile of v4, /device:TPU:225, one launch (start us, length us, event | category | flops | bytes accessed | tf_op | source)
XLA Modules:
  0.0 193.7 jit_solution(7733685649877725613)
XLA Ops:
  0.6 0.8 dynamic_slice.3
  1.4 0.8 multiply_convert_fusion
  2.3 0.7 broadcast_in_dim.40
  2.9 19.9 %all-to-all-start = ((bf16[4,116,128]{2,1,0:T(8,128)(2,1)}), bf16[4,116,128]{2,1,0:T(8,128)(2,1)S(1)}, u32[]{:S(2)}, u32[]{:S(2)}) async-start(bf16[4,116,128]{2,1,0:T(8,128)(2,1)} %broadcast_in_dim.40), calls=%async_computation | async-start | bytes 245760 | tf_op jit(solution)/shard_map/all_to_all | solution.py:31
  22.8 9.1 %collective-permute-start = (bf16[116,128]{1,0:T(8,128)(2,1)}, bf16[116,128]{1,0:T(8,128)(2,1)S(1)}, u32[]{:S(2)}, u32[]{:S(2)}) collective-permute-start(bf16[116,128]{1,0:T(8,128)(2,1)} %bitcast.64), channel_id=1, source_target_pairs={{0,0},{1,4},{2,8},{3,12},{4,64},{5,68},{6,72},{7,76},{8,128},{9,13... | collective-permute-start | bytes 89096 | tf_op jit(solution)/shard_map/ppermute | solution.py:21
  31.9 3.0 %all-to-all-done = bf16[4,116,128]{2,1,0:T(8,128)(2,1)S(1)} async-done(((bf16[4,116,128]{2,1,0:T(8,128)(2,1)}), bf16[4,116,128]{2,1,0:T(8,128)(2,1)S(1)}, u32[]{:S(2)}, u32[]{:S(2)}) %all-to-all-start) | async-done | bytes 118816 | tf_op jit(solution)/shard_map/all_to_all | solution.py:31
  35.0 12.7 %collective-permute-done = bf16[116,128]{1,0:T(8,128)(2,1)S(1)} collective-permute-done((bf16[116,128]{1,0:T(8,128)(2,1)}, bf16[116,128]{1,0:T(8,128)(2,1)S(1)}, u32[]{:S(2)}, u32[]{:S(2)}) %collective-permute-start) | collective-permute-done | bytes 29728 | tf_op jit(solution)/shard_map/ppermute | solution.py:21
  47.6 3.1 %collective-permute-start.1 = (bf16[464,128]{1,0:T(8,128)(2,1)S(1)}, bf16[464,128]{1,0:T(8,128)(2,1)S(1)}, u32[]{:S(2)}, u32[]{:S(2)}) collective-permute-start(bf16[464,128]{1,0:T(8,128)(2,1)S(1)} %reshape.46), channel_id=1, source_target_pairs={{0,3},{1,0},{2,1},{3,2},{4,7},{5,4},{6,5},{7,6},{8,11},{9,8},{10,9... | collective-permute-start | bytes 356360 | tf_op jit(solution)/shard_map/ppermute | solution.py:21
  50.8 0.7 broadcast_in_dim.90
  51.4 6.6 %all-to-all-start.1 = ((bf16[4,116,128]{2,1,0:T(8,128)(2,1)}), bf16[4,116,128]{2,1,0:T(8,128)(2,1)S(1)}, u32[]{:S(2)}, u32[]{:S(2)}) async-start(bf16[4,116,128]{2,1,0:T(8,128)(2,1)} %broadcast_in_dim.90), calls=%async_computation.1 | async-start | bytes 245760 | tf_op jit(solution)/shard_map/all_to_all | solution.py:31
  58.1 1.9 collective-permute-start.2
  60.0 4.0 %collective-permute-start.3 = (bf16[464,128]{1,0:T(8,128)(2,1)S(1)}, bf16[464,128]{1,0:T(8,128)(2,1)S(1)}, u32[]{:S(2)}, u32[]{:S(2)}) collective-permute-start(bf16[464,128]{1,0:T(8,128)(2,1)S(1)} %reshape.46), channel_id=1, source_target_pairs={{0,1},{1,2},{2,3},{3,0},{4,5},{5,6},{6,7},{7,4},{8,9},{9,10},{10,1... | collective-permute-start | bytes 356360 | tf_op jit(solution)/shard_map/ppermute | solution.py:21
  64.0 0.0 collective-permute-done.1
  64.0 0.1 broadcast_in_dim.41
  64.1 7.2 %collective-permute-done.2 = bf16[464,128]{1,0:T(8,128)(2,1)S(1)} collective-permute-done((bf16[464,128]{1,0:T(8,128)(2,1)S(1)}, bf16[464,128]{1,0:T(8,128)(2,1)S(1)}, u32[]{:S(2)}, u32[]{:S(2)}) %collective-permute-start.2) | collective-permute-done | bytes 118816 | tf_op jit(solution)/shard_map/ppermute | solution.py:21
  71.3 0.6 collective-permute-done.3
  71.9 0.1 reshape.47
  72.0 0.1 reshape.48
  72.1 0.0 all-to-all-done.1
  72.2 0.8 broadcast_in_dim.92
  73.0 11.0 %all-to-all-start.2 = ((bf16[4,464,128]{2,1,0:T(8,128)(2,1)}), bf16[4,464,128]{2,1,0:T(8,128)(2,1)S(1)}, u32[]{:S(2)}, u32[]{:S(2)}) async-start(bf16[4,464,128]{2,1,0:T(8,128)(2,1)} %broadcast_in_dim.92), calls=%async_computation.2 | async-start | bytes 950272 | tf_op jit(solution)/shard_map/all_to_all | solution.py:31
  84.0 4.4 %collective-permute-start.4 = (bf16[1856,128]{1,0:T(8,128)(2,1)S(1)}, bf16[1856,128]{1,0:T(8,128)(2,1)S(1)}, u32[]{:S(2)}, u32[]{:S(2)}) collective-permute-start(bf16[1856,128]{1,0:T(8,128)(2,1)S(1)} %reshape.48), channel_id=1, source_target_pairs={{0,16},{16,32},{32,48},{48,0},{1,17},{17,33},{33,49},{49,1},{2,18}... | collective-permute-start | bytes 1425416 | tf_op jit(solution)/shard_map/ppermute | solution.py:21
  88.5 5.4 %collective-permute-start.5 = (bf16[1856,128]{1,0:T(8,128)(2,1)S(1)}, bf16[1856,128]{1,0:T(8,128)(2,1)S(1)}, u32[]{:S(2)}, u32[]{:S(2)}) collective-permute-start(bf16[1856,128]{1,0:T(8,128)(2,1)S(1)} %reshape.48), channel_id=1, source_target_pairs={{0,48},{16,0},{32,16},{48,32},{1,49},{17,1},{33,17},{49,33},{2,50}... | collective-permute-start | bytes 1425416 | tf_op jit(solution)/shard_map/ppermute | solution.py:21
  93.9 1.2 all-to-all-done.2
  95.1 0.1 reverse_select_fusion.1
  95.2 0.1 fusion.1
  95.3 0.0 copy-start.9
  95.3 6.9 %collective-permute-done.4 = bf16[1856,128]{1,0:T(8,128)(2,1)S(1)} collective-permute-done((bf16[1856,128]{1,0:T(8,128)(2,1)S(1)}, bf16[1856,128]{1,0:T(8,128)(2,1)S(1)}, u32[]{:S(2)}, u32[]{:S(2)}) %collective-permute-start.4) | collective-permute-done | bytes 475168 | tf_op jit(solution)/shard_map/ppermute | solution.py:21
  102.2 2.1 %collective-permute-done.5 = bf16[1856,128]{1,0:T(8,128)(2,1)S(1)} collective-permute-done((bf16[1856,128]{1,0:T(8,128)(2,1)S(1)}, bf16[1856,128]{1,0:T(8,128)(2,1)S(1)}, u32[]{:S(2)}, u32[]{:S(2)}) %collective-permute-start.5) | collective-permute-done | bytes 475168 | tf_op jit(solution)/shard_map/ppermute | solution.py:21
  104.3 0.1 pad_maximum_fusion
  104.4 3.1 %collective-permute-start.6 = (bf16[2784,128]{1,0:T(8,128)(2,1)S(1)}, bf16[2784,128]{1,0:T(8,128)(2,1)S(1)}, u32[]{:S(2)}, u32[]{:S(2)}) collective-permute-start(bf16[2784,128]{1,0:T(8,128)(2,1)S(1)} %get-tuple-element.47), channel_id=1, source_target_pairs={{0,16},{16,32},{32,48},{48,0},{1,17},{17,33},{33,49},{49,1},{2,18}... | collective-permute-start | bytes 2138120 | tf_op jit(solution)/shard_map/ppermute | solution.py:21
  107.5 3.4 %collective-permute-start.7 = (bf16[2784,128]{1,0:T(8,128)(2,1)S(1)}, bf16[2784,128]{1,0:T(8,128)(2,1)S(1)}, u32[]{:S(2)}, u32[]{:S(2)}) collective-permute-start(bf16[2784,128]{1,0:T(8,128)(2,1)S(1)} %get-tuple-element.46), channel_id=1, source_target_pairs={{0,48},{16,0},{32,16},{48,32},{1,49},{17,1},{33,17},{49,33},{2,50}... | collective-permute-start | bytes 2138120 | tf_op jit(solution)/shard_map/ppermute | solution.py:21
  111.0 14.6 %collective-permute-start.8 = (bf16[464,128]{1,0:T(8,128)(2,1)S(1)}, bf16[464,128]{1,0:T(8,128)(2,1)S(1)}, u32[]{:S(2)}, u32[]{:S(2)}) collective-permute-start(bf16[464,128]{1,0:T(8,128)(2,1)S(1)} %bitcast.61), channel_id=1, source_target_pairs={{0,128},{128,0},{1,129},{129,1},{2,130},{130,2},{3,131},{131,3},{4... | collective-permute-start | bytes 356360 | tf_op jit(solution)/shard_map/ppermute | solution.py:21
  125.6 0.0 copy-start.6
  125.6 0.2 broadcast_in_dim.91
  125.8 0.8 copy-done.6
  126.6 0.1 bitcast_dynamic-update-slice_fusion.1
  126.7 0.8 fusion.5
  127.5 26.7 %collective-permute-done.8 = bf16[464,128]{1,0:T(8,128)(2,1)S(1)} collective-permute-done((bf16[464,128]{1,0:T(8,128)(2,1)S(1)}, bf16[464,128]{1,0:T(8,128)(2,1)S(1)}, u32[]{:S(2)}, u32[]{:S(2)}) %collective-permute-start.8) | collective-permute-done | bytes 118816 | tf_op jit(solution)/shard_map/ppermute | solution.py:21
  154.1 0.0 collective-permute-done.6
  154.1 0.0 collective-permute-done.7
  154.2 0.9 fusion.3
  155.0 0.2 copy-done.1
  155.2 0.8 fusion.4
  156.0 1.9 collective-permute-start.9
  157.9 4.6 %collective-permute-start.10 = (bf16[928,128]{1,0:T(8,128)(2,1)}, bf16[928,128]{1,0:T(8,128)(2,1)}, u32[]{:S(2)}, u32[]{:S(2)}) collective-permute-start(bf16[928,128]{1,0:T(8,128)(2,1)} %get-tuple-element.40), channel_id=1, source_target_pairs={{0,48},{16,0},{32,16},{48,32},{1,49},{17,1},{33,17},{49,33},{2,50}... | collective-permute-start | bytes 712712 | tf_op jit(solution)/shard_map/ppermute | solution.py:21
  162.5 1.1 broadcast_in_dim.96
  163.6 3.5 %all-to-all-start.3 = ((bf16[4,2,464,128]{3,2,1,0:T(8,128)(2,1)}), bf16[4,2,464,128]{3,2,1,0:T(8,128)(2,1)S(1)}, u32[]{:S(2)}, u32[]{:S(2)}) async-start(bf16[4,2,464,128]{3,2,1,0:T(8,128)(2,1)} %broadcast_in_dim.96), calls=%async_computation.3 | async-start | bytes 1900544 | tf_op jit(solution)/shard_map/all_to_all | solution.py:31
  167.1 1.2 fusion.2
  168.3 0.1 bitcast_dynamic-update-slice_fusion
  168.4 1.3 copy-done
  169.7 0.1 broadcast_in_dim.97
  169.8 0.1 broadcast_in_dim.101
  169.9 0.1 bitcast_dynamic-update-slice_fusion.7
  170.0 0.0 collective-permute-done.9
  170.0 0.0 collective-permute-done.10
  170.0 9.7 %all-to-all-done.3 = bf16[4,2,464,128]{3,2,1,0:T(8,128)(2,1)S(1)} async-done(((bf16[4,2,464,128]{3,2,1,0:T(8,128)(2,1)}), bf16[4,2,464,128]{3,2,1,0:T(8,128)(2,1)S(1)}, u32[]{:S(2)}, u32[]{:S(2)}) %all-to-all-start.3) | async-done | bytes 950304 | tf_op jit(solution)/shard_map/all_to_all | solution.py:31
  179.8 4.2 %collective-permute-start.11 = (bf16[4,2,464,128]{3,2,1,0:T(8,128)(2,1)S(1)}, bf16[4,2,464,128]{3,2,1,0:T(8,128)(2,1)S(1)}, u32[]{:S(2)}, u32[]{:S(2)}) collective-permute-start(bf16[4,2,464,128]{3,2,1,0:T(8,128)(2,1)S(1)} %all-to-all-done.3), channel_id=1, source_target_pairs={{0,64},{64,0},{1,65},{65,1},{2,66},{66,2},{3,67},{67,3},{4,68},{68... | collective-permute-start | bytes 2850824 | tf_op jit(solution)/shard_map/ppermute | solution.py:21
  184.0 6.2 %fusion.6 = f32[128,464]{0,1:T(8,128)} fusion(bf16[464,7424]{1,0:T(8,128)(2,1)} %param.5, bf16[7424,128]{1,0:T(8,128)(2,1)} %bitcast.58), kind=kOutput, calls=%fused_computation.26 | convolution fusion | flops 881852416 | bytes 9027584 | tf_op jit(solution)/shard_map/dot_general | solution.py:87
  190.2 1.1 bitcast_dynamic-update-slice_fusion.3
  191.3 0.1 bitcast_dynamic-update-slice_fusion.5
  191.4 0.0 collective-permute-done.11
  191.4 0.7 convolution_bitcast_fusion
  192.1 1.6 fusion
  (25 shorter events, 0.3 us)
Async XLA Ops:
  2.9 32.0 %all-to-all-start = ((bf16[4,116,128]{2,1,0:T(8,128)(2,1)}), bf16[4,116,128]{2,1,0:T(8,128)(2,1)S(1)}, u32[]{:S(2)}, u32[]{:S(2)}) async-start(bf16[4,116,128]{2,1,0:T(8,128)(2,1)} %broadcast_in_dim.40), calls=%async_computation | async-start | bytes 245760 | tf_op jit(solution)/shard_map/all_to_all | solution.py:31
  22.8 24.8 %collective-permute-start = (bf16[116,128]{1,0:T(8,128)(2,1)}, bf16[116,128]{1,0:T(8,128)(2,1)S(1)}, u32[]{:S(2)}, u32[]{:S(2)}) collective-permute-start(bf16[116,128]{1,0:T(8,128)(2,1)} %bitcast.64), channel_id=1, source_target_pairs={{0,0},{1,4},{2,8},{3,12},{4,64},{5,68},{6,72},{7,76},{8,128},{9,13... | collective-permute-start | bytes 89096 | tf_op jit(solution)/shard_map/ppermute | solution.py:21
  47.6 16.3 %collective-permute-start.1 = (bf16[464,128]{1,0:T(8,128)(2,1)S(1)}, bf16[464,128]{1,0:T(8,128)(2,1)S(1)}, u32[]{:S(2)}, u32[]{:S(2)}) collective-permute-start(bf16[464,128]{1,0:T(8,128)(2,1)S(1)} %reshape.46), channel_id=1, source_target_pairs={{0,3},{1,0},{2,1},{3,2},{4,7},{5,4},{6,5},{7,6},{8,11},{9,8},{10,9... | collective-permute-start | bytes 356360 | tf_op jit(solution)/shard_map/ppermute | solution.py:21
  51.4 20.7 %all-to-all-start.1 = ((bf16[4,116,128]{2,1,0:T(8,128)(2,1)}), bf16[4,116,128]{2,1,0:T(8,128)(2,1)S(1)}, u32[]{:S(2)}, u32[]{:S(2)}) async-start(bf16[4,116,128]{2,1,0:T(8,128)(2,1)} %broadcast_in_dim.90), calls=%async_computation.1 | async-start | bytes 245760 | tf_op jit(solution)/shard_map/all_to_all | solution.py:31
  58.1 13.2 %collective-permute-start.2 = (bf16[464,128]{1,0:T(8,128)(2,1)S(1)}, bf16[464,128]{1,0:T(8,128)(2,1)S(1)}, u32[]{:S(2)}, u32[]{:S(2)}) collective-permute-start(bf16[464,128]{1,0:T(8,128)(2,1)S(1)} %reshape.46), channel_id=1, source_target_pairs={{0,2},{1,3},{2,0},{3,1},{4,6},{5,7},{6,4},{7,5},{8,10},{9,11},{10,... | collective-permute-start | bytes 356360 | tf_op jit(solution)/shard_map/ppermute | solution.py:21
  60.0 11.9 %collective-permute-start.3 = (bf16[464,128]{1,0:T(8,128)(2,1)S(1)}, bf16[464,128]{1,0:T(8,128)(2,1)S(1)}, u32[]{:S(2)}, u32[]{:S(2)}) collective-permute-start(bf16[464,128]{1,0:T(8,128)(2,1)S(1)} %reshape.46), channel_id=1, source_target_pairs={{0,1},{1,2},{2,3},{3,0},{4,5},{5,6},{6,7},{7,4},{8,9},{9,10},{10,1... | collective-permute-start | bytes 356360 | tf_op jit(solution)/shard_map/ppermute | solution.py:21
  73.0 22.1 %all-to-all-start.2 = ((bf16[4,464,128]{2,1,0:T(8,128)(2,1)}), bf16[4,464,128]{2,1,0:T(8,128)(2,1)S(1)}, u32[]{:S(2)}, u32[]{:S(2)}) async-start(bf16[4,464,128]{2,1,0:T(8,128)(2,1)} %broadcast_in_dim.92), calls=%async_computation.2 | async-start | bytes 950272 | tf_op jit(solution)/shard_map/all_to_all | solution.py:31
  84.0 18.2 %collective-permute-start.4 = (bf16[1856,128]{1,0:T(8,128)(2,1)S(1)}, bf16[1856,128]{1,0:T(8,128)(2,1)S(1)}, u32[]{:S(2)}, u32[]{:S(2)}) collective-permute-start(bf16[1856,128]{1,0:T(8,128)(2,1)S(1)} %reshape.48), channel_id=1, source_target_pairs={{0,16},{16,32},{32,48},{48,0},{1,17},{17,33},{33,49},{49,1},{2,18}... | collective-permute-start | bytes 1425416 | tf_op jit(solution)/shard_map/ppermute | solution.py:21
  88.5 15.8 %collective-permute-start.5 = (bf16[1856,128]{1,0:T(8,128)(2,1)S(1)}, bf16[1856,128]{1,0:T(8,128)(2,1)S(1)}, u32[]{:S(2)}, u32[]{:S(2)}) collective-permute-start(bf16[1856,128]{1,0:T(8,128)(2,1)S(1)} %reshape.48), channel_id=1, source_target_pairs={{0,48},{16,0},{32,16},{48,32},{1,49},{17,1},{33,17},{49,33},{2,50}... | collective-permute-start | bytes 1425416 | tf_op jit(solution)/shard_map/ppermute | solution.py:21
  95.3 15.6 %copy-start.9 = (bf16[128,464]{0,1:T(8,128)(2,1)S(1)}, bf16[128,464]{0,1:T(8,128)(2,1)}, u32[]{:S(2)}) copy-start(bf16[128,464]{0,1:T(8,128)(2,1)} %param.4) | copy-start | bytes 356356
  104.3 6.7 %copy-start.5 = (bf16[1856,128]{1,0:T(8,128)(2,1)}, bf16[1856,128]{1,0:T(8,128)(2,1)S(1)}, u32[]{:S(2)}) copy-start(bf16[1856,128]{1,0:T(8,128)(2,1)S(1)} %collective-permute-done.5) | copy-start | bytes 1425412
  104.4 49.7 %collective-permute-start.6 = (bf16[2784,128]{1,0:T(8,128)(2,1)S(1)}, bf16[2784,128]{1,0:T(8,128)(2,1)S(1)}, u32[]{:S(2)}, u32[]{:S(2)}) collective-permute-start(bf16[2784,128]{1,0:T(8,128)(2,1)S(1)} %get-tuple-element.47), channel_id=1, source_target_pairs={{0,16},{16,32},{32,48},{48,0},{1,17},{17,33},{33,49},{49,1},{2,18}... | collective-permute-start | bytes 2138120 | tf_op jit(solution)/shard_map/ppermute | solution.py:21
  107.5 46.6 %collective-permute-start.7 = (bf16[2784,128]{1,0:T(8,128)(2,1)S(1)}, bf16[2784,128]{1,0:T(8,128)(2,1)S(1)}, u32[]{:S(2)}, u32[]{:S(2)}) collective-permute-start(bf16[2784,128]{1,0:T(8,128)(2,1)S(1)} %get-tuple-element.46), channel_id=1, source_target_pairs={{0,48},{16,0},{32,16},{48,32},{1,49},{17,1},{33,17},{49,33},{2,50}... | collective-permute-start | bytes 2138120 | tf_op jit(solution)/shard_map/ppermute | solution.py:21
  111.0 43.2 %collective-permute-start.8 = (bf16[464,128]{1,0:T(8,128)(2,1)S(1)}, bf16[464,128]{1,0:T(8,128)(2,1)S(1)}, u32[]{:S(2)}, u32[]{:S(2)}) collective-permute-start(bf16[464,128]{1,0:T(8,128)(2,1)S(1)} %bitcast.61), channel_id=1, source_target_pairs={{0,128},{128,0},{1,129},{129,1},{2,130},{130,2},{3,131},{131,3},{4... | collective-permute-start | bytes 356360 | tf_op jit(solution)/shard_map/ppermute | solution.py:21
  125.6 1.0 copy-start.6
  154.1 1.1 copy-start.1
  154.1 1.8 copy-start.3
  156.0 14.0 %collective-permute-start.9 = (bf16[928,128]{1,0:T(8,128)(2,1)}, bf16[928,128]{1,0:T(8,128)(2,1)}, u32[]{:S(2)}, u32[]{:S(2)}) collective-permute-start(bf16[928,128]{1,0:T(8,128)(2,1)} %get-tuple-element.42), channel_id=1, source_target_pairs={{0,16},{16,32},{32,48},{48,0},{1,17},{17,33},{33,49},{49,1},{2,18}... | collective-permute-start | bytes 712712 | tf_op jit(solution)/shard_map/ppermute | solution.py:21
  157.9 12.1 %collective-permute-start.10 = (bf16[928,128]{1,0:T(8,128)(2,1)}, bf16[928,128]{1,0:T(8,128)(2,1)}, u32[]{:S(2)}, u32[]{:S(2)}) collective-permute-start(bf16[928,128]{1,0:T(8,128)(2,1)} %get-tuple-element.40), channel_id=1, source_target_pairs={{0,48},{16,0},{32,16},{48,32},{1,49},{17,1},{33,17},{49,33},{2,50}... | collective-permute-start | bytes 712712 | tf_op jit(solution)/shard_map/ppermute | solution.py:21
  163.6 16.2 %all-to-all-start.3 = ((bf16[4,2,464,128]{3,2,1,0:T(8,128)(2,1)}), bf16[4,2,464,128]{3,2,1,0:T(8,128)(2,1)S(1)}, u32[]{:S(2)}, u32[]{:S(2)}) async-start(bf16[4,2,464,128]{3,2,1,0:T(8,128)(2,1)} %broadcast_in_dim.96), calls=%async_computation.3 | async-start | bytes 1900544 | tf_op jit(solution)/shard_map/all_to_all | solution.py:31
  167.1 2.6 %copy-start.8 = (bf16[928,128]{1,0:T(8,128)(2,1)S(1)}, bf16[928,128]{1,0:T(8,128)(2,1)}, u32[]{:S(2)}) copy-start(bf16[928,128]{1,0:T(8,128)(2,1)} %get-tuple-element.44) | copy-start | bytes 712708
  167.1 2.7 %copy-start.7 = (bf16[928,128]{1,0:T(8,128)(2,1)S(1)}, bf16[928,128]{1,0:T(8,128)(2,1)}, u32[]{:S(2)}) copy-start(bf16[928,128]{1,0:T(8,128)(2,1)} %get-tuple-element.45) | copy-start | bytes 712708
  168.3 1.6 copy-start.4
  168.4 1.3 copy-start
  179.8 11.6 %collective-permute-start.11 = (bf16[4,2,464,128]{3,2,1,0:T(8,128)(2,1)S(1)}, bf16[4,2,464,128]{3,2,1,0:T(8,128)(2,1)S(1)}, u32[]{:S(2)}, u32[]{:S(2)}) collective-permute-start(bf16[4,2,464,128]{3,2,1,0:T(8,128)(2,1)S(1)} %all-to-all-done.3), channel_id=1, source_target_pairs={{0,64},{64,0},{1,65},{65,1},{2,66},{66,2},{3,67},{67,3},{4,68},{68... | collective-permute-start | bytes 2850824 | tf_op jit(solution)/shard_map/ppermute | solution.py:21
  184.0 7.3 %copy-start.2 = (bf16[2784,128]{1,0:T(8,128)(2,1)S(1)}, bf16[2784,128]{1,0:T(8,128)(2,1)}, u32[]{:S(2)}) copy-start(bf16[2784,128]{1,0:T(8,128)(2,1)} %copy-done.1) | copy-start | bytes 2138116

commit v5 on v4

v5 whole, which is shorter than its diff:
```python
import itertools

import jax
import jax.numpy as jnp
import numpy as np
from jax import lax
from jax.sharding import Mesh, PartitionSpec as P

AXES = ("x", "zh", "c", "y", "za", "zb")
SIZES = (4, 2, 2, 4, 4, 4)
DP = ("x", "zh", "c")
TENSOR = ("y", "za", "zb")


def permute(value, axes, target):
    sizes = [SIZES[AXES.index(a)] for a in axes]
    pairs = []
    for place in itertools.product(*map(range, sizes)):
        to = target(*place)
        pairs.append((int(np.ravel_multi_index(place, sizes)), int(np.ravel_multi_index(to, sizes))))
    return lax.ppermute(value, axes, pairs)


def along_y(value, step):
    return permute(value, ("y",), lambda y: ((y + step) % 4,))


def spread(value, axis):
    n = SIZES[AXES.index(axis)]
    copies = jnp.broadcast_to(value[None], (n,) + value.shape)
    return lax.all_to_all(copies, axis, 0, 0, tiled=True)


def ordered(axis, blocks):
    me = lax.axis_index(axis)
    ring = jnp.broadcast_to(blocks[0][None], (4,) + blocks[0].shape)
    for k, block in enumerate(blocks[1:], 1):
        ring = lax.dynamic_update_slice(ring, block[None], ((me + k) % 4,) + (0,) * block.ndim)
    return ring


sync = lax.optimization_barrier


def per_device(activations, weight_codes, channel_scale, output_grads):
    a = activations.T
    g = output_grads.T
    tokens = a.shape[1]
    cols = g.shape[0]
    half = 8 * cols

    me = lax.axis_index(TENSOR)
    scale = lax.dynamic_slice(channel_scale, (me * cols,), (cols,))
    scaled = (g.astype(jnp.float32) * scale[:, None]).astype(jnp.bfloat16)

    part = permute(g, AXES, lambda x, zh, c, y, za, zb: (y, za // 2, za % 2, x, 2 * zh + c, zb))
    near = spread(a, "x")
    part, near, scaled, a = sync((part, near, scaled, a))

    both = spread(jnp.concatenate([scaled, part]), "za").reshape(8 * cols, tokens)
    both, near, a = sync((both, near, a))

    both = spread(both, "zb").reshape(4, 4, 2, cols, tokens).transpose(2, 1, 0, 3, 4)
    rows = both[0].reshape(2, half, tokens)
    part = both[1].reshape(2, 2, 4 * cols, tokens)
    part = jnp.where(lax.axis_index("c") == 0, part, part[:, ::-1])
    part = jnp.where(lax.axis_index("zh") == 0, part, part[::-1])
    part = part.reshape(2, half, tokens)
    both = jnp.stack([rows, part], 1)
    both, near, a = sync((both, near, a))

    behind, ahead = along_y(both, 1), along_y(both, -1)
    far = permute(a, ("zh",), lambda h: (1 - h,))
    both, behind, ahead, far, near = sync((both, behind, ahead, far, near))

    opposite = jnp.stack([along_y(behind[0], 1), along_y(ahead[1], -1)])
    far = spread(far, "x")
    near_c = permute(near, ("c",), lambda c: (1 - c,))
    opposite, far, near, near_c = sync((opposite, far, near, near_c))

    far_c = permute(far, ("c",), lambda c: (1 - c,))
    around = [both, ahead, opposite, behind]
    rows = ordered("y", [v[:, 0] for v in around]).reshape(64 * cols, tokens)
    input_grads = lax.dot_general(weight_codes, rows, (((1,), (0,)), ((), ())), preferred_element_type=jnp.float32)
    part = [[v[h, 1].reshape(2, 4 * cols, tokens) for v in around] for h in (0, 1)]
    weight_grads = 0.0
    for mine, blocks in (
        (jnp.stack([near, near_c], 1), part[0]),
        (far[:, None], [v[:1] for v in part[1]]),
        (far_c[:, None], [v[1:] for v in part[1]]),
    ):
        weight_grads += lax.dot_general(
            mine, ordered("y", blocks), (((0, 1, 3), (0, 1, 3)), ((), ())), preferred_element_type=jnp.float32
        )
    return input_grads.T, weight_grads


def solution(mesh):
    fine = Mesh(mesh.devices.reshape(SIZES), AXES)
    placed = (P(DP, TENSOR), P(TENSOR, None), P(), P(DP, TENSOR))
    return jax.shard_map(
        per_device,
        mesh=fine,
        in_specs=placed,
        out_specs=(P(DP, TENSOR), P(TENSOR, DP)),
        check_vma=False,
    )
```

time: 195 us -> 191 us (0.979)
  the two profiles are of different devices: /device:TPU:225 before, /device:TPU:1 now
where the time goes in v5:
time: 191 us; the launch traced here: 190 us
  starting transfers between devices  55.2 us (29%)
  blocking collectives  53.7 us (28%)
  waiting for transfers between devices  51.2 us (27%)
  local copies, waits for them, and re-layouts  15.7 us (8%)
  matrix products  10.6 us (6%)
  other arithmetic  2.38 us (1%)
    all_to_all x1, blocking collectives, spread(): return lax.all_to_all(copies, axis, 0, 0, tiled=True)  53.7 us
    ppermute x8, starting transfers between devices, permute(): return lax.ppermute(value, axes, pairs)  42.3 us
    ppermute x8, waiting for transfers between devices, permute(): return lax.ppermute(value, axes, pairs)  27.5 us
    all_to_all x3, waiting for transfers between devices, spread(): return lax.all_to_all(copies, axis, 0, 0, tiled=True)  23.8 us
    all_to_all x3, starting transfers between devices, spread(): return lax.all_to_all(copies, axis, 0, 0, tiled=True)  12.8 us
    dot_general x1, matrix products, per_device(): lax.dot_general(weight_codes, rows, (((1,), (0,)), ((), ())), preferred_e...  5.66 us
    dot_general x3, matrix products, per_device(): lax.dot_general(mine, ordered('y', blocks), (((0, 1, 3), (0, 1, 3)), ((),...  4.98 us
  transfers between devices with their start and end apart: 11, of which 3 were waited for; matrix products, arithmetic and copies ran while one was open for 8% of the time, Pallas kernels for 0%

profile of v5, /device:TPU:1, one launch (start us, length us, event | category | flops | bytes accessed | tf_op | source)
XLA Modules:
  0.0 189.9 jit_solution(13913833805980730847)
XLA Ops:
  0.6 1.7 broadcast_in_dim.20
  2.4 4.8 %all-to-all-start = ((bf16[4,464,128]{2,1,0:T(8,128)(2,1)}), bf16[4,464,128]{2,1,0:T(8,128)(2,1)S(1)}, u32[]{:S(2)}, u32[]{:S(2)}) async-start(bf16[4,464,128]{2,1,0:T(8,128)(2,1)} %broadcast_in_dim.20), calls=%async_computation | async-start | bytes 950272 | tf_op jit(solution)/shard_map/all_to_all | solution.py:31
  7.2 9.6 %collective-permute-start = (bf16[116,128]{1,0:T(8,128)(2,1)}, bf16[116,128]{1,0:T(8,128)(2,1)S(1)}, u32[]{:S(2)}, u32[]{:S(2)}) collective-permute-start(bf16[116,128]{1,0:T(8,128)(2,1)} %bitcast.75), channel_id=1, source_target_pairs={{0,0},{1,1},{2,2},{3,3},{4,64},{5,65},{6,66},{7,67},{8,128},{9,129... | collective-permute-start | bytes 89096 | tf_op jit(solution)/shard_map/ppermute | solution.py:21
  16.9 0.8 dynamic_slice.3
  17.7 0.8 multiply_convert_fusion
  18.5 0.1 collective-permute-done
  18.6 0.0 all-to-all-done
  18.6 0.8 copy-done.6
  19.5 53.7 %all_to_all.20 = bf16[4,232,128]{2,1,0:T(8,128)(2,1)S(1)} all-to-all(bf16[4,232,128]{2,1,0:T(8,128)(2,1)S(1)} %broadcast_in_dim.21), channel_id=1, replica_groups=mesh['x'=4,'zh'=2,'c'=2,'y'=4,'za'=4,'zb'=4] {'za'}, dimensions={0} | all-to-all | bytes 475136 | tf_op jit(solution)/shard_map/all_to_all | solution.py:31
  73.1 1.1 broadcast_in_dim.22
  74.2 3.5 %all-to-all-start.2 = ((bf16[4,928,128]{2,1,0:T(8,128)(2,1)}), bf16[4,928,128]{2,1,0:T(8,128)(2,1)S(1)}, u32[]{:S(2)}, u32[]{:S(2)}) async-start(bf16[4,928,128]{2,1,0:T(8,128)(2,1)} %broadcast_in_dim.22), calls=%async_computation.2 | async-start | bytes 1900544 | tf_op jit(solution)/shard_map/all_to_all | solution.py:31
  77.7 23.8 %all-to-all-done.2 = bf16[4,928,128]{2,1,0:T(8,128)(2,1)S(1)} async-done(((bf16[4,928,128]{2,1,0:T(8,128)(2,1)}), bf16[4,928,128]{2,1,0:T(8,128)(2,1)S(1)}, u32[]{:S(2)}, u32[]{:S(2)}) %all-to-all-start.2) | async-done | bytes 950304 | tf_op jit(solution)/shard_map/all_to_all | solution.py:31
  101.5 0.2 reshape.71
  101.7 0.1 fusion.6
  101.8 0.1 reshape_squeeze.2
  102.0 0.1 stack_reshape_squeeze.3
  102.1 0.1 reverse_select_fusion.1
  102.2 0.1 reverse_select_fusion
  102.3 0.0 copy-start.8
  102.3 0.1 pad_maximum_fusion
  102.4 1.0 copy.9
  103.4 5.5 %collective-permute-start.1 = (bf16[2,2,928,128]{3,2,1,0:T(8,128)(2,1)}, bf16[2,2,928,128]{3,2,1,0:T(8,128)(2,1)S(1)}, u32[]{:S(2)}, u32[]{:S(2)}) collective-permute-start(bf16[2,2,928,128]{3,2,1,0:T(8,128)(2,1)} %copy.9), channel_id=1, source_target_pairs={{0,16},{16,32},{32,48},{48,0},{1,17},{17,33},{33,49},{49,1},{2,18}... | collective-permute-start | bytes 2850824 | tf_op jit(solution)/shard_map/ppermute | solution.py:21
  108.9 3.3 %collective-permute-start.2 = (bf16[2,2,928,128]{3,2,0,1:T(8,128)(2,1)S(1)}, bf16[2,2,928,128]{3,2,0,1:T(8,128)(2,1)S(1)}, u32[]{:S(2)}, u32[]{:S(2)}) collective-permute-start(bf16[2,2,928,128]{3,2,0,1:T(8,128)(2,1)S(1)} %pad_maximum_fusion), channel_id=1, source_target_pairs={{0,48},{16,0},{32,16},{48,32},{1,49},{17,1},{33,17},{49,33},{2,50}... | collective-permute-start | bytes 2850824 | tf_op jit(solution)/shard_map/ppermute | solution.py:21
  112.2 1.9 %collective-permute-start.3 = (bf16[464,128]{1,0:T(8,128)(2,1)S(1)}, bf16[464,128]{1,0:T(8,128)(2,1)S(1)}, u32[]{:S(2)}, u32[]{:S(2)}) collective-permute-start(bf16[464,128]{1,0:T(8,128)(2,1)S(1)} %bitcast.74), channel_id=1, source_target_pairs={{0,128},{128,0},{1,129},{129,1},{2,130},{130,2},{3,131},{131,3},{4... | collective-permute-start | bytes 356360 | tf_op jit(solution)/shard_map/ppermute | solution.py:21
  114.2 27.3 %collective-permute-done.3 = bf16[464,128]{1,0:T(8,128)(2,1)S(1)} collective-permute-done((bf16[464,128]{1,0:T(8,128)(2,1)S(1)}, bf16[464,128]{1,0:T(8,128)(2,1)S(1)}, u32[]{:S(2)}, u32[]{:S(2)}) %collective-permute-start.3) | collective-permute-done | bytes 118816 | tf_op jit(solution)/shard_map/ppermute | solution.py:21
  141.4 0.0 collective-permute-done.1
  141.4 0.0 collective-permute-done.2
  141.4 0.7 slice.89
  142.2 0.8 slice_bitcast_fusion
  143.0 0.8 slice_bitcast_fusion.1
  143.8 0.7 slice.91
  144.5 0.7 slice.88
  145.2 3.3 %collective-permute-start.5 = (bf16[2,928,128]{2,1,0:T(8,128)(2,1)}, bf16[2,928,128]{2,1,0:T(8,128)(2,1)}, u32[]{:S(2)}, u32[]{:S(2)}) collective-permute-start(bf16[2,928,128]{2,1,0:T(8,128)(2,1)} %slice_bitcast_fusion), channel_id=1, source_target_pairs={{0,48},{16,0},{32,16},{48,32},{1,49},{17,1},{33,17},{49,33},{2,50}... | collective-permute-start | bytes 1425416 | tf_op jit(solution)/shard_map/ppermute | solution.py:21
  148.6 1.9 %collective-permute-start.4 = (bf16[2,928,128]{2,1,0:T(8,128)(2,1)}, bf16[2,928,128]{2,1,0:T(8,128)(2,1)}, u32[]{:S(2)}, u32[]{:S(2)}) collective-permute-start(bf16[2,928,128]{2,1,0:T(8,128)(2,1)} %slice_bitcast_fusion.1), channel_id=1, source_target_pairs={{0,16},{16,32},{32,48},{48,0},{1,17},{17,33},{33,49},{49,1},{2,18}... | collective-permute-start | bytes 1425416 | tf_op jit(solution)/shard_map/ppermute | solution.py:21
  150.5 0.8 broadcast_in_dim.25
  151.3 4.5 %all-to-all-start.3 = ((bf16[4,464,128]{2,1,0:T(8,128)(2,1)}), bf16[4,464,128]{2,1,0:T(8,128)(2,1)}, u32[]{:S(2)}, u32[]{:S(2)}) async-start(bf16[4,464,128]{2,1,0:T(8,128)(2,1)} %broadcast_in_dim.25), calls=%async_computation.3 | async-start | bytes 950272 | tf_op jit(solution)/shard_map/all_to_all | solution.py:31
  155.8 12.3 %collective-permute-start.6 = (bf16[4,464,128]{2,1,0:T(8,128)(2,1)}, bf16[4,464,128]{2,1,0:T(8,128)(2,1)}, u32[]{:S(2)}, u32[]{:S(2)}) collective-permute-start(bf16[4,464,128]{2,1,0:T(8,128)(2,1)} %copy-done.6), channel_id=1, source_target_pairs={{0,64},{64,0},{1,65},{65,1},{2,66},{66,2},{3,67},{67,3},{4,68},{68... | collective-permute-start | bytes 1425416 | tf_op jit(solution)/shard_map/ppermute | solution.py:21
  168.1 0.2 broadcast_in_dim.24
  168.4 0.0 copy-start.5
  168.4 0.1 bitcast_dynamic-update-slice_fusion.2
  168.5 0.0 copy-done.2
  168.5 0.1 broadcast_in_dim.27
  168.7 0.7 copy-done.5
  169.4 0.0 copy-start.3
  169.4 0.1 broadcast.16
  169.5 0.1 broadcast.17
  169.6 0.2 copy-done
  169.8 0.0 collective-permute-done.5
  169.8 0.0 collective-permute-done.4
  169.8 0.6 copy-done.3
  170.3 1.3 pad_maximum_fusion.1
  171.6 0.0 all-to-all-done.3
  171.6 0.0 collective-permute-done.6
  171.7 4.4 %collective-permute-start.7 = (bf16[4,464,128]{2,1,0:T(8,128)(2,1)}, bf16[4,464,128]{2,1,0:T(8,128)(2,1)S(1)}, u32[]{:S(2)}, u32[]{:S(2)}) collective-permute-start(bf16[4,464,128]{2,1,0:T(8,128)(2,1)} %all-to-all-done.3), channel_id=1, source_target_pairs={{0,64},{64,0},{1,65},{65,1},{2,66},{66,2},{3,67},{67,3},{4,68},{68... | collective-permute-start | bytes 1425416 | tf_op jit(solution)/shard_map/ppermute | solution.py:21
  176.1 0.8 bitcast_dynamic-update-slice_fusion.1
  176.9 0.7 constant_dynamic-update-slice_fusion.1
  177.6 0.8 bitcast_dynamic-update-slice_fusion
  178.4 0.0 copy-done.4
  178.4 0.7 constant_dynamic-update-slice_fusion
  179.2 2.2 %convolution_bitcast_fusion.2 = f32[464,464]{1,0:T(8,128)S(1)} fusion(bf16[4,2,464,128]{3,2,1,0:T(8,128)(2,1)} %constant_dynamic-update-slice_fusion, bf16[4,1,464,128]{3,2,1,0:T(8,128)(2,1)} %bitcast.16, bf16[4,1,464,128]{3,2,1,0:T(8,128)(2,1)S(1)} %bitcast.72), kind=kOutput, calls=%fused_computation.2 | convolution fusion | flops 441401344 | bytes 2761728 | tf_op jit(solution)/shard_map/dot_general | solution.py:92
  181.4 5.7 %fusion.7 = f32[128,464]{0,1:T(8,128)} fusion(bf16[464,7424]{1,0:T(8,128)(2,1)} %param.5, bf16[7424,128]{1,0:T(8,128)(2,1)S(1)} %bitcast.65), kind=kOutput, calls=%fused_computation.33 | convolution fusion | flops 881852416 | bytes 9027584 | tf_op jit(solution)/shard_map/dot_general | solution.py:84
  187.1 0.0 collective-permute-done.7
  187.1 0.4 convolution_bitcast_fusion
  187.5 2.4 %fusion.1 = f32[464,464]{1,0:T(8,128)} fusion(f32[464,464]{1,0:T(8,128)S(1)} %convolution_bitcast_fusion, f32[464,464]{1,0:T(8,128)S(1)} %convolution_bitcast_fusion.2, bf16[4,464,128]{2,1,0:T(8,128)(2,1)} %all-to-all-done.3, bf16[4,464,128]{2,1,0:T(8,128)(2,1)S(1)} %get-tuple-element.42), kind=kOutput, calls=%fused_computation.4 | convolution fusion | flops 220893696 | bytes 3533824 | tf_op jit(solution)/shard_map/dot_general | solution.py:92
  (20 shorter events, 0.3 us)
Async XLA Ops:
  2.4 16.3 %all-to-all-start = ((bf16[4,464,128]{2,1,0:T(8,128)(2,1)}), bf16[4,464,128]{2,1,0:T(8,128)(2,1)S(1)}, u32[]{:S(2)}, u32[]{:S(2)}) async-start(bf16[4,464,128]{2,1,0:T(8,128)(2,1)} %broadcast_in_dim.20), calls=%async_computation | async-start | bytes 950272 | tf_op jit(solution)/shard_map/all_to_all | solution.py:31
  7.2 11.4 %collective-permute-start = (bf16[116,128]{1,0:T(8,128)(2,1)}, bf16[116,128]{1,0:T(8,128)(2,1)S(1)}, u32[]{:S(2)}, u32[]{:S(2)}) collective-permute-start(bf16[116,128]{1,0:T(8,128)(2,1)} %bitcast.75), channel_id=1, source_target_pairs={{0,0},{1,1},{2,2},{3,3},{4,64},{5,65},{6,66},{7,67},{8,128},{9,129... | collective-permute-start | bytes 89096 | tf_op jit(solution)/shard_map/ppermute | solution.py:21
  18.6 0.8 copy-start.6
  74.2 27.3 %all-to-all-start.2 = ((bf16[4,928,128]{2,1,0:T(8,128)(2,1)}), bf16[4,928,128]{2,1,0:T(8,128)(2,1)S(1)}, u32[]{:S(2)}, u32[]{:S(2)}) async-start(bf16[4,928,128]{2,1,0:T(8,128)(2,1)} %broadcast_in_dim.22), calls=%async_computation.2 | async-start | bytes 1900544 | tf_op jit(solution)/shard_map/all_to_all | solution.py:31
  102.3 9.9 %copy-start.8 = (bf16[128,464]{0,1:T(8,128)(2,1)S(1)}, bf16[128,464]{0,1:T(8,128)(2,1)}, u32[]{:S(2)}) copy-start(bf16[128,464]{0,1:T(8,128)(2,1)} %param.4) | copy-start | bytes 356356
  103.4 38.1 %collective-permute-start.1 = (bf16[2,2,928,128]{3,2,1,0:T(8,128)(2,1)}, bf16[2,2,928,128]{3,2,1,0:T(8,128)(2,1)S(1)}, u32[]{:S(2)}, u32[]{:S(2)}) collective-permute-start(bf16[2,2,928,128]{3,2,1,0:T(8,128)(2,1)} %copy.9), channel_id=1, source_target_pairs={{0,16},{16,32},{32,48},{48,0},{1,17},{17,33},{33,49},{49,1},{2,18}... | collective-permute-start | bytes 2850824 | tf_op jit(solution)/shard_map/ppermute | solution.py:21
  108.9 32.6 %collective-permute-start.2 = (bf16[2,2,928,128]{3,2,0,1:T(8,128)(2,1)S(1)}, bf16[2,2,928,128]{3,2,0,1:T(8,128)(2,1)S(1)}, u32[]{:S(2)}, u32[]{:S(2)}) collective-permute-start(bf16[2,2,928,128]{3,2,0,1:T(8,128)(2,1)S(1)} %pad_maximum_fusion), channel_id=1, source_target_pairs={{0,48},{16,0},{32,16},{48,32},{1,49},{17,1},{33,17},{49,33},{2,50}... | collective-permute-start | bytes 2850824 | tf_op jit(solution)/shard_map/ppermute | solution.py:21
  112.2 29.3 %collective-permute-start.3 = (bf16[464,128]{1,0:T(8,128)(2,1)S(1)}, bf16[464,128]{1,0:T(8,128)(2,1)S(1)}, u32[]{:S(2)}, u32[]{:S(2)}) collective-permute-start(bf16[464,128]{1,0:T(8,128)(2,1)S(1)} %bitcast.74), channel_id=1, source_target_pairs={{0,128},{128,0},{1,129},{129,1},{2,130},{130,2},{3,131},{131,3},{4... | collective-permute-start | bytes 356360 | tf_op jit(solution)/shard_map/ppermute | solution.py:21
  145.2 24.6 %collective-permute-start.5 = (bf16[2,928,128]{2,1,0:T(8,128)(2,1)}, bf16[2,928,128]{2,1,0:T(8,128)(2,1)}, u32[]{:S(2)}, u32[]{:S(2)}) collective-permute-start(bf16[2,928,128]{2,1,0:T(8,128)(2,1)} %slice_bitcast_fusion), channel_id=1, source_target_pairs={{0,48},{16,0},{32,16},{48,32},{1,49},{17,1},{33,17},{49,33},{2,50}... | collective-permute-start | bytes 1425416 | tf_op jit(solution)/shard_map/ppermute | solution.py:21
  148.6 21.2 %collective-permute-start.4 = (bf16[2,928,128]{2,1,0:T(8,128)(2,1)}, bf16[2,928,128]{2,1,0:T(8,128)(2,1)}, u32[]{:S(2)}, u32[]{:S(2)}) collective-permute-start(bf16[2,928,128]{2,1,0:T(8,128)(2,1)} %slice_bitcast_fusion.1), channel_id=1, source_target_pairs={{0,16},{16,32},{32,48},{48,0},{1,17},{17,33},{33,49},{49,1},{2,18}... | collective-permute-start | bytes 1425416 | tf_op jit(solution)/shard_map/ppermute | solution.py:21
  151.3 20.3 %all-to-all-start.3 = ((bf16[4,464,128]{2,1,0:T(8,128)(2,1)}), bf16[4,464,128]{2,1,0:T(8,128)(2,1)}, u32[]{:S(2)}, u32[]{:S(2)}) async-start(bf16[4,464,128]{2,1,0:T(8,128)(2,1)} %broadcast_in_dim.25), calls=%async_computation.3 | async-start | bytes 950272 | tf_op jit(solution)/shard_map/all_to_all | solution.py:31
  155.8 12.7 %copy-start.2 = (bf16[1,1,928,128]{3,2,0,1:T(8,128)(2,1)S(1)}, bf16[1,1,928,128]{3,2,0,1:T(8,128)(2,1)}, u32[]{:S(2)}) copy-start(bf16[1,1,928,128]{3,2,0,1:T(8,128)(2,1)} %slice.88) | copy-start | bytes 712708
  155.8 15.8 %collective-permute-start.6 = (bf16[4,464,128]{2,1,0:T(8,128)(2,1)}, bf16[4,464,128]{2,1,0:T(8,128)(2,1)}, u32[]{:S(2)}, u32[]{:S(2)}) collective-permute-start(bf16[4,464,128]{2,1,0:T(8,128)(2,1)} %copy-done.6), channel_id=1, source_target_pairs={{0,64},{64,0},{1,65},{65,1},{2,66},{66,2},{3,67},{67,3},{4,68},{68... | collective-permute-start | bytes 1425416 | tf_op jit(solution)/shard_map/ppermute | solution.py:21
  168.4 1.0 copy-start.5
  168.5 1.3 copy-start
  169.4 0.9 copy-start.3
  171.6 6.8 %copy-start.4 = (bf16[1,1,928,128]{3,2,1,0:T(8,128)(2,1)S(1)}, bf16[1,1,928,128]{3,2,1,0:T(8,128)(2,1)}, u32[]{:S(2)}) copy-start(bf16[1,1,928,128]{3,2,1,0:T(8,128)(2,1)} %slice.91) | copy-start | bytes 712708
  171.6 7.6 %copy-start.7 = (bf16[4,464,128]{2,1,0:T(8,128)(2,1)S(1)}, bf16[4,464,128]{2,1,0:T(8,128)(2,1)}, u32[]{:S(2)}) copy-start(bf16[4,464,128]{2,1,0:T(8,128)(2,1)} %copy-done.6) | copy-start | bytes 1425412
  171.7 15.4 %collective-permute-start.7 = (bf16[4,464,128]{2,1,0:T(8,128)(2,1)}, bf16[4,464,128]{2,1,0:T(8,128)(2,1)S(1)}, u32[]{:S(2)}, u32[]{:S(2)}) collective-permute-start(bf16[4,464,128]{2,1,0:T(8,128)(2,1)} %all-to-all-done.3), channel_id=1, source_target_pairs={{0,64},{64,0},{1,65},{65,1},{2,66},{66,2},{3,67},{67,3},{4,68},{68... | collective-permute-start | bytes 1425416 | tf_op jit(solution)/shard_map/ppermute | solution.py:21
  179.2 2.2 %copy-start.1 = (bf16[4,2,928,128]{3,2,1,0:T(8,128)(2,1)S(1)}, bf16[4,2,928,128]{3,2,1,0:T(8,128)(2,1)}, u32[]{:S(2)}) copy-start(bf16[4,2,928,128]{3,2,1,0:T(8,128)(2,1)} %bitcast_dynamic-update-slice_fusion) | copy-start | bytes 5701636

commit v6 on v5

--- a/solution.py
+++ b/solution.py
@@ -31,6 +31,17 @@
     return lax.all_to_all(copies, axis, 0, 0, tiled=True)
 
 
+def paired(value, bit):
+    def flip(za, zb):
+        z = (za * 4 + zb) ^ (8 >> bit)
+        return (z // 4, z % 4)
+
+    theirs = permute(value, ("za", "zb"), flip)
+    place = lax.axis_index("za") * 4 + lax.axis_index("zb")
+    low = (place >> (3 - bit)) % 2 == 0
+    return jnp.where(low, jnp.stack([value, theirs], bit), jnp.stack([theirs, value], bit))
+
+
 def ordered(axis, blocks):
     me = lax.axis_index(axis)
     ring = jnp.broadcast_to(blocks[0][None], (4,) + blocks[0].shape)
@@ -54,43 +65,37 @@
     scaled = (g.astype(jnp.float32) * scale[:, None]).astype(jnp.bfloat16)
 
     part = permute(g, AXES, lambda x, zh, c, y, za, zb: (y, za // 2, za % 2, x, 2 * zh + c, zb))
-    near = spread(a, "x")
-    part, near, scaled, a = sync((part, near, scaled, a))
+    far = permute(a, ("zh",), lambda h: (1 - h,))
+    part, scaled, a, far = sync((part, scaled, a, far))
 
-    both = spread(jnp.concatenate([scaled, part]), "za").reshape(8 * cols, tokens)
-    both, near, a = sync((both, near, a))
-
-    both = spread(both, "zb").reshape(4, 4, 2, cols, tokens).transpose(2, 1, 0, 3, 4)
-    rows = both[0].reshape(2, half, tokens)
-    part = both[1].reshape(2, 2, 4 * cols, tokens)
+    both = jnp.concatenate([scaled, part])
+    for bit in range(4):
+        both, a, far = sync((paired(both, bit), a, far))
+    both = both.reshape(16, 2, cols, tokens)
+    rows = both[:, 0].reshape(2, half, tokens)
+    part = both[:, 1].reshape(2, 2, 4 * cols, tokens)
     part = jnp.where(lax.axis_index("c") == 0, part, part[:, ::-1])
     part = jnp.where(lax.axis_index("zh") == 0, part, part[::-1])
     part = part.reshape(2, half, tokens)
     both = jnp.stack([rows, part], 1)
-    both, near, a = sync((both, near, a))
+    both, a, far = sync((both, a, far))
 
     behind, ahead = along_y(both, 1), along_y(both, -1)
-    far = permute(a, ("zh",), lambda h: (1 - h,))
-    both, behind, ahead, far, near = sync((both, behind, ahead, far, near))
+    acts = spread(jnp.stack([a, far]), "x")
+    both, behind, ahead, acts = sync((both, behind, ahead, acts))
 
     opposite = jnp.stack([along_y(behind[0], 1), along_y(ahead[1], -1)])
-    far = spread(far, "x")
-    near_c = permute(near, ("c",), lambda c: (1 - c,))
-    opposite, far, near, near_c = sync((opposite, far, near, near_c))
+    acts_c = permute(acts, ("c",), lambda c: (1 - c,))
 
-    far_c = permute(far, ("c",), lambda c: (1 - c,))
     around = [both, ahead, opposite, behind]
     rows = ordered("y", [v[:, 0] for v in around]).reshape(64 * cols, tokens)
     input_grads = lax.dot_general(weight_codes, rows, (((1,), (0,)), ((), ())), preferred_element_type=jnp.float32)
-    part = [[v[h, 1].reshape(2, 4 * cols, tokens) for v in around] for h in (0, 1)]
     weight_grads = 0.0
-    for mine, blocks in (
-        (jnp.stack([near, near_c], 1), part[0]),
-        (far[:, None], [v[:1] for v in part[1]]),
-        (far_c[:, None], [v[1:] for v in part[1]]),
-    ):
+    for half in (0, 1):
+        mine = jnp.stack([acts[:, half], acts_c[:, half]], 1)
+        blocks = ordered("y", [v[half, 1].reshape(2, 4 * cols, tokens) for v in around])
         weight_grads += lax.dot_general(
-            mine, ordered("y", blocks), (((0, 1, 3), (0, 1, 3)), ((), ())), preferred_element_type=jnp.float32
+            mine, blocks, (((0, 1, 3), (0, 1, 3)), ((), ())), preferred_element_type=jnp.float32
         )
     return input_grads.T, weight_grads
 

time: 191 us -> 174 us (0.911)
  starting transfers between devices: 55.2 us -> 114 us
  blocking collectives: 53.7 us -> 0 us
  waiting for transfers between devices: 51.2 us -> 40.2 us
  matrix products: 10.6 us -> 4.93 us
  local copies, waits for them, and re-layouts: 15.7 us -> 10.3 us
    ppermute x8 -> x11, starting transfers between devices: 42.3 us -> 109 us  [permute(): return lax.ppermute(value, axes, pairs)]
    all_to_all x1 -> x0, blocking collectives: 53.7 us -> none  [spread(): return lax.all_to_all(copies, axis, 0, 0, tiled=True)]
    all_to_all x3 -> x1, waiting for transfers between devices: 23.8 us -> 11 us  [spread(): return lax.all_to_all(copies, axis, 0, 0, tiled=True)]
    all_to_all x3 -> x1, starting transfers between devices: 12.8 us -> 4.33 us  [spread(): return lax.all_to_all(copies, axis, 0, 0, tiled=True)]
    dot_general x1, matrix products: 5.66 us -> 2.63 us  [per_device(): lax.dot_general(weight_codes, rows, (((1,), (0,)), ((), ())), preferred_e...]
    dot_general x3 -> x2, matrix products: 4.98 us -> 2.3 us  [per_device(): lax.dot_general(mine, blocks, (((0, 1, 3), (0, 1, 3)), ((), ())), preferr...]
    broadcast_in_dim x4 -> x1, local copies, waits for them, and re-layouts: 3.66 us -> 1.09 us  [spread(): copies = jnp.broadcast_to(value[None], (n,) + value.shape)]
    ppermute x8 -> x11, waiting for transfers between devices: 27.5 us -> 29.2 us  [permute(): return lax.ppermute(value, axes, pairs)]
  transfers between devices with their start and end apart: 11 -> 12, of which waited for: 3 -> 8; matrix products, arithmetic and copies ran while one was open for 8% -> 4% of each run, Pallas kernels for 0% -> 0%
where the time goes in v6:
time: 174 us; the launch traced here: 172 us
  starting transfers between devices  114 us (66%)
  waiting for transfers between devices  40.2 us (23%)
  local copies, waits for them, and re-layouts  10.3 us (6%)
  matrix products  4.93 us (3%)
    ppermute x11, starting transfers between devices, permute(): return lax.ppermute(value, axes, pairs)  109 us
    ppermute x11, waiting for transfers between devices, permute(): return lax.ppermute(value, axes, pairs)  29.2 us
    all_to_all x1, waiting for transfers between devices, spread(): return lax.all_to_all(copies, axis, 0, 0, tiled=True)  11 us
    all_to_all x1, starting transfers between devices, spread(): return lax.all_to_all(copies, axis, 0, 0, tiled=True)  4.33 us
  transfers between devices with their start and end apart: 12, of which 8 were waited for; matrix products, arithmetic and copies ran while one was open for 4% of the time, Pallas kernels for 0%

profile of v6, /device:TPU:1, one launch (start us, length us, event | category | flops | bytes accessed | tf_op | source)
XLA Modules:
  0.0 171.7 jit_solution(16843291428601272639)
XLA Ops:
  0.6 10.2 %collective-permute-start = (bf16[116,128]{1,0:T(8,128)(2,1)}, bf16[116,128]{1,0:T(8,128)(2,1)S(1)}, u32[]{:S(2)}, u32[]{:S(2)}) collective-permute-start(bf16[116,128]{1,0:T(8,128)(2,1)} %bitcast.84), channel_id=1, source_target_pairs={{0,0},{1,1},{2,2},{3,3},{4,64},{5,65},{6,66},{7,67},{8,128},{9,129... | collective-permute-start | bytes 89096 | tf_op jit(solution)/shard_map/ppermute | solution.py:21
  10.8 21.2 %collective-permute-start.1 = (bf16[464,128]{1,0:T(8,128)(2,1)}, bf16[464,128]{1,0:T(8,128)(2,1)S(1)}, u32[]{:S(2)}, u32[]{:S(2)}) collective-permute-start(bf16[464,128]{1,0:T(8,128)(2,1)} %bitcast.80), channel_id=1, source_target_pairs={{0,128},{128,0},{1,129},{129,1},{2,130},{130,2},{3,131},{131,3},{4... | collective-permute-start | bytes 356360 | tf_op jit(solution)/shard_map/ppermute | solution.py:21
  32.1 0.8 dynamic_slice.3
  32.9 0.8 multiply_convert_fusion
  33.7 0.0 collective-permute-done
  33.7 4.0 %collective-permute-done.1 = bf16[464,128]{1,0:T(8,128)(2,1)S(1)} collective-permute-done((bf16[464,128]{1,0:T(8,128)(2,1)}, bf16[464,128]{1,0:T(8,128)(2,1)S(1)}, u32[]{:S(2)}, u32[]{:S(2)}) %collective-permute-start.1) | collective-permute-done | bytes 118816 | tf_op jit(solution)/shard_map/ppermute | solution.py:21
  37.7 25.2 %collective-permute-start.2 = (bf16[232,128]{1,0:T(8,128)(2,1)S(1)}, bf16[232,128]{1,0:T(8,128)(2,1)S(1)}, u32[]{:S(2)}, u32[]{:S(2)}) collective-permute-start(bf16[232,128]{1,0:T(8,128)(2,1)S(1)} %pad_maximum_fusion.3), channel_id=1, source_target_pairs={{0,8},{1,9},{2,10},{3,11},{4,12},{5,13},{6,14},{7,15},{8,0},{9,1},... | collective-permute-start | bytes 178184 | tf_op jit(solution)/shard_map/ppermute | solution.py:21
  63.0 1.6 collective-permute-done.2
  64.6 15.7 %collective-permute-start.3 = (bf16[2,232,128]{2,1,0:T(8,128)(2,1)S(1)}, bf16[2,232,128]{2,1,0:T(8,128)(2,1)S(1)}, u32[]{:S(2)}, u32[]{:S(2)}) collective-permute-start(bf16[2,232,128]{2,1,0:T(8,128)(2,1)S(1)} %maximum_select_fusion.3), channel_id=1, source_target_pairs={{0,4},{1,5},{2,6},{3,7},{4,0},{5,1},{6,2},{7,3},{8,12},{9,13},{10,... | collective-permute-start | bytes 356360 | tf_op jit(solution)/shard_map/ppermute | solution.py:21
  80.3 3.9 %collective-permute-done.3 = bf16[2,232,128]{2,1,0:T(8,128)(2,1)S(1)} collective-permute-done((bf16[2,232,128]{2,1,0:T(8,128)(2,1)S(1)}, bf16[2,232,128]{2,1,0:T(8,128)(2,1)S(1)}, u32[]{:S(2)}, u32[]{:S(2)}) %collective-permute-start.3) | collective-permute-done | bytes 118816 | tf_op jit(solution)/shard_map/ppermute | solution.py:21
  84.2 1.9 %collective-permute-start.4 = (bf16[2,2,232,128]{3,2,0,1:T(8,128)(2,1)S(1)}, bf16[2,2,232,128]{3,2,0,1:T(8,128)(2,1)S(1)}, u32[]{:S(2)}, u32[]{:S(2)}) collective-permute-start(bf16[2,2,232,128]{3,2,0,1:T(8,128)(2,1)S(1)} %maximum_select_fusion.2), channel_id=1, source_target_pairs={{0,2},{1,3},{2,0},{3,1},{4,6},{5,7},{6,4},{7,5},{8,10},{9,11},{10,... | collective-permute-start | bytes 712712 | tf_op jit(solution)/shard_map/ppermute | solution.py:21
  86.2 7.3 %collective-permute-done.4 = bf16[2,2,232,128]{3,2,0,1:T(8,128)(2,1)S(1)} collective-permute-done((bf16[2,2,232,128]{3,2,0,1:T(8,128)(2,1)S(1)}, bf16[2,2,232,128]{3,2,0,1:T(8,128)(2,1)S(1)}, u32[]{:S(2)}, u32[]{:S(2)}) %collective-permute-start.4) | collective-permute-done | bytes 237600 | tf_op jit(solution)/shard_map/ppermute | solution.py:21
  93.4 0.1 maximum_select_fusion.1
  93.5 16.4 %collective-permute-start.5 = (bf16[2,2,2,232,128]{4,3,0,1,2:T(8,128)(2,1)S(1)}, bf16[2,2,2,232,128]{4,3,0,1,2:T(8,128)(2,1)S(1)}, u32[]{:S(2)}, u32[]{:S(2)}) collective-permute-start(bf16[2,2,2,232,128]{4,3,0,1,2:T(8,128)(2,1)S(1)} %maximum_select_fusion.1), channel_id=1, source_target_pairs={{0,1},{1,0},{2,3},{3,2},{4,5},{5,4},{6,7},{7,6},{8,9},{9,8},{10,11... | collective-permute-start | bytes 1425416 | tf_op jit(solution)/shard_map/ppermute | solution.py:21
  109.9 9.8 %collective-permute-done.5 = bf16[2,2,2,232,128]{4,3,0,1,2:T(8,128)(2,1)S(1)} collective-permute-done((bf16[2,2,2,232,128]{4,3,0,1,2:T(8,128)(2,1)S(1)}, bf16[2,2,2,232,128]{4,3,0,1,2:T(8,128)(2,1)S(1)}, u32[]{:S(2)}, u32[]{:S(2)}) %collective-permute-start.5) | collective-permute-done | bytes 475168 | tf_op jit(solution)/shard_map/ppermute | solution.py:21
  119.7 0.2 maximum_select_fusion
  119.9 1.0 copy.6
  120.9 0.2 fusion.16
  121.0 0.1 copy.7
  121.2 0.1 stack_reshape_squeeze.3
  121.3 0.1 copy.8
  121.4 0.1 reshape_squeeze.3
  121.5 0.1 reverse_select_fusion.1
  121.6 0.1 reverse_select_fusion
  121.7 0.0 copy-start
  121.7 0.1 pad_maximum_fusion
  121.8 1.0 copy.9
  122.8 3.1 %collective-permute-start.6 = (bf16[2,2,928,128]{3,2,1,0:T(8,128)(2,1)}, bf16[2,2,928,128]{3,2,1,0:T(8,128)(2,1)S(1)}, u32[]{:S(2)}, u32[]{:S(2)}) collective-permute-start(bf16[2,2,928,128]{3,2,1,0:T(8,128)(2,1)} %copy.9), channel_id=1, source_target_pairs={{0,16},{16,32},{32,48},{48,0},{1,17},{17,33},{33,49},{49,1},{2,18}... | collective-permute-start | bytes 2850824 | tf_op jit(solution)/shard_map/ppermute | solution.py:21
  125.9 3.8 %collective-permute-start.7 = (bf16[2,2,928,128]{3,2,0,1:T(8,128)(2,1)S(1)}, bf16[2,2,928,128]{3,2,0,1:T(8,128)(2,1)}, u32[]{:S(2)}, u32[]{:S(2)}) collective-permute-start(bf16[2,2,928,128]{3,2,0,1:T(8,128)(2,1)S(1)} %pad_maximum_fusion), channel_id=1, source_target_pairs={{0,48},{16,0},{32,16},{48,32},{1,49},{17,1},{33,17},{49,33},{2,50}... | collective-permute-start | bytes 2850824 | tf_op jit(solution)/shard_map/ppermute | solution.py:21
  129.7 0.0 copy-done
  129.7 1.1 broadcast_in_dim.28
  130.8 4.3 %all-to-all-start = ((bf16[4,2,464,128]{3,2,1,0:T(8,128)(2,1)}), bf16[4,2,464,128]{3,2,1,0:T(8,128)(2,1)S(1)}, u32[]{:S(2)}, u32[]{:S(2)}) async-start(bf16[4,2,464,128]{3,2,1,0:T(8,128)(2,1)} %broadcast_in_dim.28), calls=%async_computation | async-start | bytes 1900544 | tf_op jit(solution)/shard_map/all_to_all | solution.py:31
  135.1 11.0 %all-to-all-done = bf16[4,2,464,128]{3,2,1,0:T(8,128)(2,1)S(1)} async-done(((bf16[4,2,464,128]{3,2,1,0:T(8,128)(2,1)}), bf16[4,2,464,128]{3,2,1,0:T(8,128)(2,1)S(1)}, u32[]{:S(2)}, u32[]{:S(2)}) %all-to-all-start) | async-done | bytes 950304 | tf_op jit(solution)/shard_map/all_to_all | solution.py:31
  146.1 1.2 collective-permute-done.6
  147.3 1.4 collective-permute-done.7
  148.8 1.1 fusion.14
  149.9 1.1 slice_bitcast_fusion
  151.0 3.1 %collective-permute-start.8 = (bf16[2,928,128]{2,1,0:T(8,128)(2,1)S(1)}, bf16[2,928,128]{2,1,0:T(8,128)(2,1)S(1)}, u32[]{:S(2)}, u32[]{:S(2)}) collective-permute-start(bf16[2,928,128]{2,1,0:T(8,128)(2,1)S(1)} %slice_bitcast_fusion.1), channel_id=1, source_target_pairs={{0,16},{16,32},{32,48},{48,0},{1,17},{17,33},{33,49},{49,1},{2,18}... | collective-permute-start | bytes 1425416 | tf_op jit(solution)/shard_map/ppermute | solution.py:21
  154.1 3.5 %collective-permute-start.9 = (bf16[2,928,128]{2,1,0:T(8,128)(2,1)S(1)}, bf16[2,928,128]{2,1,0:T(8,128)(2,1)S(1)}, u32[]{:S(2)}, u32[]{:S(2)}) collective-permute-start(bf16[2,928,128]{2,1,0:T(8,128)(2,1)S(1)} %slice_bitcast_fusion), channel_id=1, source_target_pairs={{0,48},{16,0},{32,16},{48,32},{1,49},{17,1},{33,17},{49,33},{2,50}... | collective-permute-start | bytes 1425416 | tf_op jit(solution)/shard_map/ppermute | solution.py:21
  157.6 5.3 %collective-permute-start.10 = (bf16[4,2,464,128]{3,2,1,0:T(8,128)(2,1)S(1)}, bf16[4,2,464,128]{3,2,1,0:T(8,128)(2,1)S(1)}, u32[]{:S(2)}, u32[]{:S(2)}) collective-permute-start(bf16[4,2,464,128]{3,2,1,0:T(8,128)(2,1)S(1)} %all-to-all-done), channel_id=1, source_target_pairs={{0,64},{64,0},{1,65},{65,1},{2,66},{66,2},{3,67},{67,3},{4,68},{68... | collective-permute-start | bytes 2850824 | tf_op jit(solution)/shard_map/ppermute | solution.py:21
  162.9 0.0 slice-start
  162.9 0.2 broadcast_in_dim.30
  163.2 1.2 bitcast_dynamic-update-slice_fusion.1
  164.4 0.1 broadcast_in_dim.34
  164.6 0.1 broadcast_in_dim.32
  164.8 0.0 slice-start.1
  164.8 0.1 fusion.11
  164.9 0.0 collective-permute-done.8
  164.9 0.0 collective-permute-done.9
  165.2 0.1 fusion.8
  165.2 0.1 bitcast_dynamic-update-slice_fusion
  165.3 0.0 slice-done
  165.3 1.3 slice-done.1
  166.7 2.6 %fusion.17 = f32[128,464]{0,1:T(8,128)} fusion(bf16[464,7424]{1,0:T(8,128)(2,1)S(1)} %bitcast.86, bf16[7424,128]{1,0:T(8,128)(2,1)S(1)} %bitcast.61), kind=kOutput, calls=%fused_computation.41 | convolution fusion | flops 881852416 | bytes 9027584 | tf_op jit(solution)/shard_map/dot_general | solution.py:92
  169.3 0.0 collective-permute-done.10
  169.3 0.1 fusion.12
  169.4 0.7 convolution_bitcast_fusion
  170.0 1.6 fusion
  (17 shorter events, 0.5 us)
Async XLA Ops:
  0.6 33.1 %collective-permute-start = (bf16[116,128]{1,0:T(8,128)(2,1)}, bf16[116,128]{1,0:T(8,128)(2,1)S(1)}, u32[]{:S(2)}, u32[]{:S(2)}) collective-permute-start(bf16[116,128]{1,0:T(8,128)(2,1)} %bitcast.84), channel_id=1, source_target_pairs={{0,0},{1,1},{2,2},{3,3},{4,64},{5,65},{6,66},{7,67},{8,128},{9,129... | collective-permute-start | bytes 89096 | tf_op jit(solution)/shard_map/ppermute | solution.py:21
  10.8 26.9 %collective-permute-start.1 = (bf16[464,128]{1,0:T(8,128)(2,1)}, bf16[464,128]{1,0:T(8,128)(2,1)S(1)}, u32[]{:S(2)}, u32[]{:S(2)}) collective-permute-start(bf16[464,128]{1,0:T(8,128)(2,1)} %bitcast.80), channel_id=1, source_target_pairs={{0,128},{128,0},{1,129},{129,1},{2,130},{130,2},{3,131},{131,3},{4... | collective-permute-start | bytes 356360 | tf_op jit(solution)/shard_map/ppermute | solution.py:21
  37.7 26.8 %collective-permute-start.2 = (bf16[232,128]{1,0:T(8,128)(2,1)S(1)}, bf16[232,128]{1,0:T(8,128)(2,1)S(1)}, u32[]{:S(2)}, u32[]{:S(2)}) collective-permute-start(bf16[232,128]{1,0:T(8,128)(2,1)S(1)} %pad_maximum_fusion.3), channel_id=1, source_target_pairs={{0,8},{1,9},{2,10},{3,11},{4,12},{5,13},{6,14},{7,15},{8,0},{9,1},... | collective-permute-start | bytes 178184 | tf_op jit(solution)/shard_map/ppermute | solution.py:21
  64.6 19.6 %collective-permute-start.3 = (bf16[2,232,128]{2,1,0:T(8,128)(2,1)S(1)}, bf16[2,232,128]{2,1,0:T(8,128)(2,1)S(1)}, u32[]{:S(2)}, u32[]{:S(2)}) collective-permute-start(bf16[2,232,128]{2,1,0:T(8,128)(2,1)S(1)} %maximum_select_fusion.3), channel_id=1, source_target_pairs={{0,4},{1,5},{2,6},{3,7},{4,0},{5,1},{6,2},{7,3},{8,12},{9,13},{10,... | collective-permute-start | bytes 356360 | tf_op jit(solution)/shard_map/ppermute | solution.py:21
  84.2 9.2 %collective-permute-start.4 = (bf16[2,2,232,128]{3,2,0,1:T(8,128)(2,1)S(1)}, bf16[2,2,232,128]{3,2,0,1:T(8,128)(2,1)S(1)}, u32[]{:S(2)}, u32[]{:S(2)}) collective-permute-start(bf16[2,2,232,128]{3,2,0,1:T(8,128)(2,1)S(1)} %maximum_select_fusion.2), channel_id=1, source_target_pairs={{0,2},{1,3},{2,0},{3,1},{4,6},{5,7},{6,4},{7,5},{8,10},{9,11},{10,... | collective-permute-start | bytes 712712 | tf_op jit(solution)/shard_map/ppermute | solution.py:21
  93.5 26.2 %collective-permute-start.5 = (bf16[2,2,2,232,128]{4,3,0,1,2:T(8,128)(2,1)S(1)}, bf16[2,2,2,232,128]{4,3,0,1,2:T(8,128)(2,1)S(1)}, u32[]{:S(2)}, u32[]{:S(2)}) collective-permute-start(bf16[2,2,2,232,128]{4,3,0,1,2:T(8,128)(2,1)S(1)} %maximum_select_fusion.1), channel_id=1, source_target_pairs={{0,1},{1,0},{2,3},{3,2},{4,5},{5,4},{6,7},{7,6},{8,9},{9,8},{10,11... | collective-permute-start | bytes 1425416 | tf_op jit(solution)/shard_map/ppermute | solution.py:21
  121.7 8.0 %copy-start = (bf16[128,464]{0,1:T(8,128)(2,1)S(1)}, bf16[128,464]{0,1:T(8,128)(2,1)}, u32[]{:S(2)}) copy-start(bf16[128,464]{0,1:T(8,128)(2,1)} %param.4) | copy-start | bytes 356356
  122.8 24.5 %collective-permute-start.6 = (bf16[2,2,928,128]{3,2,1,0:T(8,128)(2,1)}, bf16[2,2,928,128]{3,2,1,0:T(8,128)(2,1)S(1)}, u32[]{:S(2)}, u32[]{:S(2)}) collective-permute-start(bf16[2,2,928,128]{3,2,1,0:T(8,128)(2,1)} %copy.9), channel_id=1, source_target_pairs={{0,16},{16,32},{32,48},{48,0},{1,17},{17,33},{33,49},{49,1},{2,18}... | collective-permute-start | bytes 2850824 | tf_op jit(solution)/shard_map/ppermute | solution.py:21
  125.9 22.9 %collective-permute-start.7 = (bf16[2,2,928,128]{3,2,0,1:T(8,128)(2,1)S(1)}, bf16[2,2,928,128]{3,2,0,1:T(8,128)(2,1)}, u32[]{:S(2)}, u32[]{:S(2)}) collective-permute-start(bf16[2,2,928,128]{3,2,0,1:T(8,128)(2,1)S(1)} %pad_maximum_fusion), channel_id=1, source_target_pairs={{0,48},{16,0},{32,16},{48,32},{1,49},{17,1},{33,17},{49,33},{2,50}... | collective-permute-start | bytes 2850824 | tf_op jit(solution)/shard_map/ppermute | solution.py:21
  130.8 15.3 %all-to-all-start = ((bf16[4,2,464,128]{3,2,1,0:T(8,128)(2,1)}), bf16[4,2,464,128]{3,2,1,0:T(8,128)(2,1)S(1)}, u32[]{:S(2)}, u32[]{:S(2)}) async-start(bf16[4,2,464,128]{3,2,1,0:T(8,128)(2,1)} %broadcast_in_dim.28), calls=%async_computation | async-start | bytes 1900544 | tf_op jit(solution)/shard_map/all_to_all | solution.py:31
  151.0 13.9 %collective-permute-start.8 = (bf16[2,928,128]{2,1,0:T(8,128)(2,1)S(1)}, bf16[2,928,128]{2,1,0:T(8,128)(2,1)S(1)}, u32[]{:S(2)}, u32[]{:S(2)}) collective-permute-start(bf16[2,928,128]{2,1,0:T(8,128)(2,1)S(1)} %slice_bitcast_fusion.1), channel_id=1, source_target_pairs={{0,16},{16,32},{32,48},{48,0},{1,17},{17,33},{33,49},{49,1},{2,18}... | collective-permute-start | bytes 1425416 | tf_op jit(solution)/shard_map/ppermute | solution.py:21
  154.1 10.8 %collective-permute-start.9 = (bf16[2,928,128]{2,1,0:T(8,128)(2,1)S(1)}, bf16[2,928,128]{2,1,0:T(8,128)(2,1)S(1)}, u32[]{:S(2)}, u32[]{:S(2)}) collective-permute-start(bf16[2,928,128]{2,1,0:T(8,128)(2,1)S(1)} %slice_bitcast_fusion), channel_id=1, source_target_pairs={{0,48},{16,0},{32,16},{48,32},{1,49},{17,1},{33,17},{49,33},{2,50}... | collective-permute-start | bytes 1425416 | tf_op jit(solution)/shard_map/ppermute | solution.py:21
  157.6 11.7 %collective-permute-start.10 = (bf16[4,2,464,128]{3,2,1,0:T(8,128)(2,1)S(1)}, bf16[4,2,464,128]{3,2,1,0:T(8,128)(2,1)S(1)}, u32[]{:S(2)}, u32[]{:S(2)}) collective-permute-start(bf16[4,2,464,128]{3,2,1,0:T(8,128)(2,1)S(1)} %all-to-all-done), channel_id=1, source_target_pairs={{0,64},{64,0},{1,65},{65,1},{2,66},{66,2},{3,67},{67,3},{4,68},{68... | collective-permute-start | bytes 2850824 | tf_op jit(solution)/shard_map/ppermute | solution.py:21
  162.9 2.4 %slice-start = ((s8[6889472]{0:T(1024)(128)(4,1)}), s8[4194304]{0:T(1024)(128)(4,1)S(1)}, s32[]{:S(2)}) async-start(s8[6889472]{0:T(1024)(128)(4,1)} %bitcast.85), calls=%async_computation.1 | async-start | bytes 8388608
  164.8 1.9 %slice-start.1 = ((s8[6889472]{0:T(1024)(128)(4,1)}), s8[2695168]{0:T(1024)(128)(4,1)S(1)}, s32[]{:S(2)}) async-start(s8[6889472]{0:T(1024)(128)(4,1)} %bitcast.85), calls=%async_computation.2 | async-start | bytes 5390336

commit v7 on v6

--- a/solution.py
+++ b/solution.py
@@ -31,7 +31,7 @@
     return lax.all_to_all(copies, axis, 0, 0, tiled=True)
 
 
-def paired(value, bit):
+def paired(value, bit, axis):
     def flip(za, zb):
         z = (za * 4 + zb) ^ (8 >> bit)
         return (z // 4, z % 4)
@@ -39,7 +39,7 @@
     theirs = permute(value, ("za", "zb"), flip)
     place = lax.axis_index("za") * 4 + lax.axis_index("zb")
     low = (place >> (3 - bit)) % 2 == 0
-    return jnp.where(low, jnp.stack([value, theirs], bit), jnp.stack([theirs, value], bit))
+    return jnp.where(low, jnp.stack([value, theirs], axis), jnp.stack([theirs, value], axis))
 
 
 def ordered(axis, blocks):
@@ -66,34 +66,41 @@
 
     part = permute(g, AXES, lambda x, zh, c, y, za, zb: (y, za // 2, za % 2, x, 2 * zh + c, zb))
     far = permute(a, ("zh",), lambda h: (1 - h,))
-    part, scaled, a, far = sync((part, scaled, a, far))
+    part, scaled = sync((part, scaled))
 
     both = jnp.concatenate([scaled, part])
-    for bit in range(4):
-        both, a, far = sync((paired(both, bit), a, far))
-    both = both.reshape(16, 2, cols, tokens)
-    rows = both[:, 0].reshape(2, half, tokens)
-    part = both[:, 1].reshape(2, 2, 4 * cols, tokens)
+    both, acts = sync((paired(both, 0, 0), jnp.stack([a, far])))
+    both = both.reshape(2, 2, cols, tokens).transpose(1, 0, 2, 3)
+    both = sync(paired(both, 1, 2))
+    both = sync(paired(both, 2, 3))
+
+    rows, part = sync((paired(both[0], 3, 3), both[1]))
+    rows = rows.reshape(16 * cols, tokens)
+
+    rows_b, rows_a = along_y(rows, 1), along_y(rows, -1)
+    part = paired(part, 3, 3).reshape(2, 2, 4 * cols, tokens)
     part = jnp.where(lax.axis_index("c") == 0, part, part[:, ::-1])
     part = jnp.where(lax.axis_index("zh") == 0, part, part[::-1])
-    part = part.reshape(2, half, tokens)
-    both = jnp.stack([rows, part], 1)
-    both, a, far = sync((both, a, far))
+    part = part.reshape(16 * cols, tokens)
+    rows_b, rows_a, part, acts = sync((rows_b, rows_a, part, acts))
 
-    behind, ahead = along_y(both, 1), along_y(both, -1)
-    acts = spread(jnp.stack([a, far]), "x")
-    both, behind, ahead, acts = sync((both, behind, ahead, acts))
+    up = along_y(jnp.concatenate([rows_b[:half], part]), 1)
+    down = along_y(jnp.concatenate([rows_a[half:], part]), -1)
+    acts = spread(acts, "x")
+    up, down, acts = sync((up, down, acts))
+    rows_o = jnp.concatenate([up[:half], down[:half]])
+    part_b, part_a = up[half:], down[half:]
 
-    opposite = jnp.stack([along_y(behind[0], 1), along_y(ahead[1], -1)])
+    part_o = along_y(part_b[:half], 1), along_y(part_a[half:], -1)
     acts_c = permute(acts, ("c",), lambda c: (1 - c,))
 
-    around = [both, ahead, opposite, behind]
-    rows = ordered("y", [v[:, 0] for v in around]).reshape(64 * cols, tokens)
+    rows = ordered("y", [rows, rows_a, rows_o, rows_b]).reshape(64 * cols, tokens)
     input_grads = lax.dot_general(weight_codes, rows, (((1,), (0,)), ((), ())), preferred_element_type=jnp.float32)
     weight_grads = 0.0
-    for half in (0, 1):
-        mine = jnp.stack([acts[:, half], acts_c[:, half]], 1)
-        blocks = ordered("y", [v[half, 1].reshape(2, 4 * cols, tokens) for v in around])
+    for i in (0, 1):
+        mine = jnp.stack([acts[:, i], acts_c[:, i]], 1)
+        own, ahead, behind = (v[i * half : (i + 1) * half] for v in (part, part_a, part_b))
+        blocks = ordered("y", [v.reshape(2, 4 * cols, tokens) for v in (own, ahead, part_o[i], behind)])
         weight_grads += lax.dot_general(
             mine, blocks, (((0, 1, 3), (0, 1, 3)), ((), ())), preferred_element_type=jnp.float32
         )

time: 174 us -> 173 us (level)
  starting transfers between devices: 114 us -> 78.7 us
  waiting for transfers between devices: 40.2 us -> 74.3 us
  local copies, waits for them, and re-layouts: 10.3 us -> 6.48 us
  matrix products: 4.93 us -> 7.94 us
  other arithmetic: 1.52 us -> 3.53 us
    ppermute x11 -> x14, waiting for transfers between devices: 29.2 us -> 71.9 us  [permute(): return lax.ppermute(value, axes, pairs)]
    ppermute x11 -> x14, starting transfers between devices: 109 us -> 74.6 us  [permute(): return lax.ppermute(value, axes, pairs)]
    all_to_all x1, waiting for transfers between devices: 11 us -> 2.38 us  [spread(): return lax.all_to_all(copies, axis, 0, 0, tiled=True)]
    dot_general x1, matrix products: 2.63 us -> 5.64 us  [per_device(): lax.dot_general(weight_codes, rows, (((1,), (0,)), ((), ())), preferred_e...]
    optimization_barrier x2 -> x1, local copies, waits for them, and re-layouts: 1.97 us -> 0.04 us  [per_device(): rows, part = sync((paired(both[0], 3, 3), both[1]))]
  transfers between devices with their start and end apart: 12 -> 15, of which waited for: 8 -> 9; matrix products, arithmetic and copies ran while one was open for 4% -> 6% of each run, Pallas kernels for 0% -> 0%
where the time goes in v7:
time: 173 us; the launch traced here: 172 us
  starting transfers between devices  78.7 us (45%)
  waiting for transfers between devices  74.3 us (43%)
  matrix products  7.94 us (5%)
  local copies, waits for them, and re-layouts  6.48 us (4%)
  other arithmetic  3.53 us (2%)
    ppermute x14, starting transfers between devices, permute(): return lax.ppermute(value, axes, pairs)  74.6 us
    ppermute x14, waiting for transfers between devices, permute(): return lax.ppermute(value, axes, pairs)  71.9 us
    dot_general x1, matrix products, per_device(): lax.dot_general(weight_codes, rows, (((1,), (0,)), ((), ())), preferred_e...  5.64 us
    all_to_all x1, starting transfers between devices, spread(): return lax.all_to_all(copies, axis, 0, 0, tiled=True)  4.05 us
  transfers between devices with their start and end apart: 15, of which 9 were waited for; matrix products, arithmetic and copies ran while one was open for 6% of the time, Pallas kernels for 0%

profile of v7, /device:TPU:1, one launch (start us, length us, event | category | flops | bytes accessed | tf_op | source)
XLA Modules:
  0.0 172.1 jit_solution(14342779598681821717)
XLA Ops:
  0.6 10.2 %collective-permute-start = (bf16[116,128]{1,0:T(8,128)(2,1)}, bf16[116,128]{1,0:T(8,128)(2,1)S(1)}, u32[]{:S(2)}, u32[]{:S(2)}) collective-permute-start(bf16[116,128]{1,0:T(8,128)(2,1)} %bitcast.82), channel_id=1, source_target_pairs={{0,0},{1,1},{2,2},{3,3},{4,64},{5,65},{6,66},{7,67},{8,128},{9,129... | collective-permute-start | bytes 89096 | tf_op jit(solution)/shard_map/ppermute | solution.py:21
  10.8 21.2 %collective-permute-start.2 = (bf16[464,128]{1,0:T(8,128)(2,1)}, bf16[464,128]{1,0:T(8,128)(2,1)S(1)}, u32[]{:S(2)}, u32[]{:S(2)}) collective-permute-start(bf16[464,128]{1,0:T(8,128)(2,1)} %bitcast.78), channel_id=1, source_target_pairs={{0,128},{128,0},{1,129},{129,1},{2,130},{130,2},{3,131},{131,3},{4... | collective-permute-start | bytes 356360 | tf_op jit(solution)/shard_map/ppermute | solution.py:21
  32.1 0.8 dynamic_slice.3
  32.9 0.8 multiply_convert_fusion
  33.7 0.0 collective-permute-done
  33.8 8.5 %collective-permute-start.1 = (bf16[232,128]{1,0:T(8,128)(2,1)S(1)}, bf16[232,128]{1,0:T(8,128)(2,1)S(1)}, u32[]{:S(2)}, u32[]{:S(2)}) collective-permute-start(bf16[232,128]{1,0:T(8,128)(2,1)S(1)} %pad_maximum_fusion.3), channel_id=1, source_target_pairs={{0,8},{1,9},{2,10},{3,11},{4,12},{5,13},{6,14},{7,15},{8,0},{9,1},... | collective-permute-start | bytes 178184 | tf_op jit(solution)/shard_map/ppermute | solution.py:21
  42.3 25.2 %collective-permute-done.1 = bf16[232,128]{1,0:T(8,128)(2,1)S(1)} collective-permute-done((bf16[232,128]{1,0:T(8,128)(2,1)S(1)}, bf16[232,128]{1,0:T(8,128)(2,1)S(1)}, u32[]{:S(2)}, u32[]{:S(2)}) %collective-permute-start.1) | collective-permute-done | bytes 59424 | tf_op jit(solution)/shard_map/ppermute | solution.py:21
  67.5 0.0 collective-permute-done.2
  67.5 0.9 pad_maximum_fusion.2
  68.5 1.9 %collective-permute-start.3 = (bf16[2,2,116,128]{3,2,0,1:T(8,128)(2,1)S(1)}, bf16[2,2,116,128]{3,2,0,1:T(8,128)(2,1)S(1)}, u32[]{:S(2)}, u32[]{:S(2)}) collective-permute-start(bf16[2,2,116,128]{3,2,0,1:T(8,128)(2,1)S(1)} %bitcast.70), channel_id=1, source_target_pairs={{0,4},{1,5},{2,6},{3,7},{4,0},{5,1},{6,2},{7,3},{8,12},{9,13},{10,... | collective-permute-start | bytes 356360 | tf_op jit(solution)/shard_map/ppermute | solution.py:21
  70.4 12.2 %collective-permute-done.3 = bf16[2,2,116,128]{3,2,0,1:T(8,128)(2,1)S(1)} collective-permute-done((bf16[2,2,116,128]{3,2,0,1:T(8,128)(2,1)S(1)}, bf16[2,2,116,128]{3,2,0,1:T(8,128)(2,1)S(1)}, u32[]{:S(2)}, u32[]{:S(2)}) %collective-permute-start.3) | collective-permute-done | bytes 118816 | tf_op jit(solution)/shard_map/ppermute | solution.py:21
  82.6 1.9 %collective-permute-start.4 = (bf16[2,2,2,116,128]{4,3,0,1,2:T(8,128)(2,1)S(1)}, bf16[2,2,2,116,128]{4,3,0,1,2:T(8,128)(2,1)S(1)}, u32[]{:S(2)}, u32[]{:S(2)}) collective-permute-start(bf16[2,2,2,116,128]{4,3,0,1,2:T(8,128)(2,1)S(1)} %maximum_select_fusion.3), channel_id=1, source_target_pairs={{0,2},{1,3},{2,0},{3,1},{4,6},{5,7},{6,4},{7,5},{8,10},{9,11},{10,... | collective-permute-start | bytes 712712 | tf_op jit(solution)/shard_map/ppermute | solution.py:21
  84.6 11.4 %collective-permute-done.4 = bf16[2,2,2,116,128]{4,3,0,1,2:T(8,128)(2,1)S(1)} collective-permute-done((bf16[2,2,2,116,128]{4,3,0,1,2:T(8,128)(2,1)S(1)}, bf16[2,2,2,116,128]{4,3,0,1,2:T(8,128)(2,1)S(1)}, u32[]{:S(2)}, u32[]{:S(2)}) %collective-permute-start.4) | collective-permute-done | bytes 237600 | tf_op jit(solution)/shard_map/ppermute | solution.py:21
  96.0 0.1 maximum_select_fusion
  96.1 0.1 slice_bitcast_fusion
  96.2 1.9 %collective-permute-start.5 = (bf16[2,2,2,116,128]{4,3,0,1,2:T(8,128)(2,1)S(1)}, bf16[2,2,2,116,128]{4,3,0,1,2:T(8,128)(2,1)S(1)}, u32[]{:S(2)}, u32[]{:S(2)}) collective-permute-start(bf16[2,2,2,116,128]{4,3,0,1,2:T(8,128)(2,1)S(1)} %get-tuple-element.40), channel_id=1, source_target_pairs={{0,1},{1,0},{2,3},{3,2},{4,5},{5,4},{6,7},{7,6},{8,9},{9,8},{10,11... | collective-permute-start | bytes 712712 | tf_op jit(solution)/shard_map/ppermute | solution.py:21
  98.1 7.0 %collective-permute-done.5 = bf16[2,2,2,116,128]{4,3,0,1,2:T(8,128)(2,1)S(1)} collective-permute-done((bf16[2,2,2,116,128]{4,3,0,1,2:T(8,128)(2,1)S(1)}, bf16[2,2,2,116,128]{4,3,0,1,2:T(8,128)(2,1)S(1)}, u32[]{:S(2)}, u32[]{:S(2)}) %collective-permute-start.5) | collective-permute-done | bytes 237600 | tf_op jit(solution)/shard_map/ppermute | solution.py:21
  105.1 0.1 maximum_select_fusion.1
  105.2 2.2 %collective-permute-start.8 = (bf16[2,2,2,116,128]{4,3,0,1,2:T(8,128)(2,1)S(1)}, bf16[2,2,2,116,128]{4,3,0,1,2:T(8,128)(2,1)S(1)}, u32[]{:S(2)}, u32[]{:S(2)}) collective-permute-start(bf16[2,2,2,116,128]{4,3,0,1,2:T(8,128)(2,1)S(1)} %get-tuple-element.19), channel_id=1, source_target_pairs={{0,1},{1,0},{2,3},{3,2},{4,5},{5,4},{6,7},{7,6},{8,9},{9,8},{10,11... | collective-permute-start | bytes 712712 | tf_op jit(solution)/shard_map/ppermute | solution.py:21
  107.5 0.1 broadcast_in_dim.37
  107.6 3.9 %collective-permute-start.6 = (bf16[1856,128]{1,0:T(8,128)(2,1)S(1)}, bf16[1856,128]{1,0:T(8,128)(2,1)S(1)}, u32[]{:S(2)}, u32[]{:S(2)}) collective-permute-start(bf16[1856,128]{1,0:T(8,128)(2,1)S(1)} %broadcast_in_dim.37), channel_id=1, source_target_pairs={{0,16},{16,32},{32,48},{48,0},{1,17},{17,33},{33,49},{49,1},{2,18}... | collective-permute-start | bytes 1425416 | tf_op jit(solution)/shard_map/ppermute | solution.py:21
  111.6 4.1 %collective-permute-start.7 = (bf16[1856,128]{1,0:T(8,128)(2,1)S(1)}, bf16[1856,128]{1,0:T(8,128)(2,1)S(1)}, u32[]{:S(2)}, u32[]{:S(2)}) collective-permute-start(bf16[1856,128]{1,0:T(8,128)(2,1)S(1)} %broadcast_in_dim.37), channel_id=1, source_target_pairs={{0,48},{16,0},{32,16},{48,32},{1,49},{17,1},{33,17},{49,33},{2,50}... | collective-permute-start | bytes 1425416 | tf_op jit(solution)/shard_map/ppermute | solution.py:21
  115.6 0.0 collective-permute-done.8
  115.6 0.1 maximum_select_fusion.2
  115.8 0.1 select_n.131
  115.9 0.1 reverse_select_fusion.1
  116.0 0.1 reverse_select_fusion
  116.1 7.5 %collective-permute-done.6 = bf16[1856,128]{1,0:T(8,128)(2,1)S(1)} collective-permute-done((bf16[1856,128]{1,0:T(8,128)(2,1)S(1)}, bf16[1856,128]{1,0:T(8,128)(2,1)S(1)}, u32[]{:S(2)}, u32[]{:S(2)}) %collective-permute-start.6) | collective-permute-done | bytes 475168 | tf_op jit(solution)/shard_map/ppermute | solution.py:21
  123.6 1.5 collective-permute-done.7
  125.2 1.2 pad_maximum_fusion
  126.4 3.1 %collective-permute-start.9 = (bf16[2784,128]{1,0:T(8,128)(2,1)}, bf16[2784,128]{1,0:T(8,128)(2,1)}, u32[]{:S(2)}, u32[]{:S(2)}) collective-permute-start(bf16[2784,128]{1,0:T(8,128)(2,1)} %get-tuple-element.44), channel_id=1, source_target_pairs={{0,16},{16,32},{32,48},{48,0},{1,17},{17,33},{33,49},{49,1},{2,18}... | collective-permute-start | bytes 2138120 | tf_op jit(solution)/shard_map/ppermute | solution.py:21
  129.4 3.5 %collective-permute-start.10 = (bf16[2784,128]{1,0:T(8,128)(2,1)}, bf16[2784,128]{1,0:T(8,128)(2,1)}, u32[]{:S(2)}, u32[]{:S(2)}) collective-permute-start(bf16[2784,128]{1,0:T(8,128)(2,1)} %get-tuple-element.43), channel_id=1, source_target_pairs={{0,48},{16,0},{32,16},{48,32},{1,49},{17,1},{33,17},{49,33},{2,50}... | collective-permute-start | bytes 2138120 | tf_op jit(solution)/shard_map/ppermute | solution.py:21
  133.0 1.1 broadcast_in_dim.40
  134.0 0.0 copy-done.2
  134.0 4.1 %all-to-all-start = ((bf16[4,2,464,128]{3,2,1,0:T(8,128)(2,1)}), bf16[4,2,464,128]{3,2,1,0:T(8,128)(2,1)S(1)}, u32[]{:S(2)}, u32[]{:S(2)}) async-start(bf16[4,2,464,128]{3,2,1,0:T(8,128)(2,1)} %broadcast_in_dim.40), calls=%async_computation | async-start | bytes 1900544 | tf_op jit(solution)/shard_map/all_to_all | solution.py:31
  138.1 0.8 fusion.14
  138.9 0.2 broadcast_in_dim.38
  139.2 0.1 bitcast_dynamic-update-slice_fusion.1
  139.2 0.0 copy-start
  139.2 0.0 copy-start.3
  139.2 6.0 %collective-permute-done.9 = bf16[2784,128]{1,0:T(8,128)(2,1)} collective-permute-done((bf16[2784,128]{1,0:T(8,128)(2,1)}, bf16[2784,128]{1,0:T(8,128)(2,1)}, u32[]{:S(2)}, u32[]{:S(2)}) %collective-permute-start.9) | collective-permute-done | bytes 712736 | tf_op jit(solution)/shard_map/ppermute | solution.py:21
  145.2 0.0 copy-done
  145.2 1.1 collective-permute-done.10
  146.3 2.4 %all-to-all-done = bf16[4,2,464,128]{3,2,1,0:T(8,128)(2,1)S(1)} async-done(((bf16[4,2,464,128]{3,2,1,0:T(8,128)(2,1)}), bf16[4,2,464,128]{3,2,1,0:T(8,128)(2,1)S(1)}, u32[]{:S(2)}, u32[]{:S(2)}) %all-to-all-start) | async-done | bytes 950304 | tf_op jit(solution)/shard_map/all_to_all | solution.py:31
  148.7 1.2 fusion.13
  149.9 1.2 fusion.12
  151.2 3.3 %collective-permute-start.13 = (bf16[928,128]{1,0:T(8,128)(2,1)S(1)}, bf16[928,128]{1,0:T(8,128)(2,1)S(1)}, u32[]{:S(2)}, u32[]{:S(2)}) collective-permute-start(bf16[928,128]{1,0:T(8,128)(2,1)S(1)} %get-tuple-element.36), channel_id=1, source_target_pairs={{0,48},{16,0},{32,16},{48,32},{1,49},{17,1},{33,17},{49,33},{2,50}... | collective-permute-start | bytes 712712 | tf_op jit(solution)/shard_map/ppermute | solution.py:21
  154.5 2.0 %collective-permute-start.12 = (bf16[928,128]{1,0:T(8,128)(2,1)S(1)}, bf16[928,128]{1,0:T(8,128)(2,1)S(1)}, u32[]{:S(2)}, u32[]{:S(2)}) collective-permute-start(bf16[928,128]{1,0:T(8,128)(2,1)S(1)} %get-tuple-element.32), channel_id=1, source_target_pairs={{0,16},{16,32},{32,48},{48,0},{1,17},{17,33},{33,49},{49,1},{2,18}... | collective-permute-start | bytes 712712 | tf_op jit(solution)/shard_map/ppermute | solution.py:21
  156.5 6.8 %collective-permute-start.11 = (bf16[4,2,464,128]{3,2,1,0:T(8,128)(2,1)S(1)}, bf16[4,2,464,128]{3,2,1,0:T(8,128)(2,1)S(1)}, u32[]{:S(2)}, u32[]{:S(2)}) collective-permute-start(bf16[4,2,464,128]{3,2,1,0:T(8,128)(2,1)S(1)} %all-to-all-done), channel_id=1, source_target_pairs={{0,64},{64,0},{1,65},{65,1},{2,66},{66,2},{3,67},{67,3},{4,68},{68... | collective-permute-start | bytes 2850824 | tf_op jit(solution)/shard_map/ppermute | solution.py:21
  163.3 0.0 copy-done.1
  163.3 0.1 fusion.7
  163.4 0.0 copy-done.3
  163.4 0.1 bitcast_dynamic-update-slice_fusion
  163.5 5.6 %fusion.15 = f32[128,464]{0,1:T(8,128)} fusion(bf16[464,7424]{1,0:T(8,128)(2,1)} %param.5, bf16[7424,128]{1,0:T(8,128)(2,1)S(1)} %bitcast.61), kind=kOutput, calls=%fused_computation.41 | convolution fusion | flops 881852416 | bytes 9027584 | tf_op jit(solution)/shard_map/dot_general | solution.py:98
  169.1 0.1 broadcast_in_dim.46
  169.3 0.1 broadcast_in_dim.44
  169.5 0.1 fusion.10
  169.6 0.0 collective-permute-done.13
  169.6 0.0 collective-permute-done.12
  169.6 0.1 constant_dynamic-update-slice_fusion.1
  169.7 0.0 collective-permute-done.11
  169.8 0.1 fusion.11
  169.8 0.7 convolution_bitcast_fusion
  170.5 1.6 fusion
  (19 shorter events, 0.4 us)
Async XLA Ops:
  0.6 33.1 %collective-permute-start = (bf16[116,128]{1,0:T(8,128)(2,1)}, bf16[116,128]{1,0:T(8,128)(2,1)S(1)}, u32[]{:S(2)}, u32[]{:S(2)}) collective-permute-start(bf16[116,128]{1,0:T(8,128)(2,1)} %bitcast.82), channel_id=1, source_target_pairs={{0,0},{1,1},{2,2},{3,3},{4,64},{5,65},{6,66},{7,67},{8,128},{9,129... | collective-permute-start | bytes 89096 | tf_op jit(solution)/shard_map/ppermute | solution.py:21
  10.8 56.7 %collective-permute-start.2 = (bf16[464,128]{1,0:T(8,128)(2,1)}, bf16[464,128]{1,0:T(8,128)(2,1)S(1)}, u32[]{:S(2)}, u32[]{:S(2)}) collective-permute-start(bf16[464,128]{1,0:T(8,128)(2,1)} %bitcast.78), channel_id=1, source_target_pairs={{0,128},{128,0},{1,129},{129,1},{2,130},{130,2},{3,131},{131,3},{4... | collective-permute-start | bytes 356360 | tf_op jit(solution)/shard_map/ppermute | solution.py:21
  33.8 33.7 %collective-permute-start.1 = (bf16[232,128]{1,0:T(8,128)(2,1)S(1)}, bf16[232,128]{1,0:T(8,128)(2,1)S(1)}, u32[]{:S(2)}, u32[]{:S(2)}) collective-permute-start(bf16[232,128]{1,0:T(8,128)(2,1)S(1)} %pad_maximum_fusion.3), channel_id=1, source_target_pairs={{0,8},{1,9},{2,10},{3,11},{4,12},{5,13},{6,14},{7,15},{8,0},{9,1},... | collective-permute-start | bytes 178184 | tf_op jit(solution)/shard_map/ppermute | solution.py:21
  68.5 14.1 %collective-permute-start.3 = (bf16[2,2,116,128]{3,2,0,1:T(8,128)(2,1)S(1)}, bf16[2,2,116,128]{3,2,0,1:T(8,128)(2,1)S(1)}, u32[]{:S(2)}, u32[]{:S(2)}) collective-permute-start(bf16[2,2,116,128]{3,2,0,1:T(8,128)(2,1)S(1)} %bitcast.70), channel_id=1, source_target_pairs={{0,4},{1,5},{2,6},{3,7},{4,0},{5,1},{6,2},{7,3},{8,12},{9,13},{10,... | collective-permute-start | bytes 356360 | tf_op jit(solution)/shard_map/ppermute | solution.py:21
  82.6 13.4 %collective-permute-start.4 = (bf16[2,2,2,116,128]{4,3,0,1,2:T(8,128)(2,1)S(1)}, bf16[2,2,2,116,128]{4,3,0,1,2:T(8,128)(2,1)S(1)}, u32[]{:S(2)}, u32[]{:S(2)}) collective-permute-start(bf16[2,2,2,116,128]{4,3,0,1,2:T(8,128)(2,1)S(1)} %maximum_select_fusion.3), channel_id=1, source_target_pairs={{0,2},{1,3},{2,0},{3,1},{4,6},{5,7},{6,4},{7,5},{8,10},{9,11},{10,... | collective-permute-start | bytes 712712 | tf_op jit(solution)/shard_map/ppermute | solution.py:21
  96.2 8.9 %collective-permute-start.5 = (bf16[2,2,2,116,128]{4,3,0,1,2:T(8,128)(2,1)S(1)}, bf16[2,2,2,116,128]{4,3,0,1,2:T(8,128)(2,1)S(1)}, u32[]{:S(2)}, u32[]{:S(2)}) collective-permute-start(bf16[2,2,2,116,128]{4,3,0,1,2:T(8,128)(2,1)S(1)} %get-tuple-element.40), channel_id=1, source_target_pairs={{0,1},{1,0},{2,3},{3,2},{4,5},{5,4},{6,7},{7,6},{8,9},{9,8},{10,11... | collective-permute-start | bytes 712712 | tf_op jit(solution)/shard_map/ppermute | solution.py:21
  105.2 10.5 %collective-permute-start.8 = (bf16[2,2,2,116,128]{4,3,0,1,2:T(8,128)(2,1)S(1)}, bf16[2,2,2,116,128]{4,3,0,1,2:T(8,128)(2,1)S(1)}, u32[]{:S(2)}, u32[]{:S(2)}) collective-permute-start(bf16[2,2,2,116,128]{4,3,0,1,2:T(8,128)(2,1)S(1)} %get-tuple-element.19), channel_id=1, source_target_pairs={{0,1},{1,0},{2,3},{3,2},{4,5},{5,4},{6,7},{7,6},{8,9},{9,8},{10,11... | collective-permute-start | bytes 712712 | tf_op jit(solution)/shard_map/ppermute | solution.py:21
  107.6 16.0 %collective-permute-start.6 = (bf16[1856,128]{1,0:T(8,128)(2,1)S(1)}, bf16[1856,128]{1,0:T(8,128)(2,1)S(1)}, u32[]{:S(2)}, u32[]{:S(2)}) collective-permute-start(bf16[1856,128]{1,0:T(8,128)(2,1)S(1)} %broadcast_in_dim.37), channel_id=1, source_target_pairs={{0,16},{16,32},{32,48},{48,0},{1,17},{17,33},{33,49},{49,1},{2,18}... | collective-permute-start | bytes 1425416 | tf_op jit(solution)/shard_map/ppermute | solution.py:21
  111.6 13.6 %collective-permute-start.7 = (bf16[1856,128]{1,0:T(8,128)(2,1)S(1)}, bf16[1856,128]{1,0:T(8,128)(2,1)S(1)}, u32[]{:S(2)}, u32[]{:S(2)}) collective-permute-start(bf16[1856,128]{1,0:T(8,128)(2,1)S(1)} %broadcast_in_dim.37), channel_id=1, source_target_pairs={{0,48},{16,0},{32,16},{48,32},{1,49},{17,1},{33,17},{49,33},{2,50}... | collective-permute-start | bytes 1425416 | tf_op jit(solution)/shard_map/ppermute | solution.py:21
  123.6 10.5 %copy-start.2 = (bf16[1856,128]{1,0:T(8,128)(2,1)}, bf16[1856,128]{1,0:T(8,128)(2,1)S(1)}, u32[]{:S(2)}) copy-start(bf16[1856,128]{1,0:T(8,128)(2,1)S(1)} %collective-permute-done.6) | copy-start | bytes 1425412
  126.4 18.9 %collective-permute-start.9 = (bf16[2784,128]{1,0:T(8,128)(2,1)}, bf16[2784,128]{1,0:T(8,128)(2,1)}, u32[]{:S(2)}, u32[]{:S(2)}) collective-permute-start(bf16[2784,128]{1,0:T(8,128)(2,1)} %get-tuple-element.44), channel_id=1, source_target_pairs={{0,16},{16,32},{32,48},{48,0},{1,17},{17,33},{33,49},{49,1},{2,18}... | collective-permute-start | bytes 2138120 | tf_op jit(solution)/shard_map/ppermute | solution.py:21
  129.4 16.9 %collective-permute-start.10 = (bf16[2784,128]{1,0:T(8,128)(2,1)}, bf16[2784,128]{1,0:T(8,128)(2,1)}, u32[]{:S(2)}, u32[]{:S(2)}) collective-permute-start(bf16[2784,128]{1,0:T(8,128)(2,1)} %get-tuple-element.43), channel_id=1, source_target_pairs={{0,48},{16,0},{32,16},{48,32},{1,49},{17,1},{33,17},{49,33},{2,50}... | collective-permute-start | bytes 2138120 | tf_op jit(solution)/shard_map/ppermute | solution.py:21
  134.0 14.7 %all-to-all-start = ((bf16[4,2,464,128]{3,2,1,0:T(8,128)(2,1)}), bf16[4,2,464,128]{3,2,1,0:T(8,128)(2,1)S(1)}, u32[]{:S(2)}, u32[]{:S(2)}) async-start(bf16[4,2,464,128]{3,2,1,0:T(8,128)(2,1)} %broadcast_in_dim.40), calls=%async_computation | async-start | bytes 1900544 | tf_op jit(solution)/shard_map/all_to_all | solution.py:31
  139.2 6.0 %copy-start = (bf16[4,1856,128]{2,1,0:T(8,128)(2,1)}, bf16[4,1856,128]{2,1,0:T(8,128)(2,1)S(1)}, u32[]{:S(2)}) copy-start(bf16[4,1856,128]{2,1,0:T(8,128)(2,1)S(1)} %bitcast_dynamic-update-slice_fusion.1) | copy-start | bytes 5701636
  139.2 24.1 %copy-start.3 = (bf16[1856,128]{1,0:T(8,128)(2,1)S(1)}, bf16[1856,128]{1,0:T(8,128)(2,1)}, u32[]{:S(2)}) copy-start(bf16[1856,128]{1,0:T(8,128)(2,1)} %copy-done.2) | copy-start | bytes 1425412
  146.3 17.0 %copy-start.1 = (bf16[4,1856,128]{2,1,0:T(8,128)(2,1)S(1)}, bf16[4,1856,128]{2,1,0:T(8,128)(2,1)}, u32[]{:S(2)}) copy-start(bf16[4,1856,128]{2,1,0:T(8,128)(2,1)} %copy-done) | copy-start | bytes 5701636
  151.2 18.4 %collective-permute-start.13 = (bf16[928,128]{1,0:T(8,128)(2,1)S(1)}, bf16[928,128]{1,0:T(8,128)(2,1)S(1)}, u32[]{:S(2)}, u32[]{:S(2)}) collective-permute-start(bf16[928,128]{1,0:T(8,128)(2,1)S(1)} %get-tuple-element.36), channel_id=1, source_target_pairs={{0,48},{16,0},{32,16},{48,32},{1,49},{17,1},{33,17},{49,33},{2,50}... | collective-permute-start | bytes 712712 | tf_op jit(solution)/shard_map/ppermute | solution.py:21
  154.5 15.1 %collective-permute-start.12 = (bf16[928,128]{1,0:T(8,128)(2,1)S(1)}, bf16[928,128]{1,0:T(8,128)(2,1)S(1)}, u32[]{:S(2)}, u32[]{:S(2)}) collective-permute-start(bf16[928,128]{1,0:T(8,128)(2,1)S(1)} %get-tuple-element.32), channel_id=1, source_target_pairs={{0,16},{16,32},{32,48},{48,0},{1,17},{17,33},{33,49},{49,1},{2,18}... | collective-permute-start | bytes 712712 | tf_op jit(solution)/shard_map/ppermute | solution.py:21
  156.5 13.3 %collective-permute-start.11 = (bf16[4,2,464,128]{3,2,1,0:T(8,128)(2,1)S(1)}, bf16[4,2,464,128]{3,2,1,0:T(8,128)(2,1)S(1)}, u32[]{:S(2)}, u32[]{:S(2)}) collective-permute-start(bf16[4,2,464,128]{3,2,1,0:T(8,128)(2,1)S(1)} %all-to-all-done), channel_id=1, source_target_pairs={{0,64},{64,0},{1,65},{65,1},{2,66},{66,2},{3,67},{67,3},{4,68},{68... | collective-permute-start | bytes 2850824 | tf_op jit(solution)/shard_map/ppermute | solution.py:21
  163.5 5.7 %copy-start.5 = (bf16[928,128]{1,0:T(8,128)(2,1)S(1)}, bf16[928,128]{1,0:T(8,128)(2,1)}, u32[]{:S(2)}) copy-start(bf16[928,128]{1,0:T(8,128)(2,1)} %get-tuple-element.42) | copy-start | bytes 712708
  163.5 5.8 %copy-start.4 = (bf16[928,128]{1,0:T(8,128)(2,1)S(1)}, bf16[928,128]{1,0:T(8,128)(2,1)}, u32[]{:S(2)}) copy-start(bf16[928,128]{1,0:T(8,128)(2,1)} %get-tuple-element.41) | copy-start | bytes 712708

commit v8 on v7

--- a/solution.py
+++ b/solution.py
@@ -65,16 +65,17 @@
     scaled = (g.astype(jnp.float32) * scale[:, None]).astype(jnp.bfloat16)
 
     part = permute(g, AXES, lambda x, zh, c, y, za, zb: (y, za // 2, za % 2, x, 2 * zh + c, zb))
-    far = permute(a, ("zh",), lambda h: (1 - h,))
-    part, scaled = sync((part, scaled))
+    near = spread(a, "x")
+    part, scaled, near, a = sync((part, scaled, near, a))
 
     both = jnp.concatenate([scaled, part])
-    both, acts = sync((paired(both, 0, 0), jnp.stack([a, far])))
+    both = sync(paired(both, 0, 0))
     both = both.reshape(2, 2, cols, tokens).transpose(1, 0, 2, 3)
     both = sync(paired(both, 1, 2))
-    both = sync(paired(both, 2, 3))
+    both, a, near = sync((paired(both, 2, 3), a, near))
 
-    rows, part = sync((paired(both[0], 3, 3), both[1]))
+    rows, part, a = sync((paired(both[0], 3, 3), both[1], a))
+    far = permute(a, ("zh",), lambda h: (1 - h,))
     rows = rows.reshape(16 * cols, tokens)
 
     rows_b, rows_a = along_y(rows, 1), along_y(rows, -1)
@@ -82,23 +83,23 @@
     part = jnp.where(lax.axis_index("c") == 0, part, part[:, ::-1])
     part = jnp.where(lax.axis_index("zh") == 0, part, part[::-1])
     part = part.reshape(16 * cols, tokens)
-    rows_b, rows_a, part, acts = sync((rows_b, rows_a, part, acts))
+    rows_b, rows_a, part = sync((rows_b, rows_a, part))
 
     up = along_y(jnp.concatenate([rows_b[:half], part]), 1)
     down = along_y(jnp.concatenate([rows_a[half:], part]), -1)
-    acts = spread(acts, "x")
-    up, down, acts = sync((up, down, acts))
+    near_c = permute(near, ("c",), lambda c: (1 - c,))
+    up, down, far, near_c = sync((up, down, far, near_c))
     rows_o = jnp.concatenate([up[:half], down[:half]])
     part_b, part_a = up[half:], down[half:]
 
     part_o = along_y(part_b[:half], 1), along_y(part_a[half:], -1)
-    acts_c = permute(acts, ("c",), lambda c: (1 - c,))
-
+    far = spread(far, "x")
+    far_c = permute(far, ("c",), lambda c: (1 - c,))
     rows = ordered("y", [rows, rows_a, rows_o, rows_b]).reshape(64 * cols, tokens)
     input_grads = lax.dot_general(weight_codes, rows, (((1,), (0,)), ((), ())), preferred_element_type=jnp.float32)
     weight_grads = 0.0
     for i in (0, 1):
-        mine = jnp.stack([acts[:, i], acts_c[:, i]], 1)
+        mine = jnp.stack([(near, far)[i], (near_c, far_c)[i]], 1)
         own, ahead, behind = (v[i * half : (i + 1) * half] for v in (part, part_a, part_b))
         blocks = ordered("y", [v.reshape(2, 4 * cols, tokens) for v in (own, ahead, part_o[i], behind)])
         weight_grads += lax.dot_general(

time: 173 us -> 178 us (1.029)
  starting transfers between devices: 78.7 us -> 104 us
  waiting for transfers between devices: 74.3 us -> 49.6 us
  local copies, waits for them, and re-layouts: 6.48 us -> 11 us
  matrix products: 7.94 us -> 10.1 us
  other arithmetic: 3.53 us -> 1.49 us
    ppermute x14 -> x15, waiting for transfers between devices: 71.9 us -> 49.6 us  [permute(): return lax.ppermute(value, axes, pairs)]
    ppermute x14 -> x15, starting transfers between devices: 74.6 us -> 92.8 us  [permute(): return lax.ppermute(value, axes, pairs)]
    all_to_all x1 -> x2, starting transfers between devices: 4.05 us -> 10.7 us  [spread(): return lax.all_to_all(copies, axis, 0, 0, tiled=True)]
    dynamic_update_slice x7, local copies, waits for them, and re-layouts: 0.35 us -> 3.38 us  [ordered(): lax.dynamic_update_slice(ring, block[None], ((me + k) % 4,) + (0,) * bloc...]
    broadcast_in_dim x1 -> x2, local copies, waits for them, and re-layouts: 1.06 us -> 3.47 us  [spread(): copies = jnp.broadcast_to(value[None], (n,) + value.shape)]
    all_to_all x1 -> x2, waiting for transfers between devices: 2.38 us -> 0.01 us  [spread(): return lax.all_to_all(copies, axis, 0, 0, tiled=True)]
    dot_general x2, matrix products: 2.3 us -> 4.5 us  [per_device(): lax.dot_general(mine, blocks, (((0, 1, 3), (0, 1, 3)), ((), ())), preferr...]
  transfers between devices with their start and end apart: 15 -> 17, of which waited for: 9 -> 7; matrix products, arithmetic and copies ran while one was open for 6% -> 8% of each run, Pallas kernels for 0% -> 0%
where the time goes in v8:
time: 178 us; the launch traced here: 177 us
  starting transfers between devices  104 us (58%)
  waiting for transfers between devices  49.6 us (28%)
  local copies, waits for them, and re-layouts  11 us (6%)
  matrix products  10.1 us (6%)
    ppermute x15, starting transfers between devices, permute(): return lax.ppermute(value, axes, pairs)  92.8 us
    ppermute x15, waiting for transfers between devices, permute(): return lax.ppermute(value, axes, pairs)  49.6 us
    all_to_all x2, starting transfers between devices, spread(): return lax.all_to_all(copies, axis, 0, 0, tiled=True)  10.7 us
    dot_general x1, matrix products, per_device(): lax.dot_general(weight_codes, rows, (((1,), (0,)), ((), ())), preferred_e...  5.61 us
    dot_general x2, matrix products, per_device(): lax.dot_general(mine, blocks, (((0, 1, 3), (0, 1, 3)), ((), ())), preferr...  4.5 us
  transfers between devices with their start and end apart: 17, of which 7 were waited for; matrix products, arithmetic and copies ran while one was open for 8% of the time, Pallas kernels for 0%

profile of v8, /device:TPU:1, one launch (start us, length us, event | category | flops | bytes accessed | tf_op | source)
XLA Modules:
  0.0 177.0 jit_solution(2464930529914491382)
XLA Ops:
  0.6 1.7 broadcast_in_dim.43
  2.4 4.8 %all-to-all-start = ((bf16[4,464,128]{2,1,0:T(8,128)(2,1)}), bf16[4,464,128]{2,1,0:T(8,128)(2,1)}, u32[]{:S(2)}, u32[]{:S(2)}) async-start(bf16[4,464,128]{2,1,0:T(8,128)(2,1)} %broadcast_in_dim.43), calls=%async_computation | async-start | bytes 950272 | tf_op jit(solution)/shard_map/all_to_all | solution.py:31
  7.2 9.6 %collective-permute-start = (bf16[116,128]{1,0:T(8,128)(2,1)}, bf16[116,128]{1,0:T(8,128)(2,1)S(1)}, u32[]{:S(2)}, u32[]{:S(2)}) collective-permute-start(bf16[116,128]{1,0:T(8,128)(2,1)} %bitcast.79), channel_id=1, source_target_pairs={{0,0},{1,1},{2,2},{3,3},{4,64},{5,65},{6,66},{7,67},{8,128},{9,129... | collective-permute-start | bytes 89096 | tf_op jit(solution)/shard_map/ppermute | solution.py:21
  16.9 0.8 dynamic_slice.3
  17.7 0.8 multiply_convert_fusion
  18.5 0.1 collective-permute-done
  18.6 0.0 all-to-all-done
  18.7 23.9 %collective-permute-start.1 = (bf16[232,128]{1,0:T(8,128)(2,1)S(1)}, bf16[232,128]{1,0:T(8,128)(2,1)S(1)}, u32[]{:S(2)}, u32[]{:S(2)}) collective-permute-start(bf16[232,128]{1,0:T(8,128)(2,1)S(1)} %pad_maximum_fusion.2), channel_id=1, source_target_pairs={{0,8},{1,9},{2,10},{3,11},{4,12},{5,13},{6,14},{7,15},{8,0},{9,1},... | collective-permute-start | bytes 178184 | tf_op jit(solution)/shard_map/ppermute | solution.py:21
  42.6 9.7 %collective-permute-done.1 = bf16[232,128]{1,0:T(8,128)(2,1)S(1)} collective-permute-done((bf16[232,128]{1,0:T(8,128)(2,1)S(1)}, bf16[232,128]{1,0:T(8,128)(2,1)S(1)}, u32[]{:S(2)}, u32[]{:S(2)}) %collective-permute-start.1) | collective-permute-done | bytes 59424 | tf_op jit(solution)/shard_map/ppermute | solution.py:21
  52.3 1.9 %collective-permute-start.2 = (bf16[2,2,116,128]{3,2,0,1:T(8,128)(2,1)S(1)}, bf16[2,2,116,128]{3,2,0,1:T(8,128)(2,1)S(1)}, u32[]{:S(2)}, u32[]{:S(2)}) collective-permute-start(bf16[2,2,116,128]{3,2,0,1:T(8,128)(2,1)S(1)} %bitcast.70), channel_id=1, source_target_pairs={{0,4},{1,5},{2,6},{3,7},{4,0},{5,1},{6,2},{7,3},{8,12},{9,13},{10,... | collective-permute-start | bytes 356360 | tf_op jit(solution)/shard_map/ppermute | solution.py:21
  54.3 12.7 %collective-permute-done.2 = bf16[2,2,116,128]{3,2,0,1:T(8,128)(2,1)S(1)} collective-permute-done((bf16[2,2,116,128]{3,2,0,1:T(8,128)(2,1)S(1)}, bf16[2,2,116,128]{3,2,0,1:T(8,128)(2,1)S(1)}, u32[]{:S(2)}, u32[]{:S(2)}) %collective-permute-start.2) | collective-permute-done | bytes 118816 | tf_op jit(solution)/shard_map/ppermute | solution.py:21
  67.0 1.9 %collective-permute-start.3 = (bf16[2,2,2,116,128]{4,3,0,1,2:T(8,128)(2,1)S(1)}, bf16[2,2,2,116,128]{4,3,0,1,2:T(8,128)(2,1)S(1)}, u32[]{:S(2)}, u32[]{:S(2)}) collective-permute-start(bf16[2,2,2,116,128]{4,3,0,1,2:T(8,128)(2,1)S(1)} %maximum_select_fusion.3), channel_id=1, source_target_pairs={{0,2},{1,3},{2,0},{3,1},{4,6},{5,7},{6,4},{7,5},{8,10},{9,11},{10,... | collective-permute-start | bytes 712712 | tf_op jit(solution)/shard_map/ppermute | solution.py:21
  69.0 7.8 %collective-permute-done.3 = bf16[2,2,2,116,128]{4,3,0,1,2:T(8,128)(2,1)S(1)} collective-permute-done((bf16[2,2,2,116,128]{4,3,0,1,2:T(8,128)(2,1)S(1)}, bf16[2,2,2,116,128]{4,3,0,1,2:T(8,128)(2,1)S(1)}, u32[]{:S(2)}, u32[]{:S(2)}) %collective-permute-start.3) | collective-permute-done | bytes 237600 | tf_op jit(solution)/shard_map/ppermute | solution.py:21
  76.8 0.1 maximum_select_fusion
  76.9 0.1 slice_bitcast_fusion.2
  76.9 0.0 copy-start.6
  76.9 2.1 %collective-permute-start.4 = (bf16[2,2,2,116,128]{4,3,0,1,2:T(8,128)(2,1)S(1)}, bf16[2,2,2,116,128]{4,3,0,1,2:T(8,128)(2,1)S(1)}, u32[]{:S(2)}, u32[]{:S(2)}) collective-permute-start(bf16[2,2,2,116,128]{4,3,0,1,2:T(8,128)(2,1)S(1)} %get-tuple-element.43), channel_id=1, source_target_pairs={{0,1},{1,0},{2,3},{3,2},{4,5},{5,4},{6,7},{7,6},{8,9},{9,8},{10,11... | collective-permute-start | bytes 712712 | tf_op jit(solution)/shard_map/ppermute | solution.py:21
  79.0 5.9 %collective-permute-done.4 = bf16[2,2,2,116,128]{4,3,0,1,2:T(8,128)(2,1)S(1)} collective-permute-done((bf16[2,2,2,116,128]{4,3,0,1,2:T(8,128)(2,1)S(1)}, bf16[2,2,2,116,128]{4,3,0,1,2:T(8,128)(2,1)S(1)}, u32[]{:S(2)}, u32[]{:S(2)}) %collective-permute-start.4) | collective-permute-done | bytes 237600 | tf_op jit(solution)/shard_map/ppermute | solution.py:21
  85.0 0.1 maximum_select_fusion.1
  85.1 2.2 %collective-permute-start.7 = (bf16[2,2,2,116,128]{4,3,0,1,2:T(8,128)(2,1)S(1)}, bf16[2,2,2,116,128]{4,3,0,1,2:T(8,128)(2,1)S(1)}, u32[]{:S(2)}, u32[]{:S(2)}) collective-permute-start(bf16[2,2,2,116,128]{4,3,0,1,2:T(8,128)(2,1)S(1)} %slice_bitcast_fusion), channel_id=1, source_target_pairs={{0,1},{1,0},{2,3},{3,2},{4,5},{5,4},{6,7},{7,6},{8,9},{9,8},{10,11... | collective-permute-start | bytes 712712 | tf_op jit(solution)/shard_map/ppermute | solution.py:21
  87.3 4.3 %collective-permute-start.11 = (bf16[4,464,128]{2,1,0:T(8,128)(2,1)}, bf16[4,464,128]{2,1,0:T(8,128)(2,1)}, u32[]{:S(2)}, u32[]{:S(2)}) collective-permute-start(bf16[4,464,128]{2,1,0:T(8,128)(2,1)} %all-to-all-done), channel_id=1, source_target_pairs={{0,64},{64,0},{1,65},{65,1},{2,66},{66,2},{3,67},{67,3},{4,68},{68... | collective-permute-start | bytes 1425416 | tf_op jit(solution)/shard_map/ppermute | solution.py:21
  91.6 0.1 broadcast_in_dim.44
  91.7 7.5 %collective-permute-start.5 = (bf16[1856,128]{1,0:T(8,128)(2,1)S(1)}, bf16[1856,128]{1,0:T(8,128)(2,1)S(1)}, u32[]{:S(2)}, u32[]{:S(2)}) collective-permute-start(bf16[1856,128]{1,0:T(8,128)(2,1)S(1)} %broadcast_in_dim.44), channel_id=1, source_target_pairs={{0,16},{16,32},{32,48},{48,0},{1,17},{17,33},{33,49},{49,1},{2,18}... | collective-permute-start | bytes 1425416 | tf_op jit(solution)/shard_map/ppermute | solution.py:21
  99.2 2.0 %collective-permute-start.6 = (bf16[1856,128]{1,0:T(8,128)(2,1)S(1)}, bf16[1856,128]{1,0:T(8,128)(2,1)S(1)}, u32[]{:S(2)}, u32[]{:S(2)}) collective-permute-start(bf16[1856,128]{1,0:T(8,128)(2,1)S(1)} %broadcast_in_dim.44), channel_id=1, source_target_pairs={{0,48},{16,0},{32,16},{48,32},{1,49},{17,1},{33,17},{49,33},{2,50}... | collective-permute-start | bytes 1425416 | tf_op jit(solution)/shard_map/ppermute | solution.py:21
  101.3 18.2 %collective-permute-start.10 = (bf16[464,128]{1,0:T(8,128)(2,1)S(1)}, bf16[464,128]{1,0:T(8,128)(2,1)}, u32[]{:S(2)}, u32[]{:S(2)}) collective-permute-start(bf16[464,128]{1,0:T(8,128)(2,1)S(1)} %bitcast.77), channel_id=1, source_target_pairs={{0,128},{128,0},{1,129},{129,1},{2,130},{130,2},{3,131},{131,3},{4... | collective-permute-start | bytes 356360 | tf_op jit(solution)/shard_map/ppermute | solution.py:21
  119.5 0.0 collective-permute-done.7
  119.5 0.1 maximum_select_fusion.2
  119.7 0.1 select_n.131
  119.8 0.1 reverse_select_fusion.1
  119.9 0.1 reverse_select_fusion
  120.0 0.0 collective-permute-done.5
  120.0 0.0 collective-permute-done.6
  120.0 0.0 copy-start.2
  120.1 0.1 pad_maximum_fusion
  120.2 2.4 %collective-permute-start.8 = (bf16[2784,128]{1,0:T(8,128)(2,1)S(1)}, bf16[2784,128]{1,0:T(8,128)(2,1)S(1)}, u32[]{:S(2)}, u32[]{:S(2)}) collective-permute-start(bf16[2784,128]{1,0:T(8,128)(2,1)S(1)} %get-tuple-element.47), channel_id=1, source_target_pairs={{0,16},{16,32},{32,48},{48,0},{1,17},{17,33},{33,49},{49,1},{2,18}... | collective-permute-start | bytes 2138120 | tf_op jit(solution)/shard_map/ppermute | solution.py:21
  122.6 4.1 %collective-permute-start.9 = (bf16[2784,128]{1,0:T(8,128)(2,1)S(1)}, bf16[2784,128]{1,0:T(8,128)(2,1)S(1)}, u32[]{:S(2)}, u32[]{:S(2)}) collective-permute-start(bf16[2784,128]{1,0:T(8,128)(2,1)S(1)} %get-tuple-element.46), channel_id=1, source_target_pairs={{0,48},{16,0},{32,16},{48,32},{1,49},{17,1},{33,17},{49,33},{2,50}... | collective-permute-start | bytes 2138120 | tf_op jit(solution)/shard_map/ppermute | solution.py:21
  126.7 0.0 copy-start.3
  126.7 0.2 broadcast_in_dim.45
  127.0 0.8 copy-done.3
  127.7 0.1 bitcast_dynamic-update-slice_fusion.1
  127.8 0.0 collective-permute-done.10
  127.8 0.0 collective-permute-done.11
  127.9 12.4 %collective-permute-done.8 = bf16[2784,128]{1,0:T(8,128)(2,1)S(1)} collective-permute-done((bf16[2784,128]{1,0:T(8,128)(2,1)S(1)}, bf16[2784,128]{1,0:T(8,128)(2,1)S(1)}, u32[]{:S(2)}, u32[]{:S(2)}) %collective-permute-start.8) | collective-permute-done | bytes 712736 | tf_op jit(solution)/shard_map/ppermute | solution.py:21
  140.2 0.9 collective-permute-done.9
  141.1 0.9 fusion.11
  141.9 0.8 fusion.10
  142.8 5.3 %collective-permute-start.14 = (bf16[928,128]{1,0:T(8,128)(2,1)}, bf16[928,128]{1,0:T(8,128)(2,1)}, u32[]{:S(2)}, u32[]{:S(2)}) collective-permute-start(bf16[928,128]{1,0:T(8,128)(2,1)} %get-tuple-element.40), channel_id=1, source_target_pairs={{0,48},{16,0},{32,16},{48,32},{1,49},{17,1},{33,17},{49,33},{2,50}... | collective-permute-start | bytes 712712 | tf_op jit(solution)/shard_map/ppermute | solution.py:21
  148.1 1.9 %collective-permute-start.12 = (bf16[928,128]{1,0:T(8,128)(2,1)}, bf16[928,128]{1,0:T(8,128)(2,1)}, u32[]{:S(2)}, u32[]{:S(2)}) collective-permute-start(bf16[928,128]{1,0:T(8,128)(2,1)} %get-tuple-element.36), channel_id=1, source_target_pairs={{0,16},{16,32},{32,48},{48,0},{1,17},{17,33},{33,49},{49,1},{2,18}... | collective-permute-start | bytes 712712 | tf_op jit(solution)/shard_map/ppermute | solution.py:21
  150.0 1.7 broadcast_in_dim.51
  151.8 5.9 %all-to-all-start.1 = ((bf16[4,464,128]{2,1,0:T(8,128)(2,1)}), bf16[4,464,128]{2,1,0:T(8,128)(2,1)}, u32[]{:S(2)}, u32[]{:S(2)}) async-start(bf16[4,464,128]{2,1,0:T(8,128)(2,1)} %broadcast_in_dim.51), calls=%async_computation.1 | async-start | bytes 950272 | tf_op jit(solution)/shard_map/all_to_all | solution.py:31
  157.6 0.1 fusion.7
  157.7 0.1 bitcast_dynamic-update-slice_fusion
  157.8 5.6 %fusion.13 = f32[128,464]{0,1:T(8,128)} fusion(bf16[464,7424]{1,0:T(8,128)(2,1)} %param.5, bf16[7424,128]{1,0:T(8,128)(2,1)S(1)} %bitcast.63), kind=kOutput, calls=%fused_computation.38 | convolution fusion | flops 881852416 | bytes 9027584 | tf_op jit(solution)/shard_map/dot_general | solution.py:99
  163.4 0.1 broadcast_in_dim.53
  163.5 1.1 constant_dynamic-update-slice_fusion.2
  164.6 0.0 all-to-all-done.1
  164.6 5.5 %collective-permute-start.13 = (bf16[4,464,128]{2,1,0:T(8,128)(2,1)}, bf16[4,464,128]{2,1,0:T(8,128)(2,1)S(1)}, u32[]{:S(2)}, u32[]{:S(2)}) collective-permute-start(bf16[4,464,128]{2,1,0:T(8,128)(2,1)} %all-to-all-done.1), channel_id=1, source_target_pairs={{0,64},{64,0},{1,65},{65,1},{2,66},{66,2},{3,67},{67,3},{4,68},{68... | collective-permute-start | bytes 1425416 | tf_op jit(solution)/shard_map/ppermute | solution.py:21
  170.1 0.1 broadcast_in_dim.50
  170.3 0.0 collective-permute-done.14
  170.3 0.0 collective-permute-done.12
  170.3 1.1 constant_dynamic-update-slice_fusion.1
  171.5 1.0 constant_dynamic-update-slice_fusion.3
  172.5 1.7 convolution_bitcast_fusion
  174.2 2.8 %fusion = f32[464,464]{1,0:T(8,128)} fusion(f32[464,464]{1,0:T(8,128)S(1)} %convolution_bitcast_fusion, bf16[4,2,464,128]{3,2,1,0:T(8,128)(2,1)S(1)} %constant_dynamic-update-slice_fusion.3, bf16[4,1,464,128]{3,2,1,0:T(8,128)(2,1)} %bitcast.23, bf16[4,1,464,128]{3,2,1,0:T(8,128)(2,1)} %bitcast.22), kind=kOutput, calls=%fused_computation.2 | convolution fusion | flops 441616640 | bytes 3622912 | tf_op jit(solution)/shard_map/dot_general | solution.py:105
  (24 shorter events, 0.4 us)
Async XLA Ops:
  2.4 16.3 %all-to-all-start = ((bf16[4,464,128]{2,1,0:T(8,128)(2,1)}), bf16[4,464,128]{2,1,0:T(8,128)(2,1)}, u32[]{:S(2)}, u32[]{:S(2)}) async-start(bf16[4,464,128]{2,1,0:T(8,128)(2,1)} %broadcast_in_dim.43), calls=%async_computation | async-start | bytes 950272 | tf_op jit(solution)/shard_map/all_to_all | solution.py:31
  7.2 11.4 %collective-permute-start = (bf16[116,128]{1,0:T(8,128)(2,1)}, bf16[116,128]{1,0:T(8,128)(2,1)S(1)}, u32[]{:S(2)}, u32[]{:S(2)}) collective-permute-start(bf16[116,128]{1,0:T(8,128)(2,1)} %bitcast.79), channel_id=1, source_target_pairs={{0,0},{1,1},{2,2},{3,3},{4,64},{5,65},{6,66},{7,67},{8,128},{9,129... | collective-permute-start | bytes 89096 | tf_op jit(solution)/shard_map/ppermute | solution.py:21
  18.7 33.6 %collective-permute-start.1 = (bf16[232,128]{1,0:T(8,128)(2,1)S(1)}, bf16[232,128]{1,0:T(8,128)(2,1)S(1)}, u32[]{:S(2)}, u32[]{:S(2)}) collective-permute-start(bf16[232,128]{1,0:T(8,128)(2,1)S(1)} %pad_maximum_fusion.2), channel_id=1, source_target_pairs={{0,8},{1,9},{2,10},{3,11},{4,12},{5,13},{6,14},{7,15},{8,0},{9,1},... | collective-permute-start | bytes 178184 | tf_op jit(solution)/shard_map/ppermute | solution.py:21
  52.3 14.7 %collective-permute-start.2 = (bf16[2,2,116,128]{3,2,0,1:T(8,128)(2,1)S(1)}, bf16[2,2,116,128]{3,2,0,1:T(8,128)(2,1)S(1)}, u32[]{:S(2)}, u32[]{:S(2)}) collective-permute-start(bf16[2,2,116,128]{3,2,0,1:T(8,128)(2,1)S(1)} %bitcast.70), channel_id=1, source_target_pairs={{0,4},{1,5},{2,6},{3,7},{4,0},{5,1},{6,2},{7,3},{8,12},{9,13},{10,... | collective-permute-start | bytes 356360 | tf_op jit(solution)/shard_map/ppermute | solution.py:21
  67.0 9.7 %collective-permute-start.3 = (bf16[2,2,2,116,128]{4,3,0,1,2:T(8,128)(2,1)S(1)}, bf16[2,2,2,116,128]{4,3,0,1,2:T(8,128)(2,1)S(1)}, u32[]{:S(2)}, u32[]{:S(2)}) collective-permute-start(bf16[2,2,2,116,128]{4,3,0,1,2:T(8,128)(2,1)S(1)} %maximum_select_fusion.3), channel_id=1, source_target_pairs={{0,2},{1,3},{2,0},{3,1},{4,6},{5,7},{6,4},{7,5},{8,10},{9,11},{10,... | collective-permute-start | bytes 712712 | tf_op jit(solution)/shard_map/ppermute | solution.py:21
  76.9 24.3 %copy-start.6 = (bf16[128,464]{0,1:T(8,128)(2,1)S(1)}, bf16[128,464]{0,1:T(8,128)(2,1)}, u32[]{:S(2)}) copy-start(bf16[128,464]{0,1:T(8,128)(2,1)} %param.4) | copy-start | bytes 356356
  76.9 8.0 %collective-permute-start.4 = (bf16[2,2,2,116,128]{4,3,0,1,2:T(8,128)(2,1)S(1)}, bf16[2,2,2,116,128]{4,3,0,1,2:T(8,128)(2,1)S(1)}, u32[]{:S(2)}, u32[]{:S(2)}) collective-permute-start(bf16[2,2,2,116,128]{4,3,0,1,2:T(8,128)(2,1)S(1)} %get-tuple-element.43), channel_id=1, source_target_pairs={{0,1},{1,0},{2,3},{3,2},{4,5},{5,4},{6,7},{7,6},{8,9},{9,8},{10,11... | collective-permute-start | bytes 712712 | tf_op jit(solution)/shard_map/ppermute | solution.py:21
  85.1 34.5 %collective-permute-start.7 = (bf16[2,2,2,116,128]{4,3,0,1,2:T(8,128)(2,1)S(1)}, bf16[2,2,2,116,128]{4,3,0,1,2:T(8,128)(2,1)S(1)}, u32[]{:S(2)}, u32[]{:S(2)}) collective-permute-start(bf16[2,2,2,116,128]{4,3,0,1,2:T(8,128)(2,1)S(1)} %slice_bitcast_fusion), channel_id=1, source_target_pairs={{0,1},{1,0},{2,3},{3,2},{4,5},{5,4},{6,7},{7,6},{8,9},{9,8},{10,11... | collective-permute-start | bytes 712712 | tf_op jit(solution)/shard_map/ppermute | solution.py:21
  87.3 40.5 %collective-permute-start.11 = (bf16[4,464,128]{2,1,0:T(8,128)(2,1)}, bf16[4,464,128]{2,1,0:T(8,128)(2,1)}, u32[]{:S(2)}, u32[]{:S(2)}) collective-permute-start(bf16[4,464,128]{2,1,0:T(8,128)(2,1)} %all-to-all-done), channel_id=1, source_target_pairs={{0,64},{64,0},{1,65},{65,1},{2,66},{66,2},{3,67},{67,3},{4,68},{68... | collective-permute-start | bytes 1425416 | tf_op jit(solution)/shard_map/ppermute | solution.py:21
  91.7 28.2 %collective-permute-start.5 = (bf16[1856,128]{1,0:T(8,128)(2,1)S(1)}, bf16[1856,128]{1,0:T(8,128)(2,1)S(1)}, u32[]{:S(2)}, u32[]{:S(2)}) collective-permute-start(bf16[1856,128]{1,0:T(8,128)(2,1)S(1)} %broadcast_in_dim.44), channel_id=1, source_target_pairs={{0,16},{16,32},{32,48},{48,0},{1,17},{17,33},{33,49},{49,1},{2,18}... | collective-permute-start | bytes 1425416 | tf_op jit(solution)/shard_map/ppermute | solution.py:21
  99.2 20.8 %collective-permute-start.6 = (bf16[1856,128]{1,0:T(8,128)(2,1)S(1)}, bf16[1856,128]{1,0:T(8,128)(2,1)S(1)}, u32[]{:S(2)}, u32[]{:S(2)}) collective-permute-start(bf16[1856,128]{1,0:T(8,128)(2,1)S(1)} %broadcast_in_dim.44), channel_id=1, source_target_pairs={{0,48},{16,0},{32,16},{48,32},{1,49},{17,1},{33,17},{49,33},{2,50}... | collective-permute-start | bytes 1425416 | tf_op jit(solution)/shard_map/ppermute | solution.py:21
  101.3 26.6 %collective-permute-start.10 = (bf16[464,128]{1,0:T(8,128)(2,1)S(1)}, bf16[464,128]{1,0:T(8,128)(2,1)}, u32[]{:S(2)}, u32[]{:S(2)}) collective-permute-start(bf16[464,128]{1,0:T(8,128)(2,1)S(1)} %bitcast.77), channel_id=1, source_target_pairs={{0,128},{128,0},{1,129},{129,1},{2,130},{130,2},{3,131},{131,3},{4... | collective-permute-start | bytes 356360 | tf_op jit(solution)/shard_map/ppermute | solution.py:21
  120.0 2.6 %copy-start = (bf16[1856,128]{1,0:T(8,128)(2,1)}, bf16[1856,128]{1,0:T(8,128)(2,1)S(1)}, u32[]{:S(2)}) copy-start(bf16[1856,128]{1,0:T(8,128)(2,1)S(1)} %collective-permute-done.5) | copy-start | bytes 1425412
  120.0 2.5 %copy-start.2 = (bf16[1856,128]{1,0:T(8,128)(2,1)}, bf16[1856,128]{1,0:T(8,128)(2,1)S(1)}, u32[]{:S(2)}) copy-start(bf16[1856,128]{1,0:T(8,128)(2,1)S(1)} %collective-permute-done.6) | copy-start | bytes 1425412
  120.2 20.0 %collective-permute-start.8 = (bf16[2784,128]{1,0:T(8,128)(2,1)S(1)}, bf16[2784,128]{1,0:T(8,128)(2,1)S(1)}, u32[]{:S(2)}, u32[]{:S(2)}) collective-permute-start(bf16[2784,128]{1,0:T(8,128)(2,1)S(1)} %get-tuple-element.47), channel_id=1, source_target_pairs={{0,16},{16,32},{32,48},{48,0},{1,17},{17,33},{33,49},{49,1},{2,18}... | collective-permute-start | bytes 2138120 | tf_op jit(solution)/shard_map/ppermute | solution.py:21
  122.6 18.5 %collective-permute-start.9 = (bf16[2784,128]{1,0:T(8,128)(2,1)S(1)}, bf16[2784,128]{1,0:T(8,128)(2,1)S(1)}, u32[]{:S(2)}, u32[]{:S(2)}) collective-permute-start(bf16[2784,128]{1,0:T(8,128)(2,1)S(1)} %get-tuple-element.46), channel_id=1, source_target_pairs={{0,48},{16,0},{32,16},{48,32},{1,49},{17,1},{33,17},{49,33},{2,50}... | collective-permute-start | bytes 2138120 | tf_op jit(solution)/shard_map/ppermute | solution.py:21
  126.7 1.0 copy-start.3
  141.9 15.8 %copy-start.1 = (bf16[1856,128]{1,0:T(8,128)(2,1)S(1)}, bf16[1856,128]{1,0:T(8,128)(2,1)}, u32[]{:S(2)}) copy-start(bf16[1856,128]{1,0:T(8,128)(2,1)} %copy-done) | copy-start | bytes 1425412
  142.8 27.5 %collective-permute-start.14 = (bf16[928,128]{1,0:T(8,128)(2,1)}, bf16[928,128]{1,0:T(8,128)(2,1)}, u32[]{:S(2)}, u32[]{:S(2)}) collective-permute-start(bf16[928,128]{1,0:T(8,128)(2,1)} %get-tuple-element.40), channel_id=1, source_target_pairs={{0,48},{16,0},{32,16},{48,32},{1,49},{17,1},{33,17},{49,33},{2,50}... | collective-permute-start | bytes 712712 | tf_op jit(solution)/shard_map/ppermute | solution.py:21
  148.1 22.2 %collective-permute-start.12 = (bf16[928,128]{1,0:T(8,128)(2,1)}, bf16[928,128]{1,0:T(8,128)(2,1)}, u32[]{:S(2)}, u32[]{:S(2)}) collective-permute-start(bf16[928,128]{1,0:T(8,128)(2,1)} %get-tuple-element.36), channel_id=1, source_target_pairs={{0,16},{16,32},{32,48},{48,0},{1,17},{17,33},{33,49},{49,1},{2,18}... | collective-permute-start | bytes 712712 | tf_op jit(solution)/shard_map/ppermute | solution.py:21
  151.8 12.8 %all-to-all-start.1 = ((bf16[4,464,128]{2,1,0:T(8,128)(2,1)}), bf16[4,464,128]{2,1,0:T(8,128)(2,1)}, u32[]{:S(2)}, u32[]{:S(2)}) async-start(bf16[4,464,128]{2,1,0:T(8,128)(2,1)} %broadcast_in_dim.51), calls=%async_computation.1 | async-start | bytes 950272 | tf_op jit(solution)/shard_map/all_to_all | solution.py:31
  163.4 6.8 %copy-start.5 = (bf16[928,128]{1,0:T(8,128)(2,1)S(1)}, bf16[928,128]{1,0:T(8,128)(2,1)}, u32[]{:S(2)}) copy-start(bf16[928,128]{1,0:T(8,128)(2,1)} %get-tuple-element.39) | copy-start | bytes 712708
  163.4 8.0 %copy-start.4 = (bf16[928,128]{1,0:T(8,128)(2,1)S(1)}, bf16[928,128]{1,0:T(8,128)(2,1)}, u32[]{:S(2)}) copy-start(bf16[928,128]{1,0:T(8,128)(2,1)} %get-tuple-element.37) | copy-start | bytes 712708
  164.6 7.8 %collective-permute-start.13 = (bf16[4,464,128]{2,1,0:T(8,128)(2,1)}, bf16[4,464,128]{2,1,0:T(8,128)(2,1)S(1)}, u32[]{:S(2)}, u32[]{:S(2)}) collective-permute-start(bf16[4,464,128]{2,1,0:T(8,128)(2,1)} %all-to-all-done.1), channel_id=1, source_target_pairs={{0,64},{64,0},{1,65},{65,1},{2,66},{66,2},{3,67},{67,3},{4,68},{68... | collective-permute-start | bytes 1425416 | tf_op jit(solution)/shard_map/ppermute | solution.py:21

commit v9 on v7

--- a/solution.py
+++ b/solution.py
@@ -65,14 +65,14 @@
     scaled = (g.astype(jnp.float32) * scale[:, None]).astype(jnp.bfloat16)
 
     part = permute(g, AXES, lambda x, zh, c, y, za, zb: (y, za // 2, za % 2, x, 2 * zh + c, zb))
-    far = permute(a, ("zh",), lambda h: (1 - h,))
     part, scaled = sync((part, scaled))
 
     both = jnp.concatenate([scaled, part])
-    both, acts = sync((paired(both, 0, 0), jnp.stack([a, far])))
+    both = sync(paired(both, 0, 0))
     both = both.reshape(2, 2, cols, tokens).transpose(1, 0, 2, 3)
     both = sync(paired(both, 1, 2))
-    both = sync(paired(both, 2, 3))
+    both, a = sync((paired(both, 2, 3), a))
+    far = permute(a, ("zh",), lambda h: (1 - h,))
 
     rows, part = sync((paired(both[0], 3, 3), both[1]))
     rows = rows.reshape(16 * cols, tokens)
@@ -82,11 +82,11 @@
     part = jnp.where(lax.axis_index("c") == 0, part, part[:, ::-1])
     part = jnp.where(lax.axis_index("zh") == 0, part, part[::-1])
     part = part.reshape(16 * cols, tokens)
-    rows_b, rows_a, part, acts = sync((rows_b, rows_a, part, acts))
+    rows_b, rows_a, part, a, far = sync((rows_b, rows_a, part, a, far))
 
     up = along_y(jnp.concatenate([rows_b[:half], part]), 1)
     down = along_y(jnp.concatenate([rows_a[half:], part]), -1)
-    acts = spread(acts, "x")
+    acts = spread(jnp.stack([a, far]), "x")
     up, down, acts = sync((up, down, acts))
     rows_o = jnp.concatenate([up[:half], down[:half]])
     part_b, part_a = up[half:], down[half:]

time: 173 us -> 174 us (level)
  starting transfers between devices: 78.7 us -> 104 us
  waiting for transfers between devices: 74.3 us -> 49.3 us
    ppermute x14, waiting for transfers between devices: 71.9 us -> 42.5 us  [permute(): return lax.ppermute(value, axes, pairs)]
    ppermute x14, starting transfers between devices: 74.6 us -> 95.6 us  [permute(): return lax.ppermute(value, axes, pairs)]
    all_to_all x1, starting transfers between devices: 4.05 us -> 8.67 us  [spread(): return lax.all_to_all(copies, axis, 0, 0, tiled=True)]
    all_to_all x1, waiting for transfers between devices: 2.38 us -> 6.78 us  [spread(): return lax.all_to_all(copies, axis, 0, 0, tiled=True)]
  transfers between devices with their start and end apart: 15 -> 15, of which waited for: 9 -> 8; matrix products, arithmetic and copies ran while one was open for 6% -> 6% of each run, Pallas kernels for 0% -> 0%
where the time goes in v9:
time: 174 us; the launch traced here: 173 us
  starting transfers between devices  104 us (60%)
  waiting for transfers between devices  49.3 us (28%)
  matrix products  7.94 us (5%)
  local copies, waits for them, and re-layouts  7.73 us (4%)
  other arithmetic  2.63 us (2%)
    ppermute x14, starting transfers between devices, permute(): return lax.ppermute(value, axes, pairs)  95.6 us
    ppermute x14, waiting for transfers between devices, permute(): return lax.ppermute(value, axes, pairs)  42.5 us
    all_to_all x1, starting transfers between devices, spread(): return lax.all_to_all(copies, axis, 0, 0, tiled=True)  8.67 us
    all_to_all x1, waiting for transfers between devices, spread(): return lax.all_to_all(copies, axis, 0, 0, tiled=True)  6.78 us
    dot_general x1, matrix products, per_device(): lax.dot_general(weight_codes, rows, (((1,), (0,)), ((), ())), preferred_e...  5.64 us
  transfers between devices with their start and end apart: 15, of which 8 were waited for; matrix products, arithmetic and copies ran while one was open for 6% of the time, Pallas kernels for 0%

profile of v9, /device:TPU:1, one launch (start us, length us, event | category | flops | bytes accessed | tf_op | source)
XLA Modules:
  0.0 173.0 jit_solution(5330320741478772682)
XLA Ops:
  0.6 10.2 %collective-permute-start = (bf16[116,128]{1,0:T(8,128)(2,1)}, bf16[116,128]{1,0:T(8,128)(2,1)S(1)}, u32[]{:S(2)}, u32[]{:S(2)}) collective-permute-start(bf16[116,128]{1,0:T(8,128)(2,1)} %bitcast.78), channel_id=1, source_target_pairs={{0,0},{1,1},{2,2},{3,3},{4,64},{5,65},{6,66},{7,67},{8,128},{9,129... | collective-permute-start | bytes 89096 | tf_op jit(solution)/shard_map/ppermute | solution.py:21
  10.9 0.8 dynamic_slice.3
  11.6 0.8 multiply_convert_fusion
  12.5 0.1 collective-permute-done
  12.6 23.9 %collective-permute-start.1 = (bf16[232,128]{1,0:T(8,128)(2,1)S(1)}, bf16[232,128]{1,0:T(8,128)(2,1)S(1)}, u32[]{:S(2)}, u32[]{:S(2)}) collective-permute-start(bf16[232,128]{1,0:T(8,128)(2,1)S(1)} %pad_maximum_fusion.3), channel_id=1, source_target_pairs={{0,8},{1,9},{2,10},{3,11},{4,12},{5,13},{6,14},{7,15},{8,0},{9,1},... | collective-permute-start | bytes 178184 | tf_op jit(solution)/shard_map/ppermute | solution.py:21
  36.6 9.7 %collective-permute-done.1 = bf16[232,128]{1,0:T(8,128)(2,1)S(1)} collective-permute-done((bf16[232,128]{1,0:T(8,128)(2,1)S(1)}, bf16[232,128]{1,0:T(8,128)(2,1)S(1)}, u32[]{:S(2)}, u32[]{:S(2)}) %collective-permute-start.1) | collective-permute-done | bytes 59424 | tf_op jit(solution)/shard_map/ppermute | solution.py:21
  46.3 1.9 %collective-permute-start.2 = (bf16[2,2,116,128]{3,2,0,1:T(8,128)(2,1)S(1)}, bf16[2,2,116,128]{3,2,0,1:T(8,128)(2,1)S(1)}, u32[]{:S(2)}, u32[]{:S(2)}) collective-permute-start(bf16[2,2,116,128]{3,2,0,1:T(8,128)(2,1)S(1)} %bitcast.66), channel_id=1, source_target_pairs={{0,4},{1,5},{2,6},{3,7},{4,0},{5,1},{6,2},{7,3},{8,12},{9,13},{10,... | collective-permute-start | bytes 356360 | tf_op jit(solution)/shard_map/ppermute | solution.py:21
  48.2 12.8 %collective-permute-done.2 = bf16[2,2,116,128]{3,2,0,1:T(8,128)(2,1)S(1)} collective-permute-done((bf16[2,2,116,128]{3,2,0,1:T(8,128)(2,1)S(1)}, bf16[2,2,116,128]{3,2,0,1:T(8,128)(2,1)S(1)}, u32[]{:S(2)}, u32[]{:S(2)}) %collective-permute-start.2) | collective-permute-done | bytes 118816 | tf_op jit(solution)/shard_map/ppermute | solution.py:21
  61.0 2.1 %collective-permute-start.3 = (bf16[2,2,2,116,128]{4,3,0,1,2:T(8,128)(2,1)S(1)}, bf16[2,2,2,116,128]{4,3,0,1,2:T(8,128)(2,1)S(1)}, u32[]{:S(2)}, u32[]{:S(2)}) collective-permute-start(bf16[2,2,2,116,128]{4,3,0,1,2:T(8,128)(2,1)S(1)} %maximum_select_fusion.3), channel_id=1, source_target_pairs={{0,2},{1,3},{2,0},{3,1},{4,6},{5,7},{6,4},{7,5},{8,10},{9,11},{10,... | collective-permute-start | bytes 712712 | tf_op jit(solution)/shard_map/ppermute | solution.py:21
  63.1 7.8 %collective-permute-done.3 = bf16[2,2,2,116,128]{4,3,0,1,2:T(8,128)(2,1)S(1)} collective-permute-done((bf16[2,2,2,116,128]{4,3,0,1,2:T(8,128)(2,1)S(1)}, bf16[2,2,2,116,128]{4,3,0,1,2:T(8,128)(2,1)S(1)}, u32[]{:S(2)}, u32[]{:S(2)}) %collective-permute-start.3) | collective-permute-done | bytes 237600 | tf_op jit(solution)/shard_map/ppermute | solution.py:21
  70.9 0.1 maximum_select_fusion
  71.0 0.1 slice_bitcast_fusion.2
  71.1 1.9 %collective-permute-start.4 = (bf16[2,2,2,116,128]{4,3,0,1,2:T(8,128)(2,1)S(1)}, bf16[2,2,2,116,128]{4,3,0,1,2:T(8,128)(2,1)S(1)}, u32[]{:S(2)}, u32[]{:S(2)}) collective-permute-start(bf16[2,2,2,116,128]{4,3,0,1,2:T(8,128)(2,1)S(1)} %get-tuple-element.41), channel_id=1, source_target_pairs={{0,1},{1,0},{2,3},{3,2},{4,5},{5,4},{6,7},{7,6},{8,9},{9,8},{10,11... | collective-permute-start | bytes 712712 | tf_op jit(solution)/shard_map/ppermute | solution.py:21
  73.0 5.9 %collective-permute-done.4 = bf16[2,2,2,116,128]{4,3,0,1,2:T(8,128)(2,1)S(1)} collective-permute-done((bf16[2,2,2,116,128]{4,3,0,1,2:T(8,128)(2,1)S(1)}, bf16[2,2,2,116,128]{4,3,0,1,2:T(8,128)(2,1)S(1)}, u32[]{:S(2)}, u32[]{:S(2)}) %collective-permute-start.4) | collective-permute-done | bytes 237600 | tf_op jit(solution)/shard_map/ppermute | solution.py:21
  79.0 0.1 maximum_select_fusion.1
  79.0 2.2 %collective-permute-start.7 = (bf16[2,2,2,116,128]{4,3,0,1,2:T(8,128)(2,1)S(1)}, bf16[2,2,2,116,128]{4,3,0,1,2:T(8,128)(2,1)S(1)}, u32[]{:S(2)}, u32[]{:S(2)}) collective-permute-start(bf16[2,2,2,116,128]{4,3,0,1,2:T(8,128)(2,1)S(1)} %slice_bitcast_fusion), channel_id=1, source_target_pairs={{0,1},{1,0},{2,3},{3,2},{4,5},{5,4},{6,7},{7,6},{8,9},{9,8},{10,11... | collective-permute-start | bytes 712712 | tf_op jit(solution)/shard_map/ppermute | solution.py:21
  81.3 0.0 copy-done.6
  81.3 11.4 %collective-permute-start.8 = (bf16[464,128]{1,0:T(8,128)(2,1)S(1)}, bf16[464,128]{1,0:T(8,128)(2,1)S(1)}, u32[]{:S(2)}, u32[]{:S(2)}) collective-permute-start(bf16[464,128]{1,0:T(8,128)(2,1)S(1)} %bitcast.74), channel_id=1, source_target_pairs={{0,128},{128,0},{1,129},{129,1},{2,130},{130,2},{3,131},{131,3},{4... | collective-permute-start | bytes 356360 | tf_op jit(solution)/shard_map/ppermute | solution.py:21
  92.8 0.1 broadcast_in_dim.37
  92.9 5.0 %collective-permute-start.5 = (bf16[1856,128]{1,0:T(8,128)(2,1)S(1)}, bf16[1856,128]{1,0:T(8,128)(2,1)S(1)}, u32[]{:S(2)}, u32[]{:S(2)}) collective-permute-start(bf16[1856,128]{1,0:T(8,128)(2,1)S(1)} %broadcast_in_dim.37), channel_id=1, source_target_pairs={{0,16},{16,32},{32,48},{48,0},{1,17},{17,33},{33,49},{49,1},{2,18}... | collective-permute-start | bytes 1425416 | tf_op jit(solution)/shard_map/ppermute | solution.py:21
  97.9 5.6 %collective-permute-start.6 = (bf16[1856,128]{1,0:T(8,128)(2,1)S(1)}, bf16[1856,128]{1,0:T(8,128)(2,1)S(1)}, u32[]{:S(2)}, u32[]{:S(2)}) collective-permute-start(bf16[1856,128]{1,0:T(8,128)(2,1)S(1)} %broadcast_in_dim.37), channel_id=1, source_target_pairs={{0,48},{16,0},{32,16},{48,32},{1,49},{17,1},{33,17},{49,33},{2,50}... | collective-permute-start | bytes 1425416 | tf_op jit(solution)/shard_map/ppermute | solution.py:21
  103.5 0.0 collective-permute-done.7
  103.5 0.1 maximum_select_fusion.2
  103.6 0.1 select_n.131
  103.7 0.1 reverse_select_fusion.1
  103.8 0.1 reverse_select_fusion
  103.9 4.4 %collective-permute-done.8 = bf16[464,128]{1,0:T(8,128)(2,1)S(1)} collective-permute-done((bf16[464,128]{1,0:T(8,128)(2,1)S(1)}, bf16[464,128]{1,0:T(8,128)(2,1)S(1)}, u32[]{:S(2)}, u32[]{:S(2)}) %collective-permute-start.8) | collective-permute-done | bytes 118816 | tf_op jit(solution)/shard_map/ppermute | solution.py:21
  108.3 0.0 collective-permute-done.5
  108.3 1.8 %collective-permute-done.6 = bf16[1856,128]{1,0:T(8,128)(2,1)S(1)} collective-permute-done((bf16[1856,128]{1,0:T(8,128)(2,1)S(1)}, bf16[1856,128]{1,0:T(8,128)(2,1)S(1)}, u32[]{:S(2)}, u32[]{:S(2)}) %collective-permute-start.6) | collective-permute-done | bytes 475168 | tf_op jit(solution)/shard_map/ppermute | solution.py:21
  110.1 1.2 pad_maximum_fusion
  111.3 3.6 %collective-permute-start.9 = (bf16[2784,128]{1,0:T(8,128)(2,1)}, bf16[2784,128]{1,0:T(8,128)(2,1)}, u32[]{:S(2)}, u32[]{:S(2)}) collective-permute-start(bf16[2784,128]{1,0:T(8,128)(2,1)} %get-tuple-element.45), channel_id=1, source_target_pairs={{0,16},{16,32},{32,48},{48,0},{1,17},{17,33},{33,49},{49,1},{2,18}... | collective-permute-start | bytes 2138120 | tf_op jit(solution)/shard_map/ppermute | solution.py:21
  115.0 2.8 %collective-permute-start.10 = (bf16[2784,128]{1,0:T(8,128)(2,1)}, bf16[2784,128]{1,0:T(8,128)(2,1)}, u32[]{:S(2)}, u32[]{:S(2)}) collective-permute-start(bf16[2784,128]{1,0:T(8,128)(2,1)} %get-tuple-element.44), channel_id=1, source_target_pairs={{0,48},{16,0},{32,16},{48,32},{1,49},{17,1},{33,17},{49,33},{2,50}... | collective-permute-start | bytes 2138120 | tf_op jit(solution)/shard_map/ppermute | solution.py:21
  117.8 0.0 copy-done.2
  117.8 1.1 broadcast_in_dim.40
  118.9 8.7 %all-to-all-start = ((bf16[4,2,464,128]{3,2,1,0:T(8,128)(2,1)}), bf16[4,2,464,128]{3,2,1,0:T(8,128)(2,1)S(1)}, u32[]{:S(2)}, u32[]{:S(2)}) async-start(bf16[4,2,464,128]{3,2,1,0:T(8,128)(2,1)} %broadcast_in_dim.40), calls=%async_computation | async-start | bytes 1900544 | tf_op jit(solution)/shard_map/all_to_all | solution.py:31
  127.6 0.8 fusion.14
  128.4 0.2 broadcast_in_dim.38
  128.6 0.1 bitcast_dynamic-update-slice_fusion.1
  128.7 0.0 collective-permute-done.9
  128.7 1.2 copy-done
  130.0 0.0 collective-permute-done.10
  130.0 6.8 %all-to-all-done = bf16[4,2,464,128]{3,2,1,0:T(8,128)(2,1)S(1)} async-done(((bf16[4,2,464,128]{3,2,1,0:T(8,128)(2,1)}), bf16[4,2,464,128]{3,2,1,0:T(8,128)(2,1)S(1)}, u32[]{:S(2)}, u32[]{:S(2)}) %all-to-all-start) | async-done | bytes 950304 | tf_op jit(solution)/shard_map/all_to_all | solution.py:31
  136.8 1.2 fusion.13
  138.0 1.2 fusion.12
  139.2 3.7 %collective-permute-start.13 = (bf16[928,128]{1,0:T(8,128)(2,1)S(1)}, bf16[928,128]{1,0:T(8,128)(2,1)S(1)}, u32[]{:S(2)}, u32[]{:S(2)}) collective-permute-start(bf16[928,128]{1,0:T(8,128)(2,1)S(1)} %get-tuple-element.38), channel_id=1, source_target_pairs={{0,48},{16,0},{32,16},{48,32},{1,49},{17,1},{33,17},{49,33},{2,50}... | collective-permute-start | bytes 712712 | tf_op jit(solution)/shard_map/ppermute | solution.py:21
  142.9 1.9 %collective-permute-start.12 = (bf16[928,128]{1,0:T(8,128)(2,1)S(1)}, bf16[928,128]{1,0:T(8,128)(2,1)S(1)}, u32[]{:S(2)}, u32[]{:S(2)}) collective-permute-start(bf16[928,128]{1,0:T(8,128)(2,1)S(1)} %get-tuple-element.34), channel_id=1, source_target_pairs={{0,16},{16,32},{32,48},{48,0},{1,17},{17,33},{33,49},{49,1},{2,18}... | collective-permute-start | bytes 712712 | tf_op jit(solution)/shard_map/ppermute | solution.py:21
  144.8 19.3 %collective-permute-start.11 = (bf16[4,2,464,128]{3,2,1,0:T(8,128)(2,1)S(1)}, bf16[4,2,464,128]{3,2,1,0:T(8,128)(2,1)S(1)}, u32[]{:S(2)}, u32[]{:S(2)}) collective-permute-start(bf16[4,2,464,128]{3,2,1,0:T(8,128)(2,1)S(1)} %all-to-all-done), channel_id=1, source_target_pairs={{0,64},{64,0},{1,65},{65,1},{2,66},{66,2},{3,67},{67,3},{4,68},{68... | collective-permute-start | bytes 2850824 | tf_op jit(solution)/shard_map/ppermute | solution.py:21
  164.1 0.0 copy-done.1
  164.2 0.1 fusion.7
  164.2 0.1 bitcast_dynamic-update-slice_fusion
  164.3 0.0 copy-start.5
  164.3 0.0 copy-start.4
  164.3 5.6 %fusion.15 = f32[128,464]{0,1:T(8,128)} fusion(bf16[464,7424]{1,0:T(8,128)(2,1)} %param.5, bf16[7424,128]{1,0:T(8,128)(2,1)S(1)} %bitcast.57), kind=kOutput, calls=%fused_computation.41 | convolution fusion | flops 881852416 | bytes 9027584 | tf_op jit(solution)/shard_map/dot_general | solution.py:98
  170.0 0.1 broadcast_in_dim.46
  170.1 0.0 copy-done.4
  170.2 0.1 broadcast_in_dim.44
  170.3 0.1 fusion.10
  170.4 0.0 collective-permute-done.13
  170.4 0.0 collective-permute-done.12
  170.4 0.1 constant_dynamic-update-slice_fusion.1
  170.6 0.0 collective-permute-done.11
  170.6 0.1 fusion.11
  170.7 0.7 convolution_bitcast_fusion
  171.4 1.6 fusion
  (22 shorter events, 0.4 us)
Async XLA Ops:
  0.6 12.0 %collective-permute-start = (bf16[116,128]{1,0:T(8,128)(2,1)}, bf16[116,128]{1,0:T(8,128)(2,1)S(1)}, u32[]{:S(2)}, u32[]{:S(2)}) collective-permute-start(bf16[116,128]{1,0:T(8,128)(2,1)} %bitcast.78), channel_id=1, source_target_pairs={{0,0},{1,1},{2,2},{3,3},{4,64},{5,65},{6,66},{7,67},{8,128},{9,129... | collective-permute-start | bytes 89096 | tf_op jit(solution)/shard_map/ppermute | solution.py:21
  12.6 33.6 %collective-permute-start.1 = (bf16[232,128]{1,0:T(8,128)(2,1)S(1)}, bf16[232,128]{1,0:T(8,128)(2,1)S(1)}, u32[]{:S(2)}, u32[]{:S(2)}) collective-permute-start(bf16[232,128]{1,0:T(8,128)(2,1)S(1)} %pad_maximum_fusion.3), channel_id=1, source_target_pairs={{0,8},{1,9},{2,10},{3,11},{4,12},{5,13},{6,14},{7,15},{8,0},{9,1},... | collective-permute-start | bytes 178184 | tf_op jit(solution)/shard_map/ppermute | solution.py:21
  46.3 14.7 %collective-permute-start.2 = (bf16[2,2,116,128]{3,2,0,1:T(8,128)(2,1)S(1)}, bf16[2,2,116,128]{3,2,0,1:T(8,128)(2,1)S(1)}, u32[]{:S(2)}, u32[]{:S(2)}) collective-permute-start(bf16[2,2,116,128]{3,2,0,1:T(8,128)(2,1)S(1)} %bitcast.66), channel_id=1, source_target_pairs={{0,4},{1,5},{2,6},{3,7},{4,0},{5,1},{6,2},{7,3},{8,12},{9,13},{10,... | collective-permute-start | bytes 356360 | tf_op jit(solution)/shard_map/ppermute | solution.py:21
  61.0 20.3 %copy-start.6 = (bf16[128,464]{0,1:T(8,128)(2,1)S(1)}, bf16[128,464]{0,1:T(8,128)(2,1)}, u32[]{:S(2)}) copy-start(bf16[128,464]{0,1:T(8,128)(2,1)} %param.4) | copy-start | bytes 356356
  61.0 9.9 %collective-permute-start.3 = (bf16[2,2,2,116,128]{4,3,0,1,2:T(8,128)(2,1)S(1)}, bf16[2,2,2,116,128]{4,3,0,1,2:T(8,128)(2,1)S(1)}, u32[]{:S(2)}, u32[]{:S(2)}) collective-permute-start(bf16[2,2,2,116,128]{4,3,0,1,2:T(8,128)(2,1)S(1)} %maximum_select_fusion.3), channel_id=1, source_target_pairs={{0,2},{1,3},{2,0},{3,1},{4,6},{5,7},{6,4},{7,5},{8,10},{9,11},{10,... | collective-permute-start | bytes 712712 | tf_op jit(solution)/shard_map/ppermute | solution.py:21
  71.1 7.9 %collective-permute-start.4 = (bf16[2,2,2,116,128]{4,3,0,1,2:T(8,128)(2,1)S(1)}, bf16[2,2,2,116,128]{4,3,0,1,2:T(8,128)(2,1)S(1)}, u32[]{:S(2)}, u32[]{:S(2)}) collective-permute-start(bf16[2,2,2,116,128]{4,3,0,1,2:T(8,128)(2,1)S(1)} %get-tuple-element.41), channel_id=1, source_target_pairs={{0,1},{1,0},{2,3},{3,2},{4,5},{5,4},{6,7},{7,6},{8,9},{9,8},{10,11... | collective-permute-start | bytes 712712 | tf_op jit(solution)/shard_map/ppermute | solution.py:21
  79.0 24.4 %collective-permute-start.7 = (bf16[2,2,2,116,128]{4,3,0,1,2:T(8,128)(2,1)S(1)}, bf16[2,2,2,116,128]{4,3,0,1,2:T(8,128)(2,1)S(1)}, u32[]{:S(2)}, u32[]{:S(2)}) collective-permute-start(bf16[2,2,2,116,128]{4,3,0,1,2:T(8,128)(2,1)S(1)} %slice_bitcast_fusion), channel_id=1, source_target_pairs={{0,1},{1,0},{2,3},{3,2},{4,5},{5,4},{6,7},{7,6},{8,9},{9,8},{10,11... | collective-permute-start | bytes 712712 | tf_op jit(solution)/shard_map/ppermute | solution.py:21
  81.3 27.0 %collective-permute-start.8 = (bf16[464,128]{1,0:T(8,128)(2,1)S(1)}, bf16[464,128]{1,0:T(8,128)(2,1)S(1)}, u32[]{:S(2)}, u32[]{:S(2)}) collective-permute-start(bf16[464,128]{1,0:T(8,128)(2,1)S(1)} %bitcast.74), channel_id=1, source_target_pairs={{0,128},{128,0},{1,129},{129,1},{2,130},{130,2},{3,131},{131,3},{4... | collective-permute-start | bytes 356360 | tf_op jit(solution)/shard_map/ppermute | solution.py:21
  92.9 15.4 %collective-permute-start.5 = (bf16[1856,128]{1,0:T(8,128)(2,1)S(1)}, bf16[1856,128]{1,0:T(8,128)(2,1)S(1)}, u32[]{:S(2)}, u32[]{:S(2)}) collective-permute-start(bf16[1856,128]{1,0:T(8,128)(2,1)S(1)} %broadcast_in_dim.37), channel_id=1, source_target_pairs={{0,16},{16,32},{32,48},{48,0},{1,17},{17,33},{33,49},{49,1},{2,18}... | collective-permute-start | bytes 1425416 | tf_op jit(solution)/shard_map/ppermute | solution.py:21
  97.9 12.2 %collective-permute-start.6 = (bf16[1856,128]{1,0:T(8,128)(2,1)S(1)}, bf16[1856,128]{1,0:T(8,128)(2,1)S(1)}, u32[]{:S(2)}, u32[]{:S(2)}) collective-permute-start(bf16[1856,128]{1,0:T(8,128)(2,1)S(1)} %broadcast_in_dim.37), channel_id=1, source_target_pairs={{0,48},{16,0},{32,16},{48,32},{1,49},{17,1},{33,17},{49,33},{2,50}... | collective-permute-start | bytes 1425416 | tf_op jit(solution)/shard_map/ppermute | solution.py:21
  108.3 9.5 %copy-start.2 = (bf16[1856,128]{1,0:T(8,128)(2,1)}, bf16[1856,128]{1,0:T(8,128)(2,1)S(1)}, u32[]{:S(2)}) copy-start(bf16[1856,128]{1,0:T(8,128)(2,1)S(1)} %collective-permute-done.5) | copy-start | bytes 1425412
  111.3 17.4 %collective-permute-start.9 = (bf16[2784,128]{1,0:T(8,128)(2,1)}, bf16[2784,128]{1,0:T(8,128)(2,1)}, u32[]{:S(2)}, u32[]{:S(2)}) collective-permute-start(bf16[2784,128]{1,0:T(8,128)(2,1)} %get-tuple-element.45), channel_id=1, source_target_pairs={{0,16},{16,32},{32,48},{48,0},{1,17},{17,33},{33,49},{49,1},{2,18}... | collective-permute-start | bytes 2138120 | tf_op jit(solution)/shard_map/ppermute | solution.py:21
  115.0 15.0 %collective-permute-start.10 = (bf16[2784,128]{1,0:T(8,128)(2,1)}, bf16[2784,128]{1,0:T(8,128)(2,1)}, u32[]{:S(2)}, u32[]{:S(2)}) collective-permute-start(bf16[2784,128]{1,0:T(8,128)(2,1)} %get-tuple-element.44), channel_id=1, source_target_pairs={{0,48},{16,0},{32,16},{48,32},{1,49},{17,1},{33,17},{49,33},{2,50}... | collective-permute-start | bytes 2138120 | tf_op jit(solution)/shard_map/ppermute | solution.py:21
  118.9 17.9 %all-to-all-start = ((bf16[4,2,464,128]{3,2,1,0:T(8,128)(2,1)}), bf16[4,2,464,128]{3,2,1,0:T(8,128)(2,1)S(1)}, u32[]{:S(2)}, u32[]{:S(2)}) async-start(bf16[4,2,464,128]{3,2,1,0:T(8,128)(2,1)} %broadcast_in_dim.40), calls=%async_computation | async-start | bytes 1900544 | tf_op jit(solution)/shard_map/all_to_all | solution.py:31
  128.7 1.3 copy-start
  128.7 35.5 %copy-start.3 = (bf16[1856,128]{1,0:T(8,128)(2,1)S(1)}, bf16[1856,128]{1,0:T(8,128)(2,1)}, u32[]{:S(2)}) copy-start(bf16[1856,128]{1,0:T(8,128)(2,1)} %copy-done.2) | copy-start | bytes 1425412
  130.0 34.1 %copy-start.1 = (bf16[4,1856,128]{2,1,0:T(8,128)(2,1)S(1)}, bf16[4,1856,128]{2,1,0:T(8,128)(2,1)}, u32[]{:S(2)}) copy-start(bf16[4,1856,128]{2,1,0:T(8,128)(2,1)} %copy-done) | copy-start | bytes 5701636
  139.2 31.2 %collective-permute-start.13 = (bf16[928,128]{1,0:T(8,128)(2,1)S(1)}, bf16[928,128]{1,0:T(8,128)(2,1)S(1)}, u32[]{:S(2)}, u32[]{:S(2)}) collective-permute-start(bf16[928,128]{1,0:T(8,128)(2,1)S(1)} %get-tuple-element.38), channel_id=1, source_target_pairs={{0,48},{16,0},{32,16},{48,32},{1,49},{17,1},{33,17},{49,33},{2,50}... | collective-permute-start | bytes 712712 | tf_op jit(solution)/shard_map/ppermute | solution.py:21
  142.9 27.5 %collective-permute-start.12 = (bf16[928,128]{1,0:T(8,128)(2,1)S(1)}, bf16[928,128]{1,0:T(8,128)(2,1)S(1)}, u32[]{:S(2)}, u32[]{:S(2)}) collective-permute-start(bf16[928,128]{1,0:T(8,128)(2,1)S(1)} %get-tuple-element.34), channel_id=1, source_target_pairs={{0,16},{16,32},{32,48},{48,0},{1,17},{17,33},{33,49},{49,1},{2,18}... | collective-permute-start | bytes 712712 | tf_op jit(solution)/shard_map/ppermute | solution.py:21
  144.8 25.8 %collective-permute-start.11 = (bf16[4,2,464,128]{3,2,1,0:T(8,128)(2,1)S(1)}, bf16[4,2,464,128]{3,2,1,0:T(8,128)(2,1)S(1)}, u32[]{:S(2)}, u32[]{:S(2)}) collective-permute-start(bf16[4,2,464,128]{3,2,1,0:T(8,128)(2,1)S(1)} %all-to-all-done), channel_id=1, source_target_pairs={{0,64},{64,0},{1,65},{65,1},{2,66},{66,2},{3,67},{67,3},{4,68},{68... | collective-permute-start | bytes 2850824 | tf_op jit(solution)/shard_map/ppermute | solution.py:21
  164.3 5.7 %copy-start.5 = (bf16[928,128]{1,0:T(8,128)(2,1)S(1)}, bf16[928,128]{1,0:T(8,128)(2,1)}, u32[]{:S(2)}) copy-start(bf16[928,128]{1,0:T(8,128)(2,1)} %get-tuple-element.43) | copy-start | bytes 712708
  164.3 5.8 %copy-start.4 = (bf16[928,128]{1,0:T(8,128)(2,1)S(1)}, bf16[928,128]{1,0:T(8,128)(2,1)}, u32[]{:S(2)}) copy-start(bf16[928,128]{1,0:T(8,128)(2,1)} %get-tuple-element.42) | copy-start | bytes 712708

commit v10 on v9

--- a/solution.py
+++ b/solution.py
@@ -50,6 +50,10 @@
     return ring
 
 
+def product(left, right):
+    return lax.dot_general(left, right, (((1,), (0,)), ((), ())), preferred_element_type=jnp.float32)
+
+
 sync = lax.optimization_barrier
 
 
@@ -70,7 +74,7 @@
     both = jnp.concatenate([scaled, part])
     both = sync(paired(both, 0, 0))
     both = both.reshape(2, 2, cols, tokens).transpose(1, 0, 2, 3)
-    both = sync(paired(both, 1, 2))
+    both, near, a = sync((paired(both, 1, 2), spread(a, "x"), a))
     both, a = sync((paired(both, 2, 3), a))
     far = permute(a, ("zh",), lambda h: (1 - h,))
 
@@ -82,23 +86,27 @@
     part = jnp.where(lax.axis_index("c") == 0, part, part[:, ::-1])
     part = jnp.where(lax.axis_index("zh") == 0, part, part[::-1])
     part = part.reshape(16 * cols, tokens)
-    rows_b, rows_a, part, a, far = sync((rows_b, rows_a, part, a, far))
+    rows_b, rows_a, part, near, far = sync((rows_b, rows_a, part, near, far))
 
     up = along_y(jnp.concatenate([rows_b[:half], part]), 1)
     down = along_y(jnp.concatenate([rows_a[half:], part]), -1)
-    acts = spread(jnp.stack([a, far]), "x")
-    up, down, acts = sync((up, down, acts))
+    far = spread(far, "x")
+    near_c = permute(near, ("c",), lambda c: (1 - c,))
+    three = ordered("y", [rows, rows_a, jnp.zeros_like(rows), rows_b]).reshape(64 * cols, tokens)
+    input_grads = product(weight_codes, three)
+    start = (lax.axis_index("y") + 2) % 4 * (16 * cols)
+    fourth = lax.dynamic_slice(weight_codes, (0, start), (weight_codes.shape[0], 16 * cols))
+    up, down, far, near_c, input_grads, fourth = sync((up, down, far, near_c, input_grads, fourth))
     rows_o = jnp.concatenate([up[:half], down[:half]])
     part_b, part_a = up[half:], down[half:]
 
     part_o = along_y(part_b[:half], 1), along_y(part_a[half:], -1)
-    acts_c = permute(acts, ("c",), lambda c: (1 - c,))
+    far_c = permute(far, ("c",), lambda c: (1 - c,))
 
-    rows = ordered("y", [rows, rows_a, rows_o, rows_b]).reshape(64 * cols, tokens)
-    input_grads = lax.dot_general(weight_codes, rows, (((1,), (0,)), ((), ())), preferred_element_type=jnp.float32)
+    input_grads += product(fourth, rows_o)
     weight_grads = 0.0
     for i in (0, 1):
-        mine = jnp.stack([acts[:, i], acts_c[:, i]], 1)
+        mine = jnp.stack([(near, far)[i], (near_c, far_c)[i]], 1)
         own, ahead, behind = (v[i * half : (i + 1) * half] for v in (part, part_a, part_b))
         blocks = ordered("y", [v.reshape(2, 4 * cols, tokens) for v in (own, ahead, part_o[i], behind)])
         weight_grads += lax.dot_general(

time: 174 us -> 187 us (1.075)
  the two profiles are of different devices: /device:TPU:1 before, /device:TPU:32 now
where the time goes in v10:
time: 187 us; the launch traced here: 186 us
  starting transfers between devices  89.4 us (48%)
  waiting for transfers between devices  67.6 us (36%)
  local copies, waits for them, and re-layouts  14.3 us (8%)
  matrix products  9.94 us (5%)
  other arithmetic  3.29 us (2%)
    ppermute x15, starting transfers between devices, permute(): return lax.ppermute(value, axes, pairs)  77.3 us
    ppermute x15, waiting for transfers between devices, permute(): return lax.ppermute(value, axes, pairs)  67.6 us
    all_to_all x2, starting transfers between devices, spread(): return lax.all_to_all(copies, axis, 0, 0, tiled=True)  12.1 us
    dot_general x2, matrix products, product(): lax.dot_general(left, right, (((1,), (0,)), ((), ())), preferred_element_...  5.59 us
    dot_general x2, matrix products, per_device(): lax.dot_general(mine, blocks, (((0, 1, 3), (0, 1, 3)), ((), ())), preferr...  4.35 us
  transfers between devices with their start and end apart: 17, of which 8 were waited for; matrix products, arithmetic and copies ran while one was open for 9% of the time, Pallas kernels for 0%

profile of v10, /device:TPU:32, one launch (start us, length us, event | category | flops | bytes accessed | tf_op | source)
XLA Modules:
  0.0 185.7 jit_solution(15941843268131373442)
XLA Ops:
  0.6 1.4 collective-permute-start
  2.0 1.7 broadcast_in_dim.18
  3.8 7.9 %all-to-all-start = ((bf16[4,464,128]{2,1,0:T(8,128)(2,1)}), bf16[4,464,128]{2,1,0:T(8,128)(2,1)S(1)}, u32[]{:S(2)}, u32[]{:S(2)}) async-start(bf16[4,464,128]{2,1,0:T(8,128)(2,1)} %broadcast_in_dim.18), calls=%async_computation | async-start | bytes 950272 | tf_op jit(solution)/shard_map/all_to_all | solution.py:31
  11.7 0.8 dynamic_slice.6
  12.5 0.8 multiply_convert_fusion
  13.3 0.0 collective-permute-done
  13.4 28.1 %collective-permute-start.1 = (bf16[232,128]{1,0:T(8,128)(2,1)S(1)}, bf16[232,128]{1,0:T(8,128)(2,1)S(1)}, u32[]{:S(2)}, u32[]{:S(2)}) collective-permute-start(bf16[232,128]{1,0:T(8,128)(2,1)S(1)} %pad_maximum_fusion.2), channel_id=1, source_target_pairs={{0,8},{1,9},{2,10},{3,11},{4,12},{5,13},{6,14},{7,15},{8,0},{9,1},... | collective-permute-start | bytes 178184 | tf_op jit(solution)/shard_map/ppermute | solution.py:21
  41.5 9.4 %collective-permute-done.1 = bf16[232,128]{1,0:T(8,128)(2,1)S(1)} collective-permute-done((bf16[232,128]{1,0:T(8,128)(2,1)S(1)}, bf16[232,128]{1,0:T(8,128)(2,1)S(1)}, u32[]{:S(2)}, u32[]{:S(2)}) %collective-permute-start.1) | collective-permute-done | bytes 59424 | tf_op jit(solution)/shard_map/ppermute | solution.py:21
  50.9 1.9 %collective-permute-start.2 = (bf16[2,2,116,128]{3,2,0,1:T(8,128)(2,1)S(1)}, bf16[2,2,116,128]{3,2,0,1:T(8,128)(2,1)S(1)}, u32[]{:S(2)}, u32[]{:S(2)}) collective-permute-start(bf16[2,2,116,128]{3,2,0,1:T(8,128)(2,1)S(1)} %bitcast.73), channel_id=1, source_target_pairs={{0,4},{1,5},{2,6},{3,7},{4,0},{5,1},{6,2},{7,3},{8,12},{9,13},{10,... | collective-permute-start | bytes 356360 | tf_op jit(solution)/shard_map/ppermute | solution.py:21
  52.9 12.2 %collective-permute-done.2 = bf16[2,2,116,128]{3,2,0,1:T(8,128)(2,1)S(1)} collective-permute-done((bf16[2,2,116,128]{3,2,0,1:T(8,128)(2,1)S(1)}, bf16[2,2,116,128]{3,2,0,1:T(8,128)(2,1)S(1)}, u32[]{:S(2)}, u32[]{:S(2)}) %collective-permute-start.2) | collective-permute-done | bytes 118816 | tf_op jit(solution)/shard_map/ppermute | solution.py:21
  65.1 0.0 all-to-all-done
  65.1 1.9 %collective-permute-start.3 = (bf16[2,2,2,116,128]{4,3,0,1,2:T(8,128)(2,1)S(1)}, bf16[2,2,2,116,128]{4,3,0,1,2:T(8,128)(2,1)S(1)}, u32[]{:S(2)}, u32[]{:S(2)}) collective-permute-start(bf16[2,2,2,116,128]{4,3,0,1,2:T(8,128)(2,1)S(1)} %maximum_select_fusion.3), channel_id=1, source_target_pairs={{0,2},{1,3},{2,0},{3,1},{4,6},{5,7},{6,4},{7,5},{8,10},{9,11},{10,... | collective-permute-start | bytes 712712 | tf_op jit(solution)/shard_map/ppermute | solution.py:21
  67.1 10.8 %collective-permute-done.3 = bf16[2,2,2,116,128]{4,3,0,1,2:T(8,128)(2,1)S(1)} collective-permute-done((bf16[2,2,2,116,128]{4,3,0,1,2:T(8,128)(2,1)S(1)}, bf16[2,2,2,116,128]{4,3,0,1,2:T(8,128)(2,1)S(1)}, u32[]{:S(2)}, u32[]{:S(2)}) %collective-permute-start.3) | collective-permute-done | bytes 237600 | tf_op jit(solution)/shard_map/ppermute | solution.py:21
  77.9 0.1 maximum_select_fusion
  78.0 0.1 slice_bitcast_fusion.2
  78.1 6.5 %collective-permute-start.4 = (bf16[2,2,2,116,128]{4,3,0,1,2:T(8,128)(2,1)S(1)}, bf16[2,2,2,116,128]{4,3,0,1,2:T(8,128)(2,1)S(1)}, u32[]{:S(2)}, u32[]{:S(2)}) collective-permute-start(bf16[2,2,2,116,128]{4,3,0,1,2:T(8,128)(2,1)S(1)} %get-tuple-element.49), channel_id=1, source_target_pairs={{0,1},{1,0},{2,3},{3,2},{4,5},{5,4},{6,7},{7,6},{8,9},{9,8},{10,11... | collective-permute-start | bytes 712712 | tf_op jit(solution)/shard_map/ppermute | solution.py:21
  84.6 6.1 %collective-permute-done.4 = bf16[2,2,2,116,128]{4,3,0,1,2:T(8,128)(2,1)S(1)} collective-permute-done((bf16[2,2,2,116,128]{4,3,0,1,2:T(8,128)(2,1)S(1)}, bf16[2,2,2,116,128]{4,3,0,1,2:T(8,128)(2,1)S(1)}, u32[]{:S(2)}, u32[]{:S(2)}) %collective-permute-start.4) | collective-permute-done | bytes 237600 | tf_op jit(solution)/shard_map/ppermute | solution.py:21
  90.7 0.1 maximum_select_fusion.1
  90.8 3.6 %collective-permute-start.7 = (bf16[2,2,2,116,128]{4,3,0,1,2:T(8,128)(2,1)S(1)}, bf16[2,2,2,116,128]{4,3,0,1,2:T(8,128)(2,1)S(1)}, u32[]{:S(2)}, u32[]{:S(2)}) collective-permute-start(bf16[2,2,2,116,128]{4,3,0,1,2:T(8,128)(2,1)S(1)} %slice_bitcast_fusion), channel_id=1, source_target_pairs={{0,1},{1,0},{2,3},{3,2},{4,5},{5,4},{6,7},{7,6},{8,9},{9,8},{10,11... | collective-permute-start | bytes 712712 | tf_op jit(solution)/shard_map/ppermute | solution.py:21
  94.4 2.4 %constant_dynamic-slice_fusion = bf16[464,1856]{1,0:T(8,128)(2,1)S(1)} fusion(bf16[464,7424]{1,0:T(8,128)(2,1)} %param.5, s32[]{:T(128)S(6)} %select_n.145), kind=kLoop, calls=%fused_computation.38 | loop fusion | bytes 3444740 | tf_op jit(solution)/shard_map/dynamic_slice | solution.py:98
  96.8 4.5 %collective-permute-start.8 = (bf16[464,128]{1,0:T(8,128)(2,1)}, bf16[464,128]{1,0:T(8,128)(2,1)}, u32[]{:S(2)}, u32[]{:S(2)}) collective-permute-start(bf16[464,128]{1,0:T(8,128)(2,1)} %bitcast.7), channel_id=1, source_target_pairs={{0,128},{128,0},{1,129},{129,1},{2,130},{130,2},{3,131},{131,3},{4... | collective-permute-start | bytes 356360 | tf_op jit(solution)/shard_map/ppermute | solution.py:21
  101.4 0.1 reshape.28
  101.5 5.5 %collective-permute-start.5 = (bf16[1856,128]{1,0:T(8,128)(2,1)S(1)}, bf16[1856,128]{1,0:T(8,128)(2,1)}, u32[]{:S(2)}, u32[]{:S(2)}) collective-permute-start(bf16[1856,128]{1,0:T(8,128)(2,1)S(1)} %reshape.28), channel_id=1, source_target_pairs={{0,16},{16,32},{32,48},{48,0},{1,17},{17,33},{33,49},{49,1},{2,18}... | collective-permute-start | bytes 1425416 | tf_op jit(solution)/shard_map/ppermute | solution.py:21
  107.0 5.9 %collective-permute-start.6 = (bf16[1856,128]{1,0:T(8,128)(2,1)S(1)}, bf16[1856,128]{1,0:T(8,128)(2,1)}, u32[]{:S(2)}, u32[]{:S(2)}) collective-permute-start(bf16[1856,128]{1,0:T(8,128)(2,1)S(1)} %reshape.28), channel_id=1, source_target_pairs={{0,48},{16,0},{32,16},{48,32},{1,49},{17,1},{33,17},{49,33},{2,50}... | collective-permute-start | bytes 1425416 | tf_op jit(solution)/shard_map/ppermute | solution.py:21
  112.9 5.0 %collective-permute-done.7 = bf16[2,2,2,116,128]{4,3,0,1,2:T(8,128)(2,1)S(1)} collective-permute-done((bf16[2,2,2,116,128]{4,3,0,1,2:T(8,128)(2,1)S(1)}, bf16[2,2,2,116,128]{4,3,0,1,2:T(8,128)(2,1)S(1)}, u32[]{:S(2)}, u32[]{:S(2)}) %collective-permute-start.7) | collective-permute-done | bytes 237600 | tf_op jit(solution)/shard_map/ppermute | solution.py:21
  117.9 0.1 maximum_select_fusion.2
  118.0 0.1 select_n.136
  118.1 0.1 reverse_select_fusion.1
  118.2 0.1 reverse_select_fusion
  118.3 19.9 %collective-permute-done.8 = bf16[464,128]{1,0:T(8,128)(2,1)} collective-permute-done((bf16[464,128]{1,0:T(8,128)(2,1)}, bf16[464,128]{1,0:T(8,128)(2,1)}, u32[]{:S(2)}, u32[]{:S(2)}) %collective-permute-start.8) | collective-permute-done | bytes 118816 | tf_op jit(solution)/shard_map/ppermute | solution.py:21
  138.2 0.0 collective-permute-done.5
  138.2 0.0 collective-permute-done.6
  138.2 1.0 slice.47
  139.1 1.0 slice.46
  140.1 1.2 pad_maximum_fusion
  141.3 3.2 %collective-permute-start.9 = (bf16[2784,128]{1,0:T(8,128)(2,1)}, bf16[2784,128]{1,0:T(8,128)(2,1)}, u32[]{:S(2)}, u32[]{:S(2)}) collective-permute-start(bf16[2784,128]{1,0:T(8,128)(2,1)} %get-tuple-element.53), channel_id=1, source_target_pairs={{0,16},{16,32},{32,48},{48,0},{1,17},{17,33},{33,49},{49,1},{2,18}... | collective-permute-start | bytes 2138120 | tf_op jit(solution)/shard_map/ppermute | solution.py:21
  144.5 3.9 %collective-permute-start.10 = (bf16[2784,128]{1,0:T(8,128)(2,1)}, bf16[2784,128]{1,0:T(8,128)(2,1)}, u32[]{:S(2)}, u32[]{:S(2)}) collective-permute-start(bf16[2784,128]{1,0:T(8,128)(2,1)} %get-tuple-element.52), channel_id=1, source_target_pairs={{0,48},{16,0},{32,16},{48,32},{1,49},{17,1},{33,17},{49,33},{2,50}... | collective-permute-start | bytes 2138120 | tf_op jit(solution)/shard_map/ppermute | solution.py:21
  148.4 1.7 broadcast_in_dim.19
  150.1 4.1 %all-to-all-start.1 = ((bf16[4,464,128]{2,1,0:T(8,128)(2,1)}), bf16[4,464,128]{2,1,0:T(8,128)(2,1)}, u32[]{:S(2)}, u32[]{:S(2)}) async-start(bf16[4,464,128]{2,1,0:T(8,128)(2,1)} %broadcast_in_dim.19), calls=%async_computation.1 | async-start | bytes 950272 | tf_op jit(solution)/shard_map/all_to_all | solution.py:31
  154.3 1.9 %collective-permute-start.11 = (bf16[4,464,128]{2,1,0:T(8,128)(2,1)S(1)}, bf16[4,464,128]{2,1,0:T(8,128)(2,1)}, u32[]{:S(2)}, u32[]{:S(2)}) collective-permute-start(bf16[4,464,128]{2,1,0:T(8,128)(2,1)S(1)} %copy-done.1), channel_id=1, source_target_pairs={{0,64},{64,0},{1,65},{65,1},{2,66},{66,2},{3,67},{67,3},{4,68},{68... | collective-permute-start | bytes 1425416 | tf_op jit(solution)/shard_map/ppermute | solution.py:21
  156.2 0.2 broadcast_in_dim.40
  156.5 1.1 bitcast_dynamic-update-slice_fusion.1
  157.6 0.1 broadcast_dynamic-update-slice_fusion
  157.7 1.1 bitcast_dynamic-update-slice_fusion
  158.8 4.9 %convolution_bitcast_fusion.2 = f32[464,128]{1,0:T(8,128)S(1)} fusion(bf16[464,7424]{1,0:T(8,128)(2,1)} %param.5, bf16[7424,128]{1,0:T(8,128)(2,1)S(1)} %bitcast.64), kind=kOutput, calls=%fused_computation.3 | convolution fusion | flops 881852416 | bytes 9027584 | tf_op jit(solution)/shard_map/dot_general | solution.py:54
  163.7 0.0 all-to-all-done.1
  163.7 0.0 collective-permute-done.11
  163.8 0.0 collective-permute-done.9
  163.8 0.6 collective-permute-done.10
  164.3 1.2 fusion.15
  165.5 1.2 fusion.14
  166.8 5.1 %collective-permute-start.14 = (bf16[928,128]{1,0:T(8,128)(2,1)S(1)}, bf16[928,128]{1,0:T(8,128)(2,1)S(1)}, u32[]{:S(2)}, u32[]{:S(2)}) collective-permute-start(bf16[928,128]{1,0:T(8,128)(2,1)S(1)} %get-tuple-element.46), channel_id=1, source_target_pairs={{0,48},{16,0},{32,16},{48,32},{1,49},{17,1},{33,17},{49,33},{2,50}... | collective-permute-start | bytes 712712 | tf_op jit(solution)/shard_map/ppermute | solution.py:21
  171.9 1.9 %collective-permute-start.12 = (bf16[928,128]{1,0:T(8,128)(2,1)S(1)}, bf16[928,128]{1,0:T(8,128)(2,1)S(1)}, u32[]{:S(2)}, u32[]{:S(2)}) collective-permute-start(bf16[928,128]{1,0:T(8,128)(2,1)S(1)} %get-tuple-element.42), channel_id=1, source_target_pairs={{0,16},{16,32},{32,48},{48,0},{1,17},{17,33},{33,49},{49,1},{2,18}... | collective-permute-start | bytes 712712 | tf_op jit(solution)/shard_map/ppermute | solution.py:21
  173.8 1.9 %collective-permute-start.13 = (bf16[4,464,128]{2,1,0:T(8,128)(2,1)}, bf16[4,464,128]{2,1,0:T(8,128)(2,1)S(1)}, u32[]{:S(2)}, u32[]{:S(2)}) collective-permute-start(bf16[4,464,128]{2,1,0:T(8,128)(2,1)} %all-to-all-done.1), channel_id=1, source_target_pairs={{0,64},{64,0},{1,65},{65,1},{2,66},{66,2},{3,67},{67,3},{4,68},{68... | collective-permute-start | bytes 1425416 | tf_op jit(solution)/shard_map/ppermute | solution.py:21
  175.7 0.7 fusion.7
  176.4 0.7 add_bitcast_fusion
  177.1 0.1 broadcast_in_dim.46
  177.3 0.1 broadcast_in_dim.44
  177.5 0.0 collective-permute-done.14
  177.5 3.7 %collective-permute-done.12 = bf16[928,128]{1,0:T(8,128)(2,1)S(1)} collective-permute-done((bf16[928,128]{1,0:T(8,128)(2,1)S(1)}, bf16[928,128]{1,0:T(8,128)(2,1)S(1)}, u32[]{:S(2)}, u32[]{:S(2)}) %collective-permute-start.12) | collective-permute-done | bytes 237600 | tf_op jit(solution)/shard_map/ppermute | solution.py:21
  181.2 0.1 constant_dynamic-update-slice_fusion.1
  181.4 0.0 collective-permute-done.13
  181.4 1.7 convolution_bitcast_fusion
  183.1 2.6 %fusion = f32[464,464]{1,0:T(8,128)} fusion(f32[464,464]{1,0:T(8,128)S(1)} %convolution_bitcast_fusion, bf16[4,2,464,128]{3,2,1,0:T(8,128)(2,1)S(1)} %constant_dynamic-update-slice_fusion.3, bf16[4,1,464,128]{3,2,1,0:T(8,128)(2,1)} %bitcast.24, bf16[4,1,464,128]{3,2,1,0:T(8,128)(2,1)S(1)} %bitcast.75), kind=kOutput, calls=%fused_computation.2 | convolution fusion | flops 441616640 | bytes 3622912 | tf_op jit(solution)/shard_map/dot_general | solution.py:112
  (17 shorter events, 0.4 us)
Async XLA Ops:
  0.6 12.7 %collective-permute-start = (bf16[116,128]{1,0:T(8,128)(2,1)}, bf16[116,128]{1,0:T(8,128)(2,1)S(1)}, u32[]{:S(2)}, u32[]{:S(2)}) collective-permute-start(bf16[116,128]{1,0:T(8,128)(2,1)} %bitcast.83), channel_id=1, source_target_pairs={{0,0},{1,1},{2,2},{3,3},{4,64},{5,65},{6,66},{7,67},{8,128},{9,129... | collective-permute-start | bytes 89096 | tf_op jit(solution)/shard_map/ppermute | solution.py:21
  3.8 61.3 %all-to-all-start = ((bf16[4,464,128]{2,1,0:T(8,128)(2,1)}), bf16[4,464,128]{2,1,0:T(8,128)(2,1)S(1)}, u32[]{:S(2)}, u32[]{:S(2)}) async-start(bf16[4,464,128]{2,1,0:T(8,128)(2,1)} %broadcast_in_dim.18), calls=%async_computation | async-start | bytes 950272 | tf_op jit(solution)/shard_map/all_to_all | solution.py:31
  13.4 37.5 %collective-permute-start.1 = (bf16[232,128]{1,0:T(8,128)(2,1)S(1)}, bf16[232,128]{1,0:T(8,128)(2,1)S(1)}, u32[]{:S(2)}, u32[]{:S(2)}) collective-permute-start(bf16[232,128]{1,0:T(8,128)(2,1)S(1)} %pad_maximum_fusion.2), channel_id=1, source_target_pairs={{0,8},{1,9},{2,10},{3,11},{4,12},{5,13},{6,14},{7,15},{8,0},{9,1},... | collective-permute-start | bytes 178184 | tf_op jit(solution)/shard_map/ppermute | solution.py:21
  50.9 14.1 %collective-permute-start.2 = (bf16[2,2,116,128]{3,2,0,1:T(8,128)(2,1)S(1)}, bf16[2,2,116,128]{3,2,0,1:T(8,128)(2,1)S(1)}, u32[]{:S(2)}, u32[]{:S(2)}) collective-permute-start(bf16[2,2,116,128]{3,2,0,1:T(8,128)(2,1)S(1)} %bitcast.73), channel_id=1, source_target_pairs={{0,4},{1,5},{2,6},{3,7},{4,0},{5,1},{6,2},{7,3},{8,12},{9,13},{10,... | collective-permute-start | bytes 356360 | tf_op jit(solution)/shard_map/ppermute | solution.py:21
  65.1 12.8 %copy-start = (bf16[4,464,128]{2,1,0:T(8,128)(2,1)}, bf16[4,464,128]{2,1,0:T(8,128)(2,1)S(1)}, u32[]{:S(2)}) copy-start(bf16[4,464,128]{2,1,0:T(8,128)(2,1)S(1)} %all-to-all-done) | copy-start | bytes 1425412
  65.1 12.8 %collective-permute-start.3 = (bf16[2,2,2,116,128]{4,3,0,1,2:T(8,128)(2,1)S(1)}, bf16[2,2,2,116,128]{4,3,0,1,2:T(8,128)(2,1)S(1)}, u32[]{:S(2)}, u32[]{:S(2)}) collective-permute-start(bf16[2,2,2,116,128]{4,3,0,1,2:T(8,128)(2,1)S(1)} %maximum_select_fusion.3), channel_id=1, source_target_pairs={{0,2},{1,3},{2,0},{3,1},{4,6},{5,7},{6,4},{7,5},{8,10},{9,11},{10,... | collective-permute-start | bytes 712712 | tf_op jit(solution)/shard_map/ppermute | solution.py:21
  78.1 12.6 %collective-permute-start.4 = (bf16[2,2,2,116,128]{4,3,0,1,2:T(8,128)(2,1)S(1)}, bf16[2,2,2,116,128]{4,3,0,1,2:T(8,128)(2,1)S(1)}, u32[]{:S(2)}, u32[]{:S(2)}) collective-permute-start(bf16[2,2,2,116,128]{4,3,0,1,2:T(8,128)(2,1)S(1)} %get-tuple-element.49), channel_id=1, source_target_pairs={{0,1},{1,0},{2,3},{3,2},{4,5},{5,4},{6,7},{7,6},{8,9},{9,8},{10,11... | collective-permute-start | bytes 712712 | tf_op jit(solution)/shard_map/ppermute | solution.py:21
  90.8 27.1 %collective-permute-start.7 = (bf16[2,2,2,116,128]{4,3,0,1,2:T(8,128)(2,1)S(1)}, bf16[2,2,2,116,128]{4,3,0,1,2:T(8,128)(2,1)S(1)}, u32[]{:S(2)}, u32[]{:S(2)}) collective-permute-start(bf16[2,2,2,116,128]{4,3,0,1,2:T(8,128)(2,1)S(1)} %slice_bitcast_fusion), channel_id=1, source_target_pairs={{0,1},{1,0},{2,3},{3,2},{4,5},{5,4},{6,7},{7,6},{8,9},{9,8},{10,11... | collective-permute-start | bytes 712712 | tf_op jit(solution)/shard_map/ppermute | solution.py:21
  96.8 41.4 %collective-permute-start.8 = (bf16[464,128]{1,0:T(8,128)(2,1)}, bf16[464,128]{1,0:T(8,128)(2,1)}, u32[]{:S(2)}, u32[]{:S(2)}) collective-permute-start(bf16[464,128]{1,0:T(8,128)(2,1)} %bitcast.7), channel_id=1, source_target_pairs={{0,128},{128,0},{1,129},{129,1},{2,130},{130,2},{3,131},{131,3},{4... | collective-permute-start | bytes 356360 | tf_op jit(solution)/shard_map/ppermute | solution.py:21
  101.5 36.7 %collective-permute-start.5 = (bf16[1856,128]{1,0:T(8,128)(2,1)S(1)}, bf16[1856,128]{1,0:T(8,128)(2,1)}, u32[]{:S(2)}, u32[]{:S(2)}) collective-permute-start(bf16[1856,128]{1,0:T(8,128)(2,1)S(1)} %reshape.28), channel_id=1, source_target_pairs={{0,16},{16,32},{32,48},{48,0},{1,17},{17,33},{33,49},{49,1},{2,18}... | collective-permute-start | bytes 1425416 | tf_op jit(solution)/shard_map/ppermute | solution.py:21
  107.0 31.2 %collective-permute-start.6 = (bf16[1856,128]{1,0:T(8,128)(2,1)S(1)}, bf16[1856,128]{1,0:T(8,128)(2,1)}, u32[]{:S(2)}, u32[]{:S(2)}) collective-permute-start(bf16[1856,128]{1,0:T(8,128)(2,1)S(1)} %reshape.28), channel_id=1, source_target_pairs={{0,48},{16,0},{32,16},{48,32},{1,49},{17,1},{33,17},{49,33},{2,50}... | collective-permute-start | bytes 1425416 | tf_op jit(solution)/shard_map/ppermute | solution.py:21
  140.1 14.2 %copy-start.1 = (bf16[4,464,128]{2,1,0:T(8,128)(2,1)S(1)}, bf16[4,464,128]{2,1,0:T(8,128)(2,1)}, u32[]{:S(2)}) copy-start(bf16[4,464,128]{2,1,0:T(8,128)(2,1)} %copy-done) | copy-start | bytes 1425412
  141.3 22.4 %collective-permute-start.9 = (bf16[2784,128]{1,0:T(8,128)(2,1)}, bf16[2784,128]{1,0:T(8,128)(2,1)}, u32[]{:S(2)}, u32[]{:S(2)}) collective-permute-start(bf16[2784,128]{1,0:T(8,128)(2,1)} %get-tuple-element.53), channel_id=1, source_target_pairs={{0,16},{16,32},{32,48},{48,0},{1,17},{17,33},{33,49},{49,1},{2,18}... | collective-permute-start | bytes 2138120 | tf_op jit(solution)/shard_map/ppermute | solution.py:21
  144.5 19.8 %collective-permute-start.10 = (bf16[2784,128]{1,0:T(8,128)(2,1)}, bf16[2784,128]{1,0:T(8,128)(2,1)}, u32[]{:S(2)}, u32[]{:S(2)}) collective-permute-start(bf16[2784,128]{1,0:T(8,128)(2,1)} %get-tuple-element.52), channel_id=1, source_target_pairs={{0,48},{16,0},{32,16},{48,32},{1,49},{17,1},{33,17},{49,33},{2,50}... | collective-permute-start | bytes 2138120 | tf_op jit(solution)/shard_map/ppermute | solution.py:21
  150.1 13.6 %all-to-all-start.1 = ((bf16[4,464,128]{2,1,0:T(8,128)(2,1)}), bf16[4,464,128]{2,1,0:T(8,128)(2,1)}, u32[]{:S(2)}, u32[]{:S(2)}) async-start(bf16[4,464,128]{2,1,0:T(8,128)(2,1)} %broadcast_in_dim.19), calls=%async_computation.1 | async-start | bytes 950272 | tf_op jit(solution)/shard_map/all_to_all | solution.py:31
  154.3 9.4 %collective-permute-start.11 = (bf16[4,464,128]{2,1,0:T(8,128)(2,1)S(1)}, bf16[4,464,128]{2,1,0:T(8,128)(2,1)}, u32[]{:S(2)}, u32[]{:S(2)}) collective-permute-start(bf16[4,464,128]{2,1,0:T(8,128)(2,1)S(1)} %copy-done.1), channel_id=1, source_target_pairs={{0,64},{64,0},{1,65},{65,1},{2,66},{66,2},{3,67},{67,3},{4,68},{68... | collective-permute-start | bytes 1425416 | tf_op jit(solution)/shard_map/ppermute | solution.py:21
  166.8 10.7 %collective-permute-start.14 = (bf16[928,128]{1,0:T(8,128)(2,1)S(1)}, bf16[928,128]{1,0:T(8,128)(2,1)S(1)}, u32[]{:S(2)}, u32[]{:S(2)}) collective-permute-start(bf16[928,128]{1,0:T(8,128)(2,1)S(1)} %get-tuple-element.46), channel_id=1, source_target_pairs={{0,48},{16,0},{32,16},{48,32},{1,49},{17,1},{33,17},{49,33},{2,50}... | collective-permute-start | bytes 712712 | tf_op jit(solution)/shard_map/ppermute | solution.py:21
  171.9 9.4 %collective-permute-start.12 = (bf16[928,128]{1,0:T(8,128)(2,1)S(1)}, bf16[928,128]{1,0:T(8,128)(2,1)S(1)}, u32[]{:S(2)}, u32[]{:S(2)}) collective-permute-start(bf16[928,128]{1,0:T(8,128)(2,1)S(1)} %get-tuple-element.42), channel_id=1, source_target_pairs={{0,16},{16,32},{32,48},{48,0},{1,17},{17,33},{33,49},{49,1},{2,18}... | collective-permute-start | bytes 712712 | tf_op jit(solution)/shard_map/ppermute | solution.py:21
  173.8 7.6 %collective-permute-start.13 = (bf16[4,464,128]{2,1,0:T(8,128)(2,1)}, bf16[4,464,128]{2,1,0:T(8,128)(2,1)S(1)}, u32[]{:S(2)}, u32[]{:S(2)}) collective-permute-start(bf16[4,464,128]{2,1,0:T(8,128)(2,1)} %all-to-all-done.1), channel_id=1, source_target_pairs={{0,64},{64,0},{1,65},{65,1},{2,66},{66,2},{3,67},{67,3},{4,68},{68... | collective-permute-start | bytes 1425416 | tf_op jit(solution)/shard_map/ppermute | solution.py:21

commit v11 on v9

--- a/solution.py
+++ b/solution.py
@@ -87,7 +87,7 @@
     up = along_y(jnp.concatenate([rows_b[:half], part]), 1)
     down = along_y(jnp.concatenate([rows_a[half:], part]), -1)
     acts = spread(jnp.stack([a, far]), "x")
-    up, down, acts = sync((up, down, acts))
+    up, down = sync((up, down))
     rows_o = jnp.concatenate([up[:half], down[:half]])
     part_b, part_a = up[half:], down[half:]
 

time: 174 us -> 175 us (level)
  the two profiles are of different devices: /device:TPU:1 before, /device:TPU:27 now
where the time goes in v11:
time: 175 us; the launch traced here: 174 us
  starting transfers between devices  108 us (62%)
  waiting for transfers between devices  44 us (25%)
  local copies, waits for them, and re-layouts  9.52 us (5%)
  matrix products  8.42 us (5%)
  other arithmetic  3.42 us (2%)
    ppermute x14, starting transfers between devices, permute(): return lax.ppermute(value, axes, pairs)  103 us
    ppermute x14, waiting for transfers between devices, permute(): return lax.ppermute(value, axes, pairs)  44 us
    dot_general x1, matrix products, per_device(): lax.dot_general(weight_codes, rows, (((1,), (0,)), ((), ())), preferred_e...  6.12 us
    all_to_all x1, starting transfers between devices, spread(): return lax.all_to_all(copies, axis, 0, 0, tiled=True)  4.52 us
  transfers between devices with their start and end apart: 15, of which 8 were waited for; matrix products, arithmetic and copies ran while one was open for 10% of the time, Pallas kernels for 0%

profile of v11, /device:TPU:27, one launch (start us, length us, event | category | flops | bytes accessed | tf_op | source)
XLA Modules:
  0.0 174.2 jit_solution(12699799606636195966)
XLA Ops:
  0.6 11.6 %collective-permute-start = (bf16[116,128]{1,0:T(8,128)(2,1)}, bf16[116,128]{1,0:T(8,128)(2,1)S(1)}, u32[]{:S(2)}, u32[]{:S(2)}) collective-permute-start(bf16[116,128]{1,0:T(8,128)(2,1)} %bitcast.75), channel_id=1, source_target_pairs={{0,0},{1,1},{2,2},{3,3},{4,64},{5,65},{6,66},{7,67},{8,128},{9,129... | collective-permute-start | bytes 89096 | tf_op jit(solution)/shard_map/ppermute | solution.py:21
  12.3 0.8 dynamic_slice.3
  13.0 0.8 multiply_convert_fusion
  13.9 0.9 collective-permute-done
  14.8 25.3 %collective-permute-start.1 = (bf16[232,128]{1,0:T(8,128)(2,1)S(1)}, bf16[232,128]{1,0:T(8,128)(2,1)S(1)}, u32[]{:S(2)}, u32[]{:S(2)}) collective-permute-start(bf16[232,128]{1,0:T(8,128)(2,1)S(1)} %pad_maximum_fusion.3), channel_id=1, source_target_pairs={{0,8},{1,9},{2,10},{3,11},{4,12},{5,13},{6,14},{7,15},{8,0},{9,1},... | collective-permute-start | bytes 178184 | tf_op jit(solution)/shard_map/ppermute | solution.py:21
  40.1 8.5 %collective-permute-done.1 = bf16[232,128]{1,0:T(8,128)(2,1)S(1)} collective-permute-done((bf16[232,128]{1,0:T(8,128)(2,1)S(1)}, bf16[232,128]{1,0:T(8,128)(2,1)S(1)}, u32[]{:S(2)}, u32[]{:S(2)}) %collective-permute-start.1) | collective-permute-done | bytes 59424 | tf_op jit(solution)/shard_map/ppermute | solution.py:21
  48.6 1.9 %collective-permute-start.2 = (bf16[2,2,116,128]{3,2,0,1:T(8,128)(2,1)S(1)}, bf16[2,2,116,128]{3,2,0,1:T(8,128)(2,1)S(1)}, u32[]{:S(2)}, u32[]{:S(2)}) collective-permute-start(bf16[2,2,116,128]{3,2,0,1:T(8,128)(2,1)S(1)} %bitcast.65), channel_id=1, source_target_pairs={{0,4},{1,5},{2,6},{3,7},{4,0},{5,1},{6,2},{7,3},{8,12},{9,13},{10,... | collective-permute-start | bytes 356360 | tf_op jit(solution)/shard_map/ppermute | solution.py:21
  50.5 10.2 %collective-permute-done.2 = bf16[2,2,116,128]{3,2,0,1:T(8,128)(2,1)S(1)} collective-permute-done((bf16[2,2,116,128]{3,2,0,1:T(8,128)(2,1)S(1)}, bf16[2,2,116,128]{3,2,0,1:T(8,128)(2,1)S(1)}, u32[]{:S(2)}, u32[]{:S(2)}) %collective-permute-start.2) | collective-permute-done | bytes 118816 | tf_op jit(solution)/shard_map/ppermute | solution.py:21
  60.8 0.0 copy-start
  60.8 2.1 %collective-permute-start.3 = (bf16[2,2,2,116,128]{4,3,0,1,2:T(8,128)(2,1)S(1)}, bf16[2,2,2,116,128]{4,3,0,1,2:T(8,128)(2,1)S(1)}, u32[]{:S(2)}, u32[]{:S(2)}) collective-permute-start(bf16[2,2,2,116,128]{4,3,0,1,2:T(8,128)(2,1)S(1)} %maximum_select_fusion.3), channel_id=1, source_target_pairs={{0,2},{1,3},{2,0},{3,1},{4,6},{5,7},{6,4},{7,5},{8,10},{9,11},{10,... | collective-permute-start | bytes 712712 | tf_op jit(solution)/shard_map/ppermute | solution.py:21
  62.9 9.0 %collective-permute-done.3 = bf16[2,2,2,116,128]{4,3,0,1,2:T(8,128)(2,1)S(1)} collective-permute-done((bf16[2,2,2,116,128]{4,3,0,1,2:T(8,128)(2,1)S(1)}, bf16[2,2,2,116,128]{4,3,0,1,2:T(8,128)(2,1)S(1)}, u32[]{:S(2)}, u32[]{:S(2)}) %collective-permute-start.3) | collective-permute-done | bytes 237600 | tf_op jit(solution)/shard_map/ppermute | solution.py:21
  71.9 0.1 maximum_select_fusion
  72.0 0.1 slice_bitcast_fusion.2
  72.1 1.9 %collective-permute-start.4 = (bf16[2,2,2,116,128]{4,3,0,1,2:T(8,128)(2,1)S(1)}, bf16[2,2,2,116,128]{4,3,0,1,2:T(8,128)(2,1)S(1)}, u32[]{:S(2)}, u32[]{:S(2)}) collective-permute-start(bf16[2,2,2,116,128]{4,3,0,1,2:T(8,128)(2,1)S(1)} %get-tuple-element.39), channel_id=1, source_target_pairs={{0,1},{1,0},{2,3},{3,2},{4,5},{5,4},{6,7},{7,6},{8,9},{9,8},{10,11... | collective-permute-start | bytes 712712 | tf_op jit(solution)/shard_map/ppermute | solution.py:21
  74.1 5.0 %collective-permute-done.4 = bf16[2,2,2,116,128]{4,3,0,1,2:T(8,128)(2,1)S(1)} collective-permute-done((bf16[2,2,2,116,128]{4,3,0,1,2:T(8,128)(2,1)S(1)}, bf16[2,2,2,116,128]{4,3,0,1,2:T(8,128)(2,1)S(1)}, u32[]{:S(2)}, u32[]{:S(2)}) %collective-permute-start.4) | collective-permute-done | bytes 237600 | tf_op jit(solution)/shard_map/ppermute | solution.py:21
  79.0 0.1 maximum_select_fusion.1
  79.1 1.9 %collective-permute-start.7 = (bf16[2,2,2,116,128]{4,3,0,1,2:T(8,128)(2,1)S(1)}, bf16[2,2,2,116,128]{4,3,0,1,2:T(8,128)(2,1)S(1)}, u32[]{:S(2)}, u32[]{:S(2)}) collective-permute-start(bf16[2,2,2,116,128]{4,3,0,1,2:T(8,128)(2,1)S(1)} %slice_bitcast_fusion), channel_id=1, source_target_pairs={{0,1},{1,0},{2,3},{3,2},{4,5},{5,4},{6,7},{7,6},{8,9},{9,8},{10,11... | collective-permute-start | bytes 712712 | tf_op jit(solution)/shard_map/ppermute | solution.py:21
  81.1 0.0 copy-done
  81.1 15.5 %collective-permute-start.8 = (bf16[464,128]{1,0:T(8,128)(2,1)S(1)}, bf16[464,128]{1,0:T(8,128)(2,1)S(1)}, u32[]{:S(2)}, u32[]{:S(2)}) collective-permute-start(bf16[464,128]{1,0:T(8,128)(2,1)S(1)} %bitcast.71), channel_id=1, source_target_pairs={{0,128},{128,0},{1,129},{129,1},{2,130},{130,2},{3,131},{131,3},{4... | collective-permute-start | bytes 356360 | tf_op jit(solution)/shard_map/ppermute | solution.py:21
  96.7 0.1 broadcast_in_dim.37
  96.8 1.9 %collective-permute-start.5 = (bf16[1856,128]{1,0:T(8,128)(2,1)S(1)}, bf16[1856,128]{1,0:T(8,128)(2,1)S(1)}, u32[]{:S(2)}, u32[]{:S(2)}) collective-permute-start(bf16[1856,128]{1,0:T(8,128)(2,1)S(1)} %broadcast_in_dim.37), channel_id=1, source_target_pairs={{0,16},{16,32},{32,48},{48,0},{1,17},{17,33},{33,49},{49,1},{2,18}... | collective-permute-start | bytes 1425416 | tf_op jit(solution)/shard_map/ppermute | solution.py:21
  98.7 3.4 %collective-permute-start.6 = (bf16[1856,128]{1,0:T(8,128)(2,1)S(1)}, bf16[1856,128]{1,0:T(8,128)(2,1)S(1)}, u32[]{:S(2)}, u32[]{:S(2)}) collective-permute-start(bf16[1856,128]{1,0:T(8,128)(2,1)S(1)} %broadcast_in_dim.37), channel_id=1, source_target_pairs={{0,48},{16,0},{32,16},{48,32},{1,49},{17,1},{33,17},{49,33},{2,50}... | collective-permute-start | bytes 1425416 | tf_op jit(solution)/shard_map/ppermute | solution.py:21
  102.1 0.0 collective-permute-done.7
  102.1 0.1 maximum_select_fusion.2
  102.2 0.1 select_n.131
  102.3 0.1 reverse_select_fusion.1
  102.4 0.1 reverse_select_fusion
  102.5 4.0 %collective-permute-done.8 = bf16[464,128]{1,0:T(8,128)(2,1)S(1)} collective-permute-done((bf16[464,128]{1,0:T(8,128)(2,1)S(1)}, bf16[464,128]{1,0:T(8,128)(2,1)S(1)}, u32[]{:S(2)}, u32[]{:S(2)}) %collective-permute-start.8) | collective-permute-done | bytes 118816 | tf_op jit(solution)/shard_map/ppermute | solution.py:21
  106.5 0.0 collective-permute-done.5
  106.5 2.8 %collective-permute-done.6 = bf16[1856,128]{1,0:T(8,128)(2,1)S(1)} collective-permute-done((bf16[1856,128]{1,0:T(8,128)(2,1)S(1)}, bf16[1856,128]{1,0:T(8,128)(2,1)S(1)}, u32[]{:S(2)}, u32[]{:S(2)}) %collective-permute-start.6) | collective-permute-done | bytes 475168 | tf_op jit(solution)/shard_map/ppermute | solution.py:21
  109.4 1.2 pad_maximum_fusion
  110.6 7.9 %collective-permute-start.9 = (bf16[2784,128]{1,0:T(8,128)(2,1)}, bf16[2784,128]{1,0:T(8,128)(2,1)}, u32[]{:S(2)}, u32[]{:S(2)}) collective-permute-start(bf16[2784,128]{1,0:T(8,128)(2,1)} %get-tuple-element.43), channel_id=1, source_target_pairs={{0,16},{16,32},{32,48},{48,0},{1,17},{17,33},{33,49},{49,1},{2,18}... | collective-permute-start | bytes 2138120 | tf_op jit(solution)/shard_map/ppermute | solution.py:21
  118.5 1.9 %collective-permute-start.10 = (bf16[2784,128]{1,0:T(8,128)(2,1)}, bf16[2784,128]{1,0:T(8,128)(2,1)}, u32[]{:S(2)}, u32[]{:S(2)}) collective-permute-start(bf16[2784,128]{1,0:T(8,128)(2,1)} %get-tuple-element.42), channel_id=1, source_target_pairs={{0,48},{16,0},{32,16},{48,32},{1,49},{17,1},{33,17},{49,33},{2,50}... | collective-permute-start | bytes 2138120 | tf_op jit(solution)/shard_map/ppermute | solution.py:21
  120.5 1.1 broadcast_in_dim.42
  121.5 4.5 %all-to-all-start = ((bf16[4,2,464,128]{3,2,1,0:T(8,128)(2,1)}), bf16[4,2,464,128]{3,2,1,0:T(8,128)(2,1)S(1)}, u32[]{:S(2)}, u32[]{:S(2)}) async-start(bf16[4,2,464,128]{3,2,1,0:T(8,128)(2,1)} %broadcast_in_dim.42), calls=%async_computation | async-start | bytes 1900544 | tf_op jit(solution)/shard_map/all_to_all | solution.py:31
  126.1 1.5 broadcast_in_dim.38
  127.6 0.8 bitcast_dynamic-update-slice_fusion.1
  128.4 0.0 collective-permute-done.9
  128.4 3.6 %collective-permute-done.10 = bf16[2784,128]{1,0:T(8,128)(2,1)} collective-permute-done((bf16[2784,128]{1,0:T(8,128)(2,1)}, bf16[2784,128]{1,0:T(8,128)(2,1)}, u32[]{:S(2)}, u32[]{:S(2)}) %collective-permute-start.10) | collective-permute-done | bytes 712736 | tf_op jit(solution)/shard_map/ppermute | solution.py:21
  132.0 1.2 fusion.13
  133.2 1.2 fusion.12
  134.4 1.9 %collective-permute-start.13 = (bf16[928,128]{1,0:T(8,128)(2,1)S(1)}, bf16[928,128]{1,0:T(8,128)(2,1)}, u32[]{:S(2)}, u32[]{:S(2)}) collective-permute-start(bf16[928,128]{1,0:T(8,128)(2,1)S(1)} %get-tuple-element.36), channel_id=1, source_target_pairs={{0,48},{16,0},{32,16},{48,32},{1,49},{17,1},{33,17},{49,33},{2,50}... | collective-permute-start | bytes 712712 | tf_op jit(solution)/shard_map/ppermute | solution.py:21
  136.3 4.6 %collective-permute-start.12 = (bf16[928,128]{1,0:T(8,128)(2,1)S(1)}, bf16[928,128]{1,0:T(8,128)(2,1)}, u32[]{:S(2)}, u32[]{:S(2)}) collective-permute-start(bf16[928,128]{1,0:T(8,128)(2,1)S(1)} %get-tuple-element.32), channel_id=1, source_target_pairs={{0,16},{16,32},{32,48},{48,0},{1,17},{17,33},{33,49},{49,1},{2,18}... | collective-permute-start | bytes 712712 | tf_op jit(solution)/shard_map/ppermute | solution.py:21
  140.9 0.8 fusion.7
  141.7 0.8 bitcast_dynamic-update-slice_fusion
  142.6 0.0 all-to-all-done
  142.6 21.4 %collective-permute-start.11 = (bf16[4,2,464,128]{3,2,1,0:T(8,128)(2,1)S(1)}, bf16[4,2,464,128]{3,2,1,0:T(8,128)(2,1)S(1)}, u32[]{:S(2)}, u32[]{:S(2)}) collective-permute-start(bf16[4,2,464,128]{3,2,1,0:T(8,128)(2,1)S(1)} %all-to-all-done), channel_id=1, source_target_pairs={{0,64},{64,0},{1,65},{65,1},{2,66},{66,2},{3,67},{67,3},{4,68},{68... | collective-permute-start | bytes 2850824 | tf_op jit(solution)/shard_map/ppermute | solution.py:21
  164.0 6.1 %fusion.15 = f32[128,464]{0,1:T(8,128)} fusion(bf16[464,7424]{1,0:T(8,128)(2,1)} %param.5, bf16[7424,128]{1,0:T(8,128)(2,1)} %bitcast.20), kind=kOutput, calls=%fused_computation.41 | convolution fusion | flops 881852416 | bytes 9027584 | tf_op jit(solution)/shard_map/dot_general | solution.py:98
  170.1 0.1 broadcast_in_dim.46
  170.3 0.1 broadcast_in_dim.44
  170.5 0.1 fusion.10
  170.5 0.0 collective-permute-done.13
  170.5 0.0 collective-permute-done.12
  170.6 1.1 constant_dynamic-update-slice_fusion.1
  171.8 0.0 collective-permute-done.11
  171.8 0.1 fusion.11
  171.9 0.7 convolution_bitcast_fusion
  172.5 1.6 fusion
  (16 shorter events, 0.4 us)
Async XLA Ops:
  0.6 14.1 %collective-permute-start = (bf16[116,128]{1,0:T(8,128)(2,1)}, bf16[116,128]{1,0:T(8,128)(2,1)S(1)}, u32[]{:S(2)}, u32[]{:S(2)}) collective-permute-start(bf16[116,128]{1,0:T(8,128)(2,1)} %bitcast.75), channel_id=1, source_target_pairs={{0,0},{1,1},{2,2},{3,3},{4,64},{5,65},{6,66},{7,67},{8,128},{9,129... | collective-permute-start | bytes 89096 | tf_op jit(solution)/shard_map/ppermute | solution.py:21
  14.8 33.8 %collective-permute-start.1 = (bf16[232,128]{1,0:T(8,128)(2,1)S(1)}, bf16[232,128]{1,0:T(8,128)(2,1)S(1)}, u32[]{:S(2)}, u32[]{:S(2)}) collective-permute-start(bf16[232,128]{1,0:T(8,128)(2,1)S(1)} %pad_maximum_fusion.3), channel_id=1, source_target_pairs={{0,8},{1,9},{2,10},{3,11},{4,12},{5,13},{6,14},{7,15},{8,0},{9,1},... | collective-permute-start | bytes 178184 | tf_op jit(solution)/shard_map/ppermute | solution.py:21
  48.6 12.2 %collective-permute-start.2 = (bf16[2,2,116,128]{3,2,0,1:T(8,128)(2,1)S(1)}, bf16[2,2,116,128]{3,2,0,1:T(8,128)(2,1)S(1)}, u32[]{:S(2)}, u32[]{:S(2)}) collective-permute-start(bf16[2,2,116,128]{3,2,0,1:T(8,128)(2,1)S(1)} %bitcast.65), channel_id=1, source_target_pairs={{0,4},{1,5},{2,6},{3,7},{4,0},{5,1},{6,2},{7,3},{8,12},{9,13},{10,... | collective-permute-start | bytes 356360 | tf_op jit(solution)/shard_map/ppermute | solution.py:21
  60.8 20.3 %copy-start = (bf16[128,464]{0,1:T(8,128)(2,1)S(1)}, bf16[128,464]{0,1:T(8,128)(2,1)}, u32[]{:S(2)}) copy-start(bf16[128,464]{0,1:T(8,128)(2,1)} %param.4) | copy-start | bytes 356356
  60.8 11.1 %collective-permute-start.3 = (bf16[2,2,2,116,128]{4,3,0,1,2:T(8,128)(2,1)S(1)}, bf16[2,2,2,116,128]{4,3,0,1,2:T(8,128)(2,1)S(1)}, u32[]{:S(2)}, u32[]{:S(2)}) collective-permute-start(bf16[2,2,2,116,128]{4,3,0,1,2:T(8,128)(2,1)S(1)} %maximum_select_fusion.3), channel_id=1, source_target_pairs={{0,2},{1,3},{2,0},{3,1},{4,6},{5,7},{6,4},{7,5},{8,10},{9,11},{10,... | collective-permute-start | bytes 712712 | tf_op jit(solution)/shard_map/ppermute | solution.py:21
  72.1 6.9 %collective-permute-start.4 = (bf16[2,2,2,116,128]{4,3,0,1,2:T(8,128)(2,1)S(1)}, bf16[2,2,2,116,128]{4,3,0,1,2:T(8,128)(2,1)S(1)}, u32[]{:S(2)}, u32[]{:S(2)}) collective-permute-start(bf16[2,2,2,116,128]{4,3,0,1,2:T(8,128)(2,1)S(1)} %get-tuple-element.39), channel_id=1, source_target_pairs={{0,1},{1,0},{2,3},{3,2},{4,5},{5,4},{6,7},{7,6},{8,9},{9,8},{10,11... | collective-permute-start | bytes 712712 | tf_op jit(solution)/shard_map/ppermute | solution.py:21
  79.1 23.0 %collective-permute-start.7 = (bf16[2,2,2,116,128]{4,3,0,1,2:T(8,128)(2,1)S(1)}, bf16[2,2,2,116,128]{4,3,0,1,2:T(8,128)(2,1)S(1)}, u32[]{:S(2)}, u32[]{:S(2)}) collective-permute-start(bf16[2,2,2,116,128]{4,3,0,1,2:T(8,128)(2,1)S(1)} %slice_bitcast_fusion), channel_id=1, source_target_pairs={{0,1},{1,0},{2,3},{3,2},{4,5},{5,4},{6,7},{7,6},{8,9},{9,8},{10,11... | collective-permute-start | bytes 712712 | tf_op jit(solution)/shard_map/ppermute | solution.py:21
  81.1 25.4 %collective-permute-start.8 = (bf16[464,128]{1,0:T(8,128)(2,1)S(1)}, bf16[464,128]{1,0:T(8,128)(2,1)S(1)}, u32[]{:S(2)}, u32[]{:S(2)}) collective-permute-start(bf16[464,128]{1,0:T(8,128)(2,1)S(1)} %bitcast.71), channel_id=1, source_target_pairs={{0,128},{128,0},{1,129},{129,1},{2,130},{130,2},{3,131},{131,3},{4... | collective-permute-start | bytes 356360 | tf_op jit(solution)/shard_map/ppermute | solution.py:21
  96.8 9.7 %collective-permute-start.5 = (bf16[1856,128]{1,0:T(8,128)(2,1)S(1)}, bf16[1856,128]{1,0:T(8,128)(2,1)S(1)}, u32[]{:S(2)}, u32[]{:S(2)}) collective-permute-start(bf16[1856,128]{1,0:T(8,128)(2,1)S(1)} %broadcast_in_dim.37), channel_id=1, source_target_pairs={{0,16},{16,32},{32,48},{48,0},{1,17},{17,33},{33,49},{49,1},{2,18}... | collective-permute-start | bytes 1425416 | tf_op jit(solution)/shard_map/ppermute | solution.py:21
  98.7 10.6 %collective-permute-start.6 = (bf16[1856,128]{1,0:T(8,128)(2,1)S(1)}, bf16[1856,128]{1,0:T(8,128)(2,1)S(1)}, u32[]{:S(2)}, u32[]{:S(2)}) collective-permute-start(bf16[1856,128]{1,0:T(8,128)(2,1)S(1)} %broadcast_in_dim.37), channel_id=1, source_target_pairs={{0,48},{16,0},{32,16},{48,32},{1,49},{17,1},{33,17},{49,33},{2,50}... | collective-permute-start | bytes 1425416 | tf_op jit(solution)/shard_map/ppermute | solution.py:21
  110.6 17.8 %collective-permute-start.9 = (bf16[2784,128]{1,0:T(8,128)(2,1)}, bf16[2784,128]{1,0:T(8,128)(2,1)}, u32[]{:S(2)}, u32[]{:S(2)}) collective-permute-start(bf16[2784,128]{1,0:T(8,128)(2,1)} %get-tuple-element.43), channel_id=1, source_target_pairs={{0,16},{16,32},{32,48},{48,0},{1,17},{17,33},{33,49},{49,1},{2,18}... | collective-permute-start | bytes 2138120 | tf_op jit(solution)/shard_map/ppermute | solution.py:21
  118.5 13.5 %collective-permute-start.10 = (bf16[2784,128]{1,0:T(8,128)(2,1)}, bf16[2784,128]{1,0:T(8,128)(2,1)}, u32[]{:S(2)}, u32[]{:S(2)}) collective-permute-start(bf16[2784,128]{1,0:T(8,128)(2,1)} %get-tuple-element.42), channel_id=1, source_target_pairs={{0,48},{16,0},{32,16},{48,32},{1,49},{17,1},{33,17},{49,33},{2,50}... | collective-permute-start | bytes 2138120 | tf_op jit(solution)/shard_map/ppermute | solution.py:21
  121.5 21.1 %all-to-all-start = ((bf16[4,2,464,128]{3,2,1,0:T(8,128)(2,1)}), bf16[4,2,464,128]{3,2,1,0:T(8,128)(2,1)S(1)}, u32[]{:S(2)}, u32[]{:S(2)}) async-start(bf16[4,2,464,128]{3,2,1,0:T(8,128)(2,1)} %broadcast_in_dim.42), calls=%async_computation | async-start | bytes 1900544 | tf_op jit(solution)/shard_map/all_to_all | solution.py:31
  134.4 36.1 %collective-permute-start.13 = (bf16[928,128]{1,0:T(8,128)(2,1)S(1)}, bf16[928,128]{1,0:T(8,128)(2,1)}, u32[]{:S(2)}, u32[]{:S(2)}) collective-permute-start(bf16[928,128]{1,0:T(8,128)(2,1)S(1)} %get-tuple-element.36), channel_id=1, source_target_pairs={{0,48},{16,0},{32,16},{48,32},{1,49},{17,1},{33,17},{49,33},{2,50}... | collective-permute-start | bytes 712712 | tf_op jit(solution)/shard_map/ppermute | solution.py:21
  136.3 34.2 %collective-permute-start.12 = (bf16[928,128]{1,0:T(8,128)(2,1)S(1)}, bf16[928,128]{1,0:T(8,128)(2,1)}, u32[]{:S(2)}, u32[]{:S(2)}) collective-permute-start(bf16[928,128]{1,0:T(8,128)(2,1)S(1)} %get-tuple-element.32), channel_id=1, source_target_pairs={{0,16},{16,32},{32,48},{48,0},{1,17},{17,33},{33,49},{49,1},{2,18}... | collective-permute-start | bytes 712712 | tf_op jit(solution)/shard_map/ppermute | solution.py:21
  142.6 29.2 %collective-permute-start.11 = (bf16[4,2,464,128]{3,2,1,0:T(8,128)(2,1)S(1)}, bf16[4,2,464,128]{3,2,1,0:T(8,128)(2,1)S(1)}, u32[]{:S(2)}, u32[]{:S(2)}) collective-permute-start(bf16[4,2,464,128]{3,2,1,0:T(8,128)(2,1)S(1)} %all-to-all-done), channel_id=1, source_target_pairs={{0,64},{64,0},{1,65},{65,1},{2,66},{66,2},{3,67},{67,3},{4,68},{68... | collective-permute-start | bytes 2850824 | tf_op jit(solution)/shard_map/ppermute | solution.py:21

commit v12 on v11

--- a/solution.py
+++ b/solution.py
@@ -82,7 +82,8 @@
     part = jnp.where(lax.axis_index("c") == 0, part, part[:, ::-1])
     part = jnp.where(lax.axis_index("zh") == 0, part, part[::-1])
     part = part.reshape(16 * cols, tokens)
-    rows_b, rows_a, part, a, far = sync((rows_b, rows_a, part, a, far))
+    rows_b, rows_a, part, a = sync((rows_b, rows_a, part, a))
+    far, kept = sync((far, part))
 
     up = along_y(jnp.concatenate([rows_b[:half], part]), 1)
     down = along_y(jnp.concatenate([rows_a[half:], part]), -1)
@@ -99,7 +100,7 @@
     weight_grads = 0.0
     for i in (0, 1):
         mine = jnp.stack([acts[:, i], acts_c[:, i]], 1)
-        own, ahead, behind = (v[i * half : (i + 1) * half] for v in (part, part_a, part_b))
+        own, ahead, behind = (v[i * half : (i + 1) * half] for v in (kept, part_a, part_b))
         blocks = ordered("y", [v.reshape(2, 4 * cols, tokens) for v in (own, ahead, part_o[i], behind)])
         weight_grads += lax.dot_general(
             mine, blocks, (((0, 1, 3), (0, 1, 3)), ((), ())), preferred_element_type=jnp.float32

time: 175 us -> 165 us (0.943)
  the two profiles are of different devices: /device:TPU:27 before, /device:TPU:1 now
where the time goes in v12:
time: 165 us; the launch traced here: 163 us
  starting transfers between devices  96.3 us (58%)
  waiting for transfers between devices  44.4 us (27%)
  local copies, waits for them, and re-layouts  9.5 us (6%)
  matrix products  8.41 us (5%)
  other arithmetic  3.44 us (2%)
    ppermute x14, starting transfers between devices, permute(): return lax.ppermute(value, axes, pairs)  92 us
    ppermute x14, waiting for transfers between devices, permute(): return lax.ppermute(value, axes, pairs)  44.4 us
    dot_general x1, matrix products, per_device(): lax.dot_general(weight_codes, rows, (((1,), (0,)), ((), ())), preferred_e...  6.12 us
    all_to_all x1, starting transfers between devices, spread(): return lax.all_to_all(copies, axis, 0, 0, tiled=True)  4.28 us
  transfers between devices with their start and end apart: 15, of which 8 were waited for; matrix products, arithmetic and copies ran while one was open for 11% of the time, Pallas kernels for 0%

profile of v12, /device:TPU:1, one launch (start us, length us, event | category | flops | bytes accessed | tf_op | source)
XLA Modules:
  0.0 163.2 jit_solution(15536621200988520220)
XLA Ops:
  0.6 10.2 %collective-permute-start = (bf16[116,128]{1,0:T(8,128)(2,1)}, bf16[116,128]{1,0:T(8,128)(2,1)S(1)}, u32[]{:S(2)}, u32[]{:S(2)}) collective-permute-start(bf16[116,128]{1,0:T(8,128)(2,1)} %bitcast.75), channel_id=1, source_target_pairs={{0,0},{1,1},{2,2},{3,3},{4,64},{5,65},{6,66},{7,67},{8,128},{9,129... | collective-permute-start | bytes 89096 | tf_op jit(solution)/shard_map/ppermute | solution.py:21
  10.9 0.8 dynamic_slice.3
  11.6 0.8 multiply_convert_fusion
  12.5 0.1 collective-permute-done
  12.6 23.9 %collective-permute-start.1 = (bf16[232,128]{1,0:T(8,128)(2,1)S(1)}, bf16[232,128]{1,0:T(8,128)(2,1)S(1)}, u32[]{:S(2)}, u32[]{:S(2)}) collective-permute-start(bf16[232,128]{1,0:T(8,128)(2,1)S(1)} %pad_maximum_fusion.3), channel_id=1, source_target_pairs={{0,8},{1,9},{2,10},{3,11},{4,12},{5,13},{6,14},{7,15},{8,0},{9,1},... | collective-permute-start | bytes 178184 | tf_op jit(solution)/shard_map/ppermute | solution.py:21
  36.6 9.7 %collective-permute-done.1 = bf16[232,128]{1,0:T(8,128)(2,1)S(1)} collective-permute-done((bf16[232,128]{1,0:T(8,128)(2,1)S(1)}, bf16[232,128]{1,0:T(8,128)(2,1)S(1)}, u32[]{:S(2)}, u32[]{:S(2)}) %collective-permute-start.1) | collective-permute-done | bytes 59424 | tf_op jit(solution)/shard_map/ppermute | solution.py:21
  46.3 1.9 %collective-permute-start.2 = (bf16[2,2,116,128]{3,2,0,1:T(8,128)(2,1)S(1)}, bf16[2,2,116,128]{3,2,0,1:T(8,128)(2,1)S(1)}, u32[]{:S(2)}, u32[]{:S(2)}) collective-permute-start(bf16[2,2,116,128]{3,2,0,1:T(8,128)(2,1)S(1)} %bitcast.65), channel_id=1, source_target_pairs={{0,4},{1,5},{2,6},{3,7},{4,0},{5,1},{6,2},{7,3},{8,12},{9,13},{10,... | collective-permute-start | bytes 356360 | tf_op jit(solution)/shard_map/ppermute | solution.py:21
  48.2 12.8 %collective-permute-done.2 = bf16[2,2,116,128]{3,2,0,1:T(8,128)(2,1)S(1)} collective-permute-done((bf16[2,2,116,128]{3,2,0,1:T(8,128)(2,1)S(1)}, bf16[2,2,116,128]{3,2,0,1:T(8,128)(2,1)S(1)}, u32[]{:S(2)}, u32[]{:S(2)}) %collective-permute-start.2) | collective-permute-done | bytes 118816 | tf_op jit(solution)/shard_map/ppermute | solution.py:21
  61.0 0.0 copy-start
  61.0 2.1 %collective-permute-start.3 = (bf16[2,2,2,116,128]{4,3,0,1,2:T(8,128)(2,1)S(1)}, bf16[2,2,2,116,128]{4,3,0,1,2:T(8,128)(2,1)S(1)}, u32[]{:S(2)}, u32[]{:S(2)}) collective-permute-start(bf16[2,2,2,116,128]{4,3,0,1,2:T(8,128)(2,1)S(1)} %maximum_select_fusion.3), channel_id=1, source_target_pairs={{0,2},{1,3},{2,0},{3,1},{4,6},{5,7},{6,4},{7,5},{8,10},{9,11},{10,... | collective-permute-start | bytes 712712 | tf_op jit(solution)/shard_map/ppermute | solution.py:21
  63.1 7.8 %collective-permute-done.3 = bf16[2,2,2,116,128]{4,3,0,1,2:T(8,128)(2,1)S(1)} collective-permute-done((bf16[2,2,2,116,128]{4,3,0,1,2:T(8,128)(2,1)S(1)}, bf16[2,2,2,116,128]{4,3,0,1,2:T(8,128)(2,1)S(1)}, u32[]{:S(2)}, u32[]{:S(2)}) %collective-permute-start.3) | collective-permute-done | bytes 237600 | tf_op jit(solution)/shard_map/ppermute | solution.py:21
  70.9 0.1 maximum_select_fusion
  71.0 0.1 slice_bitcast_fusion.2
  71.1 1.9 %collective-permute-start.4 = (bf16[2,2,2,116,128]{4,3,0,1,2:T(8,128)(2,1)S(1)}, bf16[2,2,2,116,128]{4,3,0,1,2:T(8,128)(2,1)S(1)}, u32[]{:S(2)}, u32[]{:S(2)}) collective-permute-start(bf16[2,2,2,116,128]{4,3,0,1,2:T(8,128)(2,1)S(1)} %get-tuple-element.41), channel_id=1, source_target_pairs={{0,1},{1,0},{2,3},{3,2},{4,5},{5,4},{6,7},{7,6},{8,9},{9,8},{10,11... | collective-permute-start | bytes 712712 | tf_op jit(solution)/shard_map/ppermute | solution.py:21
  73.0 5.9 %collective-permute-done.4 = bf16[2,2,2,116,128]{4,3,0,1,2:T(8,128)(2,1)S(1)} collective-permute-done((bf16[2,2,2,116,128]{4,3,0,1,2:T(8,128)(2,1)S(1)}, bf16[2,2,2,116,128]{4,3,0,1,2:T(8,128)(2,1)S(1)}, u32[]{:S(2)}, u32[]{:S(2)}) %collective-permute-start.4) | collective-permute-done | bytes 237600 | tf_op jit(solution)/shard_map/ppermute | solution.py:21
  79.0 0.1 maximum_select_fusion.1
  79.0 2.2 %collective-permute-start.7 = (bf16[2,2,2,116,128]{4,3,0,1,2:T(8,128)(2,1)S(1)}, bf16[2,2,2,116,128]{4,3,0,1,2:T(8,128)(2,1)S(1)}, u32[]{:S(2)}, u32[]{:S(2)}) collective-permute-start(bf16[2,2,2,116,128]{4,3,0,1,2:T(8,128)(2,1)S(1)} %slice_bitcast_fusion), channel_id=1, source_target_pairs={{0,1},{1,0},{2,3},{3,2},{4,5},{5,4},{6,7},{7,6},{8,9},{9,8},{10,11... | collective-permute-start | bytes 712712 | tf_op jit(solution)/shard_map/ppermute | solution.py:21
  81.3 0.0 copy-done
  81.3 11.4 %collective-permute-start.10 = (bf16[464,128]{1,0:T(8,128)(2,1)S(1)}, bf16[464,128]{1,0:T(8,128)(2,1)S(1)}, u32[]{:S(2)}, u32[]{:S(2)}) collective-permute-start(bf16[464,128]{1,0:T(8,128)(2,1)S(1)} %bitcast.71), channel_id=1, source_target_pairs={{0,128},{128,0},{1,129},{129,1},{2,130},{130,2},{3,131},{131,3},{4... | collective-permute-start | bytes 356360 | tf_op jit(solution)/shard_map/ppermute | solution.py:21
  92.8 0.1 broadcast_in_dim.37
  92.9 5.0 %collective-permute-start.5 = (bf16[1856,128]{1,0:T(8,128)(2,1)S(1)}, bf16[1856,128]{1,0:T(8,128)(2,1)S(1)}, u32[]{:S(2)}, u32[]{:S(2)}) collective-permute-start(bf16[1856,128]{1,0:T(8,128)(2,1)S(1)} %broadcast_in_dim.37), channel_id=1, source_target_pairs={{0,16},{16,32},{32,48},{48,0},{1,17},{17,33},{33,49},{49,1},{2,18}... | collective-permute-start | bytes 1425416 | tf_op jit(solution)/shard_map/ppermute | solution.py:21
  97.9 5.6 %collective-permute-start.6 = (bf16[1856,128]{1,0:T(8,128)(2,1)S(1)}, bf16[1856,128]{1,0:T(8,128)(2,1)S(1)}, u32[]{:S(2)}, u32[]{:S(2)}) collective-permute-start(bf16[1856,128]{1,0:T(8,128)(2,1)S(1)} %broadcast_in_dim.37), channel_id=1, source_target_pairs={{0,48},{16,0},{32,16},{48,32},{1,49},{17,1},{33,17},{49,33},{2,50}... | collective-permute-start | bytes 1425416 | tf_op jit(solution)/shard_map/ppermute | solution.py:21
  103.5 0.0 collective-permute-done.7
  103.5 0.1 maximum_select_fusion.2
  103.6 0.1 select_n.131
  103.7 0.1 reverse_select_fusion.1
  103.8 0.1 reverse_select_fusion
  103.9 4.0 %collective-permute-done.5 = bf16[1856,128]{1,0:T(8,128)(2,1)S(1)} collective-permute-done((bf16[1856,128]{1,0:T(8,128)(2,1)S(1)}, bf16[1856,128]{1,0:T(8,128)(2,1)S(1)}, u32[]{:S(2)}, u32[]{:S(2)}) %collective-permute-start.5) | collective-permute-done | bytes 475168 | tf_op jit(solution)/shard_map/ppermute | solution.py:21
  107.9 2.2 %collective-permute-done.6 = bf16[1856,128]{1,0:T(8,128)(2,1)S(1)} collective-permute-done((bf16[1856,128]{1,0:T(8,128)(2,1)S(1)}, bf16[1856,128]{1,0:T(8,128)(2,1)S(1)}, u32[]{:S(2)}, u32[]{:S(2)}) %collective-permute-start.6) | collective-permute-done | bytes 475168 | tf_op jit(solution)/shard_map/ppermute | solution.py:21
  110.1 1.2 pad_maximum_fusion
  111.3 3.6 %collective-permute-start.8 = (bf16[2784,128]{1,0:T(8,128)(2,1)}, bf16[2784,128]{1,0:T(8,128)(2,1)}, u32[]{:S(2)}, u32[]{:S(2)}) collective-permute-start(bf16[2784,128]{1,0:T(8,128)(2,1)} %get-tuple-element.45), channel_id=1, source_target_pairs={{0,16},{16,32},{32,48},{48,0},{1,17},{17,33},{33,49},{49,1},{2,18}... | collective-permute-start | bytes 2138120 | tf_op jit(solution)/shard_map/ppermute | solution.py:21
  115.0 2.8 %collective-permute-start.9 = (bf16[2784,128]{1,0:T(8,128)(2,1)}, bf16[2784,128]{1,0:T(8,128)(2,1)}, u32[]{:S(2)}, u32[]{:S(2)}) collective-permute-start(bf16[2784,128]{1,0:T(8,128)(2,1)} %get-tuple-element.44), channel_id=1, source_target_pairs={{0,48},{16,0},{32,16},{48,32},{1,49},{17,1},{33,17},{49,33},{2,50}... | collective-permute-start | bytes 2138120 | tf_op jit(solution)/shard_map/ppermute | solution.py:21
  117.8 0.0 collective-permute-done.10
  117.9 1.1 broadcast_in_dim.42
  118.9 4.3 %all-to-all-start = ((bf16[4,2,464,128]{3,2,1,0:T(8,128)(2,1)}), bf16[4,2,464,128]{3,2,1,0:T(8,128)(2,1)S(1)}, u32[]{:S(2)}, u32[]{:S(2)}) async-start(bf16[4,2,464,128]{3,2,1,0:T(8,128)(2,1)} %broadcast_in_dim.42), calls=%async_computation | async-start | bytes 1900544 | tf_op jit(solution)/shard_map/all_to_all | solution.py:31
  123.3 1.5 broadcast_in_dim.38
  124.8 0.8 bitcast_dynamic-update-slice_fusion.1
  125.6 0.0 collective-permute-done.8
  125.6 2.0 %collective-permute-done.9 = bf16[2784,128]{1,0:T(8,128)(2,1)} collective-permute-done((bf16[2784,128]{1,0:T(8,128)(2,1)}, bf16[2784,128]{1,0:T(8,128)(2,1)}, u32[]{:S(2)}, u32[]{:S(2)}) %collective-permute-start.9) | collective-permute-done | bytes 712736 | tf_op jit(solution)/shard_map/ppermute | solution.py:21
  127.5 1.2 fusion.13
  128.8 1.2 fusion.12
  130.0 3.8 %collective-permute-start.13 = (bf16[928,128]{1,0:T(8,128)(2,1)S(1)}, bf16[928,128]{1,0:T(8,128)(2,1)}, u32[]{:S(2)}, u32[]{:S(2)}) collective-permute-start(bf16[928,128]{1,0:T(8,128)(2,1)S(1)} %get-tuple-element.38), channel_id=1, source_target_pairs={{0,48},{16,0},{32,16},{48,32},{1,49},{17,1},{33,17},{49,33},{2,50}... | collective-permute-start | bytes 712712 | tf_op jit(solution)/shard_map/ppermute | solution.py:21
  133.7 1.9 %collective-permute-start.12 = (bf16[928,128]{1,0:T(8,128)(2,1)S(1)}, bf16[928,128]{1,0:T(8,128)(2,1)}, u32[]{:S(2)}, u32[]{:S(2)}) collective-permute-start(bf16[928,128]{1,0:T(8,128)(2,1)S(1)} %get-tuple-element.34), channel_id=1, source_target_pairs={{0,16},{16,32},{32,48},{48,0},{1,17},{17,33},{33,49},{49,1},{2,18}... | collective-permute-start | bytes 712712 | tf_op jit(solution)/shard_map/ppermute | solution.py:21
  135.7 0.9 fusion.7
  136.5 0.8 bitcast_dynamic-update-slice_fusion
  137.4 0.0 all-to-all-done
  137.4 15.7 %collective-permute-start.11 = (bf16[4,2,464,128]{3,2,1,0:T(8,128)(2,1)S(1)}, bf16[4,2,464,128]{3,2,1,0:T(8,128)(2,1)S(1)}, u32[]{:S(2)}, u32[]{:S(2)}) collective-permute-start(bf16[4,2,464,128]{3,2,1,0:T(8,128)(2,1)S(1)} %all-to-all-done), channel_id=1, source_target_pairs={{0,64},{64,0},{1,65},{65,1},{2,66},{66,2},{3,67},{67,3},{4,68},{68... | collective-permute-start | bytes 2850824 | tf_op jit(solution)/shard_map/ppermute | solution.py:21
  153.1 6.1 %fusion.15 = f32[128,464]{0,1:T(8,128)} fusion(bf16[464,7424]{1,0:T(8,128)(2,1)} %param.5, bf16[7424,128]{1,0:T(8,128)(2,1)} %bitcast.20), kind=kOutput, calls=%fused_computation.41 | convolution fusion | flops 881852416 | bytes 9027584 | tf_op jit(solution)/shard_map/dot_general | solution.py:99
  159.2 0.1 broadcast_in_dim.46
  159.4 0.1 broadcast_in_dim.44
  159.5 0.1 fusion.10
  159.6 0.0 collective-permute-done.13
  159.6 0.0 collective-permute-done.12
  159.6 1.1 constant_dynamic-update-slice_fusion.1
  160.8 0.0 collective-permute-done.11
  160.8 0.1 fusion.11
  160.9 0.7 convolution_bitcast_fusion
  161.6 1.6 fusion
  (16 shorter events, 0.4 us)
Async XLA Ops:
  0.6 12.0 %collective-permute-start = (bf16[116,128]{1,0:T(8,128)(2,1)}, bf16[116,128]{1,0:T(8,128)(2,1)S(1)}, u32[]{:S(2)}, u32[]{:S(2)}) collective-permute-start(bf16[116,128]{1,0:T(8,128)(2,1)} %bitcast.75), channel_id=1, source_target_pairs={{0,0},{1,1},{2,2},{3,3},{4,64},{5,65},{6,66},{7,67},{8,128},{9,129... | collective-permute-start | bytes 89096 | tf_op jit(solution)/shard_map/ppermute | solution.py:21
  12.6 33.6 %collective-permute-start.1 = (bf16[232,128]{1,0:T(8,128)(2,1)S(1)}, bf16[232,128]{1,0:T(8,128)(2,1)S(1)}, u32[]{:S(2)}, u32[]{:S(2)}) collective-permute-start(bf16[232,128]{1,0:T(8,128)(2,1)S(1)} %pad_maximum_fusion.3), channel_id=1, source_target_pairs={{0,8},{1,9},{2,10},{3,11},{4,12},{5,13},{6,14},{7,15},{8,0},{9,1},... | collective-permute-start | bytes 178184 | tf_op jit(solution)/shard_map/ppermute | solution.py:21
  46.3 14.7 %collective-permute-start.2 = (bf16[2,2,116,128]{3,2,0,1:T(8,128)(2,1)S(1)}, bf16[2,2,116,128]{3,2,0,1:T(8,128)(2,1)S(1)}, u32[]{:S(2)}, u32[]{:S(2)}) collective-permute-start(bf16[2,2,116,128]{3,2,0,1:T(8,128)(2,1)S(1)} %bitcast.65), channel_id=1, source_target_pairs={{0,4},{1,5},{2,6},{3,7},{4,0},{5,1},{6,2},{7,3},{8,12},{9,13},{10,... | collective-permute-start | bytes 356360 | tf_op jit(solution)/shard_map/ppermute | solution.py:21
  61.0 20.3 %copy-start = (bf16[128,464]{0,1:T(8,128)(2,1)S(1)}, bf16[128,464]{0,1:T(8,128)(2,1)}, u32[]{:S(2)}) copy-start(bf16[128,464]{0,1:T(8,128)(2,1)} %param.4) | copy-start | bytes 356356
  61.0 9.9 %collective-permute-start.3 = (bf16[2,2,2,116,128]{4,3,0,1,2:T(8,128)(2,1)S(1)}, bf16[2,2,2,116,128]{4,3,0,1,2:T(8,128)(2,1)S(1)}, u32[]{:S(2)}, u32[]{:S(2)}) collective-permute-start(bf16[2,2,2,116,128]{4,3,0,1,2:T(8,128)(2,1)S(1)} %maximum_select_fusion.3), channel_id=1, source_target_pairs={{0,2},{1,3},{2,0},{3,1},{4,6},{5,7},{6,4},{7,5},{8,10},{9,11},{10,... | collective-permute-start | bytes 712712 | tf_op jit(solution)/shard_map/ppermute | solution.py:21
  71.1 7.9 %collective-permute-start.4 = (bf16[2,2,2,116,128]{4,3,0,1,2:T(8,128)(2,1)S(1)}, bf16[2,2,2,116,128]{4,3,0,1,2:T(8,128)(2,1)S(1)}, u32[]{:S(2)}, u32[]{:S(2)}) collective-permute-start(bf16[2,2,2,116,128]{4,3,0,1,2:T(8,128)(2,1)S(1)} %get-tuple-element.41), channel_id=1, source_target_pairs={{0,1},{1,0},{2,3},{3,2},{4,5},{5,4},{6,7},{7,6},{8,9},{9,8},{10,11... | collective-permute-start | bytes 712712 | tf_op jit(solution)/shard_map/ppermute | solution.py:21
  79.0 24.4 %collective-permute-start.7 = (bf16[2,2,2,116,128]{4,3,0,1,2:T(8,128)(2,1)S(1)}, bf16[2,2,2,116,128]{4,3,0,1,2:T(8,128)(2,1)S(1)}, u32[]{:S(2)}, u32[]{:S(2)}) collective-permute-start(bf16[2,2,2,116,128]{4,3,0,1,2:T(8,128)(2,1)S(1)} %slice_bitcast_fusion), channel_id=1, source_target_pairs={{0,1},{1,0},{2,3},{3,2},{4,5},{5,4},{6,7},{7,6},{8,9},{9,8},{10,11... | collective-permute-start | bytes 712712 | tf_op jit(solution)/shard_map/ppermute | solution.py:21
  81.3 36.5 %collective-permute-start.10 = (bf16[464,128]{1,0:T(8,128)(2,1)S(1)}, bf16[464,128]{1,0:T(8,128)(2,1)S(1)}, u32[]{:S(2)}, u32[]{:S(2)}) collective-permute-start(bf16[464,128]{1,0:T(8,128)(2,1)S(1)} %bitcast.71), channel_id=1, source_target_pairs={{0,128},{128,0},{1,129},{129,1},{2,130},{130,2},{3,131},{131,3},{4... | collective-permute-start | bytes 356360 | tf_op jit(solution)/shard_map/ppermute | solution.py:21
  92.9 15.0 %collective-permute-start.5 = (bf16[1856,128]{1,0:T(8,128)(2,1)S(1)}, bf16[1856,128]{1,0:T(8,128)(2,1)S(1)}, u32[]{:S(2)}, u32[]{:S(2)}) collective-permute-start(bf16[1856,128]{1,0:T(8,128)(2,1)S(1)} %broadcast_in_dim.37), channel_id=1, source_target_pairs={{0,16},{16,32},{32,48},{48,0},{1,17},{17,33},{33,49},{49,1},{2,18}... | collective-permute-start | bytes 1425416 | tf_op jit(solution)/shard_map/ppermute | solution.py:21
  97.9 12.2 %collective-permute-start.6 = (bf16[1856,128]{1,0:T(8,128)(2,1)S(1)}, bf16[1856,128]{1,0:T(8,128)(2,1)S(1)}, u32[]{:S(2)}, u32[]{:S(2)}) collective-permute-start(bf16[1856,128]{1,0:T(8,128)(2,1)S(1)} %broadcast_in_dim.37), channel_id=1, source_target_pairs={{0,48},{16,0},{32,16},{48,32},{1,49},{17,1},{33,17},{49,33},{2,50}... | collective-permute-start | bytes 1425416 | tf_op jit(solution)/shard_map/ppermute | solution.py:21
  111.3 14.3 %collective-permute-start.8 = (bf16[2784,128]{1,0:T(8,128)(2,1)}, bf16[2784,128]{1,0:T(8,128)(2,1)}, u32[]{:S(2)}, u32[]{:S(2)}) collective-permute-start(bf16[2784,128]{1,0:T(8,128)(2,1)} %get-tuple-element.45), channel_id=1, source_target_pairs={{0,16},{16,32},{32,48},{48,0},{1,17},{17,33},{33,49},{49,1},{2,18}... | collective-permute-start | bytes 2138120 | tf_op jit(solution)/shard_map/ppermute | solution.py:21
  115.0 12.6 %collective-permute-start.9 = (bf16[2784,128]{1,0:T(8,128)(2,1)}, bf16[2784,128]{1,0:T(8,128)(2,1)}, u32[]{:S(2)}, u32[]{:S(2)}) collective-permute-start(bf16[2784,128]{1,0:T(8,128)(2,1)} %get-tuple-element.44), channel_id=1, source_target_pairs={{0,48},{16,0},{32,16},{48,32},{1,49},{17,1},{33,17},{49,33},{2,50}... | collective-permute-start | bytes 2138120 | tf_op jit(solution)/shard_map/ppermute | solution.py:21
  118.9 18.4 %all-to-all-start = ((bf16[4,2,464,128]{3,2,1,0:T(8,128)(2,1)}), bf16[4,2,464,128]{3,2,1,0:T(8,128)(2,1)S(1)}, u32[]{:S(2)}, u32[]{:S(2)}) async-start(bf16[4,2,464,128]{3,2,1,0:T(8,128)(2,1)} %broadcast_in_dim.42), calls=%async_computation | async-start | bytes 1900544 | tf_op jit(solution)/shard_map/all_to_all | solution.py:31
  130.0 29.6 %collective-permute-start.13 = (bf16[928,128]{1,0:T(8,128)(2,1)S(1)}, bf16[928,128]{1,0:T(8,128)(2,1)}, u32[]{:S(2)}, u32[]{:S(2)}) collective-permute-start(bf16[928,128]{1,0:T(8,128)(2,1)S(1)} %get-tuple-element.38), channel_id=1, source_target_pairs={{0,48},{16,0},{32,16},{48,32},{1,49},{17,1},{33,17},{49,33},{2,50}... | collective-permute-start | bytes 712712 | tf_op jit(solution)/shard_map/ppermute | solution.py:21
  133.7 25.9 %collective-permute-start.12 = (bf16[928,128]{1,0:T(8,128)(2,1)S(1)}, bf16[928,128]{1,0:T(8,128)(2,1)}, u32[]{:S(2)}, u32[]{:S(2)}) collective-permute-start(bf16[928,128]{1,0:T(8,128)(2,1)S(1)} %get-tuple-element.34), channel_id=1, source_target_pairs={{0,16},{16,32},{32,48},{48,0},{1,17},{17,33},{33,49},{49,1},{2,18}... | collective-permute-start | bytes 712712 | tf_op jit(solution)/shard_map/ppermute | solution.py:21
  137.4 23.5 %collective-permute-start.11 = (bf16[4,2,464,128]{3,2,1,0:T(8,128)(2,1)S(1)}, bf16[4,2,464,128]{3,2,1,0:T(8,128)(2,1)S(1)}, u32[]{:S(2)}, u32[]{:S(2)}) collective-permute-start(bf16[4,2,464,128]{3,2,1,0:T(8,128)(2,1)S(1)} %all-to-all-done), channel_id=1, source_target_pairs={{0,64},{64,0},{1,65},{65,1},{2,66},{66,2},{3,67},{67,3},{4,68},{68... | collective-permute-start | bytes 2850824 | tf_op jit(solution)/shard_map/ppermute | solution.py:21

commit v13 on v12

--- a/solution.py
+++ b/solution.py
@@ -74,7 +74,7 @@
     both, a = sync((paired(both, 2, 3), a))
     far = permute(a, ("zh",), lambda h: (1 - h,))
 
-    rows, part = sync((paired(both[0], 3, 3), both[1]))
+    rows, part = paired(both[0], 3, 3), both[1]
     rows = rows.reshape(16 * cols, tokens)
 
     rows_b, rows_a = along_y(rows, 1), along_y(rows, -1)

time: 165 us -> 161 us (0.976)
  the two profiles are of different devices: /device:TPU:1 before, /device:TPU:287 now
where the time goes in v13:
time: 161 us; the launch traced here: 160 us
  waiting for transfers between devices  79.1 us (49%)
  starting transfers between devices  61.3 us (38%)
  matrix products  7.93 us (5%)
  local copies, waits for them, and re-layouts  7.61 us (5%)
  other arithmetic  2.65 us (2%)
    ppermute x14, waiting for transfers between devices, permute(): return lax.ppermute(value, axes, pairs)  79.1 us
    ppermute x14, starting transfers between devices, permute(): return lax.ppermute(value, axes, pairs)  57.3 us
    dot_general x1, matrix products, per_device(): lax.dot_general(weight_codes, rows, (((1,), (0,)), ((), ())), preferred_e...  5.64 us
    all_to_all x1, starting transfers between devices, spread(): return lax.all_to_all(copies, axis, 0, 0, tiled=True)  3.94 us
  transfers between devices with their start and end apart: 15, of which 10 were waited for; matrix products, arithmetic and copies ran while one was open for 10% of the time, Pallas kernels for 0%

profile of v13, /device:TPU:287, one launch (start us, length us, event | category | flops | bytes accessed | tf_op | source)
XLA Modules:
  0.0 159.7 jit_solution(9634568472875715083)
XLA Ops:
  0.6 17.8 %collective-permute-start = (bf16[116,128]{1,0:T(8,128)(2,1)}, bf16[116,128]{1,0:T(8,128)(2,1)S(1)}, u32[]{:S(2)}, u32[]{:S(2)}) collective-permute-start(bf16[116,128]{1,0:T(8,128)(2,1)} %bitcast.76), channel_id=1, source_target_pairs={{0,0},{1,1},{2,2},{3,3},{4,64},{5,65},{6,66},{7,67},{8,128},{9,129... | collective-permute-start | bytes 89096 | tf_op jit(solution)/shard_map/ppermute | solution.py:21
  18.5 0.8 dynamic_slice.3
  19.3 0.8 multiply_convert_fusion
  20.1 0.1 collective-permute-done
  20.3 0.0 copy-start
  20.3 2.1 %collective-permute-start.1 = (bf16[232,128]{1,0:T(8,128)(2,1)S(1)}, bf16[232,128]{1,0:T(8,128)(2,1)S(1)}, u32[]{:S(2)}, u32[]{:S(2)}) collective-permute-start(bf16[232,128]{1,0:T(8,128)(2,1)S(1)} %pad_maximum_fusion.3), channel_id=1, source_target_pairs={{0,8},{1,9},{2,10},{3,11},{4,12},{5,13},{6,14},{7,15},{8,0},{9,1},... | collective-permute-start | bytes 178184 | tf_op jit(solution)/shard_map/ppermute | solution.py:21
  22.3 11.9 %collective-permute-done.1 = bf16[232,128]{1,0:T(8,128)(2,1)S(1)} collective-permute-done((bf16[232,128]{1,0:T(8,128)(2,1)S(1)}, bf16[232,128]{1,0:T(8,128)(2,1)S(1)}, u32[]{:S(2)}, u32[]{:S(2)}) %collective-permute-start.1) | collective-permute-done | bytes 59424 | tf_op jit(solution)/shard_map/ppermute | solution.py:21
  34.3 3.1 %collective-permute-start.2 = (bf16[2,2,116,128]{3,2,0,1:T(8,128)(2,1)S(1)}, bf16[2,2,116,128]{3,2,0,1:T(8,128)(2,1)S(1)}, u32[]{:S(2)}, u32[]{:S(2)}) collective-permute-start(bf16[2,2,116,128]{3,2,0,1:T(8,128)(2,1)S(1)} %bitcast.66), channel_id=1, source_target_pairs={{0,4},{1,5},{2,6},{3,7},{4,0},{5,1},{6,2},{7,3},{8,12},{9,13},{10,... | collective-permute-start | bytes 356360 | tf_op jit(solution)/shard_map/ppermute | solution.py:21
  37.4 15.5 %collective-permute-done.2 = bf16[2,2,116,128]{3,2,0,1:T(8,128)(2,1)S(1)} collective-permute-done((bf16[2,2,116,128]{3,2,0,1:T(8,128)(2,1)S(1)}, bf16[2,2,116,128]{3,2,0,1:T(8,128)(2,1)S(1)}, u32[]{:S(2)}, u32[]{:S(2)}) %collective-permute-start.2) | collective-permute-done | bytes 118816 | tf_op jit(solution)/shard_map/ppermute | solution.py:21
  53.0 1.9 %collective-permute-start.3 = (bf16[2,2,2,116,128]{4,3,0,1,2:T(8,128)(2,1)S(1)}, bf16[2,2,2,116,128]{4,3,0,1,2:T(8,128)(2,1)S(1)}, u32[]{:S(2)}, u32[]{:S(2)}) collective-permute-start(bf16[2,2,2,116,128]{4,3,0,1,2:T(8,128)(2,1)S(1)} %maximum_select_fusion.3), channel_id=1, source_target_pairs={{0,2},{1,3},{2,0},{3,1},{4,6},{5,7},{6,4},{7,5},{8,10},{9,11},{10,... | collective-permute-start | bytes 712712 | tf_op jit(solution)/shard_map/ppermute | solution.py:21
  54.9 13.3 %collective-permute-done.3 = bf16[2,2,2,116,128]{4,3,0,1,2:T(8,128)(2,1)S(1)} collective-permute-done((bf16[2,2,2,116,128]{4,3,0,1,2:T(8,128)(2,1)S(1)}, bf16[2,2,2,116,128]{4,3,0,1,2:T(8,128)(2,1)S(1)}, u32[]{:S(2)}, u32[]{:S(2)}) %collective-permute-start.3) | collective-permute-done | bytes 237600 | tf_op jit(solution)/shard_map/ppermute | solution.py:21
  68.2 0.1 maximum_select_fusion
  68.3 0.1 slice_bitcast_fusion.1
  68.4 0.1 slice_bitcast_fusion.3
  68.4 1.9 %collective-permute-start.4 = (bf16[2,2,2,116,128]{4,3,0,1,2:T(8,128)(2,1)S(1)}, bf16[2,2,2,116,128]{4,3,0,1,2:T(8,128)(2,1)S(1)}, u32[]{:S(2)}, u32[]{:S(2)}) collective-permute-start(bf16[2,2,2,116,128]{4,3,0,1,2:T(8,128)(2,1)S(1)} %get-tuple-element.39), channel_id=1, source_target_pairs={{0,1},{1,0},{2,3},{3,2},{4,5},{5,4},{6,7},{7,6},{8,9},{9,8},{10,11... | collective-permute-start | bytes 712712 | tf_op jit(solution)/shard_map/ppermute | solution.py:21
  70.4 3.4 %collective-permute-start.7 = (bf16[2,2,2,116,128]{4,3,0,1,2:T(8,128)(2,1)S(1)}, bf16[2,2,2,116,128]{4,3,0,1,2:T(8,128)(2,1)S(1)}, u32[]{:S(2)}, u32[]{:S(2)}) collective-permute-start(bf16[2,2,2,116,128]{4,3,0,1,2:T(8,128)(2,1)S(1)} %get-tuple-element.37), channel_id=1, source_target_pairs={{0,1},{1,0},{2,3},{3,2},{4,5},{5,4},{6,7},{7,6},{8,9},{9,8},{10,11... | collective-permute-start | bytes 712712 | tf_op jit(solution)/shard_map/ppermute | solution.py:21
  73.8 0.0 copy-done
  73.8 1.9 %collective-permute-start.10 = (bf16[464,128]{1,0:T(8,128)(2,1)S(1)}, bf16[464,128]{1,0:T(8,128)(2,1)S(1)}, u32[]{:S(2)}, u32[]{:S(2)}) collective-permute-start(bf16[464,128]{1,0:T(8,128)(2,1)S(1)} %bitcast.72), channel_id=1, source_target_pairs={{0,128},{128,0},{1,129},{129,1},{2,130},{130,2},{3,131},{131,3},{4... | collective-permute-start | bytes 356360 | tf_op jit(solution)/shard_map/ppermute | solution.py:21
  75.7 1.6 %collective-permute-done.4 = bf16[2,2,2,116,128]{4,3,0,1,2:T(8,128)(2,1)S(1)} collective-permute-done((bf16[2,2,2,116,128]{4,3,0,1,2:T(8,128)(2,1)S(1)}, bf16[2,2,2,116,128]{4,3,0,1,2:T(8,128)(2,1)S(1)}, u32[]{:S(2)}, u32[]{:S(2)}) %collective-permute-start.4) | collective-permute-done | bytes 237600 | tf_op jit(solution)/shard_map/ppermute | solution.py:21
  77.4 21.4 %collective-permute-done.7 = bf16[2,2,2,116,128]{4,3,0,1,2:T(8,128)(2,1)S(1)} collective-permute-done((bf16[2,2,2,116,128]{4,3,0,1,2:T(8,128)(2,1)S(1)}, bf16[2,2,2,116,128]{4,3,0,1,2:T(8,128)(2,1)S(1)}, u32[]{:S(2)}, u32[]{:S(2)}) %collective-permute-start.7) | collective-permute-done | bytes 237600 | tf_op jit(solution)/shard_map/ppermute | solution.py:21
  98.8 0.1 maximum_select_fusion.1
  99.0 0.1 select_n.136
  99.1 1.9 %collective-permute-start.5 = (bf16[1856,128]{1,0:T(8,128)(2,1)S(1)}, bf16[1856,128]{1,0:T(8,128)(2,1)S(1)}, u32[]{:S(2)}, u32[]{:S(2)}) collective-permute-start(bf16[1856,128]{1,0:T(8,128)(2,1)S(1)} %select_n.136), channel_id=1, source_target_pairs={{0,16},{16,32},{32,48},{48,0},{1,17},{17,33},{33,49},{49,1},{2,18}... | collective-permute-start | bytes 1425416 | tf_op jit(solution)/shard_map/ppermute | solution.py:21
  101.0 3.4 %collective-permute-start.6 = (bf16[1856,128]{1,0:T(8,128)(2,1)S(1)}, bf16[1856,128]{1,0:T(8,128)(2,1)S(1)}, u32[]{:S(2)}, u32[]{:S(2)}) collective-permute-start(bf16[1856,128]{1,0:T(8,128)(2,1)S(1)} %select_n.136), channel_id=1, source_target_pairs={{0,48},{16,0},{32,16},{48,32},{1,49},{17,1},{33,17},{49,33},{2,50}... | collective-permute-start | bytes 1425416 | tf_op jit(solution)/shard_map/ppermute | solution.py:21
  104.5 0.1 select_n.140
  104.6 0.1 reverse_select_fusion.1
  104.7 0.1 reverse_select_fusion
  104.8 4.7 %collective-permute-done.5 = bf16[1856,128]{1,0:T(8,128)(2,1)S(1)} collective-permute-done((bf16[1856,128]{1,0:T(8,128)(2,1)S(1)}, bf16[1856,128]{1,0:T(8,128)(2,1)S(1)}, u32[]{:S(2)}, u32[]{:S(2)}) %collective-permute-start.5) | collective-permute-done | bytes 475168 | tf_op jit(solution)/shard_map/ppermute | solution.py:21
  109.5 3.1 %collective-permute-done.6 = bf16[1856,128]{1,0:T(8,128)(2,1)S(1)} collective-permute-done((bf16[1856,128]{1,0:T(8,128)(2,1)S(1)}, bf16[1856,128]{1,0:T(8,128)(2,1)S(1)}, u32[]{:S(2)}, u32[]{:S(2)}) %collective-permute-start.6) | collective-permute-done | bytes 475168 | tf_op jit(solution)/shard_map/ppermute | solution.py:21
  112.6 1.2 pad_maximum_fusion
  113.9 1.9 %collective-permute-start.8 = (bf16[2784,128]{1,0:T(8,128)(2,1)}, bf16[2784,128]{1,0:T(8,128)(2,1)}, u32[]{:S(2)}, u32[]{:S(2)}) collective-permute-start(bf16[2784,128]{1,0:T(8,128)(2,1)} %get-tuple-element.43), channel_id=1, source_target_pairs={{0,16},{16,32},{32,48},{48,0},{1,17},{17,33},{33,49},{49,1},{2,18}... | collective-permute-start | bytes 2138120 | tf_op jit(solution)/shard_map/ppermute | solution.py:21
  115.8 3.4 %collective-permute-start.9 = (bf16[2784,128]{1,0:T(8,128)(2,1)}, bf16[2784,128]{1,0:T(8,128)(2,1)}, u32[]{:S(2)}, u32[]{:S(2)}) collective-permute-start(bf16[2784,128]{1,0:T(8,128)(2,1)} %get-tuple-element.42), channel_id=1, source_target_pairs={{0,48},{16,0},{32,16},{48,32},{1,49},{17,1},{33,17},{49,33},{2,50}... | collective-permute-start | bytes 2138120 | tf_op jit(solution)/shard_map/ppermute | solution.py:21
  119.2 0.0 collective-permute-done.10
  119.2 1.1 broadcast_in_dim.39
  120.3 3.9 %all-to-all-start = ((bf16[4,2,464,128]{3,2,1,0:T(8,128)(2,1)}), bf16[4,2,464,128]{3,2,1,0:T(8,128)(2,1)S(1)}, u32[]{:S(2)}, u32[]{:S(2)}) async-start(bf16[4,2,464,128]{3,2,1,0:T(8,128)(2,1)} %broadcast_in_dim.39), calls=%async_computation | async-start | bytes 1900544 | tf_op jit(solution)/shard_map/all_to_all | solution.py:31
  124.2 0.2 broadcast_in_dim.35
  124.5 0.1 bitcast_dynamic-update-slice_fusion.1
  124.6 4.1 %collective-permute-done.8 = bf16[2784,128]{1,0:T(8,128)(2,1)} collective-permute-done((bf16[2784,128]{1,0:T(8,128)(2,1)}, bf16[2784,128]{1,0:T(8,128)(2,1)}, u32[]{:S(2)}, u32[]{:S(2)}) %collective-permute-start.8) | collective-permute-done | bytes 712736 | tf_op jit(solution)/shard_map/ppermute | solution.py:21
  128.7 3.1 %collective-permute-done.9 = bf16[2784,128]{1,0:T(8,128)(2,1)} collective-permute-done((bf16[2784,128]{1,0:T(8,128)(2,1)}, bf16[2784,128]{1,0:T(8,128)(2,1)}, u32[]{:S(2)}, u32[]{:S(2)}) %collective-permute-start.9) | collective-permute-done | bytes 712736 | tf_op jit(solution)/shard_map/ppermute | solution.py:21
  131.8 1.2 fusion.13
  133.1 1.2 fusion.12
  134.3 1.9 %collective-permute-start.13 = (bf16[928,128]{1,0:T(8,128)(2,1)S(1)}, bf16[928,128]{1,0:T(8,128)(2,1)}, u32[]{:S(2)}, u32[]{:S(2)}) collective-permute-start(bf16[928,128]{1,0:T(8,128)(2,1)S(1)} %get-tuple-element.34), channel_id=1, source_target_pairs={{0,48},{16,0},{32,16},{48,32},{1,49},{17,1},{33,17},{49,33},{2,50}... | collective-permute-start | bytes 712712 | tf_op jit(solution)/shard_map/ppermute | solution.py:21
  136.2 4.6 %collective-permute-start.12 = (bf16[928,128]{1,0:T(8,128)(2,1)S(1)}, bf16[928,128]{1,0:T(8,128)(2,1)}, u32[]{:S(2)}, u32[]{:S(2)}) collective-permute-start(bf16[928,128]{1,0:T(8,128)(2,1)S(1)} %get-tuple-element.30), channel_id=1, source_target_pairs={{0,16},{16,32},{32,48},{48,0},{1,17},{17,33},{33,49},{49,1},{2,18}... | collective-permute-start | bytes 712712 | tf_op jit(solution)/shard_map/ppermute | solution.py:21
  140.8 0.1 fusion.7
  140.9 0.1 bitcast_dynamic-update-slice_fusion
  140.9 5.6 %fusion.15 = f32[128,464]{0,1:T(8,128)} fusion(bf16[464,7424]{1,0:T(8,128)(2,1)} %param.5, bf16[7424,128]{1,0:T(8,128)(2,1)S(1)} %bitcast.58), kind=kOutput, calls=%fused_computation.42 | convolution fusion | flops 881852416 | bytes 9027584 | tf_op jit(solution)/shard_map/dot_general | solution.py:99
  146.6 0.0 all-to-all-done
  146.6 8.2 %collective-permute-start.11 = (bf16[4,2,464,128]{3,2,1,0:T(8,128)(2,1)S(1)}, bf16[4,2,464,128]{3,2,1,0:T(8,128)(2,1)S(1)}, u32[]{:S(2)}, u32[]{:S(2)}) collective-permute-start(bf16[4,2,464,128]{3,2,1,0:T(8,128)(2,1)S(1)} %all-to-all-done), channel_id=1, source_target_pairs={{0,64},{64,0},{1,65},{65,1},{2,66},{66,2},{3,67},{67,3},{4,68},{68... | collective-permute-start | bytes 2850824 | tf_op jit(solution)/shard_map/ppermute | solution.py:21
  154.8 0.1 fusion.10
  154.9 0.1 broadcast_in_dim.43
  155.0 0.1 broadcast_in_dim.41
  155.2 0.0 collective-permute-done.13
  155.2 1.0 constant_dynamic-update-slice_fusion.1
  156.3 0.0 collective-permute-done.12
  156.3 1.0 constant_dynamic-update-slice_fusion.4
  157.3 0.0 collective-permute-done.11
  157.3 0.1 fusion.11
  157.4 0.7 convolution_bitcast_fusion
  158.1 1.6 %fusion = f32[464,464]{1,0:T(8,128)} fusion(f32[464,464]{1,0:T(8,128)S(1)} %convolution_bitcast_fusion, bf16[4,2,464,128]{3,2,1,0:T(8,128)(2,1)S(1)} %constant_dynamic-update-slice_fusion.3, bf16[4,1,464,128]{3,2,1,0:T(8,128)(2,1)S(1)} %get-tuple-element.28, bf16[4,1,464,128]{3,2,1,0:T(8,128)(2,1)S(1)} %get-tuple-element.26), kind=kOutput, calls=%fused_computation.2 | convolution fusion | flops 441616640 | bytes 3622912 | tf_op jit(solution)/shard_map/dot_general | solution.py:105
  (15 shorter events, 0.4 us)
Async XLA Ops:
  0.6 19.6 %collective-permute-start = (bf16[116,128]{1,0:T(8,128)(2,1)}, bf16[116,128]{1,0:T(8,128)(2,1)S(1)}, u32[]{:S(2)}, u32[]{:S(2)}) collective-permute-start(bf16[116,128]{1,0:T(8,128)(2,1)} %bitcast.76), channel_id=1, source_target_pairs={{0,0},{1,1},{2,2},{3,3},{4,64},{5,65},{6,66},{7,67},{8,128},{9,129... | collective-permute-start | bytes 89096 | tf_op jit(solution)/shard_map/ppermute | solution.py:21
  20.3 53.6 %copy-start = (bf16[128,464]{0,1:T(8,128)(2,1)S(1)}, bf16[128,464]{0,1:T(8,128)(2,1)}, u32[]{:S(2)}) copy-start(bf16[128,464]{0,1:T(8,128)(2,1)} %param.4) | copy-start | bytes 356356
  20.3 14.0 %collective-permute-start.1 = (bf16[232,128]{1,0:T(8,128)(2,1)S(1)}, bf16[232,128]{1,0:T(8,128)(2,1)S(1)}, u32[]{:S(2)}, u32[]{:S(2)}) collective-permute-start(bf16[232,128]{1,0:T(8,128)(2,1)S(1)} %pad_maximum_fusion.3), channel_id=1, source_target_pairs={{0,8},{1,9},{2,10},{3,11},{4,12},{5,13},{6,14},{7,15},{8,0},{9,1},... | collective-permute-start | bytes 178184 | tf_op jit(solution)/shard_map/ppermute | solution.py:21
  34.3 18.6 %collective-permute-start.2 = (bf16[2,2,116,128]{3,2,0,1:T(8,128)(2,1)S(1)}, bf16[2,2,116,128]{3,2,0,1:T(8,128)(2,1)S(1)}, u32[]{:S(2)}, u32[]{:S(2)}) collective-permute-start(bf16[2,2,116,128]{3,2,0,1:T(8,128)(2,1)S(1)} %bitcast.66), channel_id=1, source_target_pairs={{0,4},{1,5},{2,6},{3,7},{4,0},{5,1},{6,2},{7,3},{8,12},{9,13},{10,... | collective-permute-start | bytes 356360 | tf_op jit(solution)/shard_map/ppermute | solution.py:21
  53.0 15.3 %collective-permute-start.3 = (bf16[2,2,2,116,128]{4,3,0,1,2:T(8,128)(2,1)S(1)}, bf16[2,2,2,116,128]{4,3,0,1,2:T(8,128)(2,1)S(1)}, u32[]{:S(2)}, u32[]{:S(2)}) collective-permute-start(bf16[2,2,2,116,128]{4,3,0,1,2:T(8,128)(2,1)S(1)} %maximum_select_fusion.3), channel_id=1, source_target_pairs={{0,2},{1,3},{2,0},{3,1},{4,6},{5,7},{6,4},{7,5},{8,10},{9,11},{10,... | collective-permute-start | bytes 712712 | tf_op jit(solution)/shard_map/ppermute | solution.py:21
  68.4 8.9 %collective-permute-start.4 = (bf16[2,2,2,116,128]{4,3,0,1,2:T(8,128)(2,1)S(1)}, bf16[2,2,2,116,128]{4,3,0,1,2:T(8,128)(2,1)S(1)}, u32[]{:S(2)}, u32[]{:S(2)}) collective-permute-start(bf16[2,2,2,116,128]{4,3,0,1,2:T(8,128)(2,1)S(1)} %get-tuple-element.39), channel_id=1, source_target_pairs={{0,1},{1,0},{2,3},{3,2},{4,5},{5,4},{6,7},{7,6},{8,9},{9,8},{10,11... | collective-permute-start | bytes 712712 | tf_op jit(solution)/shard_map/ppermute | solution.py:21
  70.4 28.4 %collective-permute-start.7 = (bf16[2,2,2,116,128]{4,3,0,1,2:T(8,128)(2,1)S(1)}, bf16[2,2,2,116,128]{4,3,0,1,2:T(8,128)(2,1)S(1)}, u32[]{:S(2)}, u32[]{:S(2)}) collective-permute-start(bf16[2,2,2,116,128]{4,3,0,1,2:T(8,128)(2,1)S(1)} %get-tuple-element.37), channel_id=1, source_target_pairs={{0,1},{1,0},{2,3},{3,2},{4,5},{5,4},{6,7},{7,6},{8,9},{9,8},{10,11... | collective-permute-start | bytes 712712 | tf_op jit(solution)/shard_map/ppermute | solution.py:21
  73.8 45.3 %collective-permute-start.10 = (bf16[464,128]{1,0:T(8,128)(2,1)S(1)}, bf16[464,128]{1,0:T(8,128)(2,1)S(1)}, u32[]{:S(2)}, u32[]{:S(2)}) collective-permute-start(bf16[464,128]{1,0:T(8,128)(2,1)S(1)} %bitcast.72), channel_id=1, source_target_pairs={{0,128},{128,0},{1,129},{129,1},{2,130},{130,2},{3,131},{131,3},{4... | collective-permute-start | bytes 356360 | tf_op jit(solution)/shard_map/ppermute | solution.py:21
  99.1 10.3 %collective-permute-start.5 = (bf16[1856,128]{1,0:T(8,128)(2,1)S(1)}, bf16[1856,128]{1,0:T(8,128)(2,1)S(1)}, u32[]{:S(2)}, u32[]{:S(2)}) collective-permute-start(bf16[1856,128]{1,0:T(8,128)(2,1)S(1)} %select_n.136), channel_id=1, source_target_pairs={{0,16},{16,32},{32,48},{48,0},{1,17},{17,33},{33,49},{49,1},{2,18}... | collective-permute-start | bytes 1425416 | tf_op jit(solution)/shard_map/ppermute | solution.py:21
  101.0 11.6 %collective-permute-start.6 = (bf16[1856,128]{1,0:T(8,128)(2,1)S(1)}, bf16[1856,128]{1,0:T(8,128)(2,1)S(1)}, u32[]{:S(2)}, u32[]{:S(2)}) collective-permute-start(bf16[1856,128]{1,0:T(8,128)(2,1)S(1)} %select_n.136), channel_id=1, source_target_pairs={{0,48},{16,0},{32,16},{48,32},{1,49},{17,1},{33,17},{49,33},{2,50}... | collective-permute-start | bytes 1425416 | tf_op jit(solution)/shard_map/ppermute | solution.py:21
  113.9 14.8 %collective-permute-start.8 = (bf16[2784,128]{1,0:T(8,128)(2,1)}, bf16[2784,128]{1,0:T(8,128)(2,1)}, u32[]{:S(2)}, u32[]{:S(2)}) collective-permute-start(bf16[2784,128]{1,0:T(8,128)(2,1)} %get-tuple-element.43), channel_id=1, source_target_pairs={{0,16},{16,32},{32,48},{48,0},{1,17},{17,33},{33,49},{49,1},{2,18}... | collective-permute-start | bytes 2138120 | tf_op jit(solution)/shard_map/ppermute | solution.py:21
  115.8 16.0 %collective-permute-start.9 = (bf16[2784,128]{1,0:T(8,128)(2,1)}, bf16[2784,128]{1,0:T(8,128)(2,1)}, u32[]{:S(2)}, u32[]{:S(2)}) collective-permute-start(bf16[2784,128]{1,0:T(8,128)(2,1)} %get-tuple-element.42), channel_id=1, source_target_pairs={{0,48},{16,0},{32,16},{48,32},{1,49},{17,1},{33,17},{49,33},{2,50}... | collective-permute-start | bytes 2138120 | tf_op jit(solution)/shard_map/ppermute | solution.py:21
  120.3 26.3 %all-to-all-start = ((bf16[4,2,464,128]{3,2,1,0:T(8,128)(2,1)}), bf16[4,2,464,128]{3,2,1,0:T(8,128)(2,1)S(1)}, u32[]{:S(2)}, u32[]{:S(2)}) async-start(bf16[4,2,464,128]{3,2,1,0:T(8,128)(2,1)} %broadcast_in_dim.39), calls=%async_computation | async-start | bytes 1900544 | tf_op jit(solution)/shard_map/all_to_all | solution.py:31
  134.3 20.9 %collective-permute-start.13 = (bf16[928,128]{1,0:T(8,128)(2,1)S(1)}, bf16[928,128]{1,0:T(8,128)(2,1)}, u32[]{:S(2)}, u32[]{:S(2)}) collective-permute-start(bf16[928,128]{1,0:T(8,128)(2,1)S(1)} %get-tuple-element.34), channel_id=1, source_target_pairs={{0,48},{16,0},{32,16},{48,32},{1,49},{17,1},{33,17},{49,33},{2,50}... | collective-permute-start | bytes 712712 | tf_op jit(solution)/shard_map/ppermute | solution.py:21
  136.2 20.1 %collective-permute-start.12 = (bf16[928,128]{1,0:T(8,128)(2,1)S(1)}, bf16[928,128]{1,0:T(8,128)(2,1)}, u32[]{:S(2)}, u32[]{:S(2)}) collective-permute-start(bf16[928,128]{1,0:T(8,128)(2,1)S(1)} %get-tuple-element.30), channel_id=1, source_target_pairs={{0,16},{16,32},{32,48},{48,0},{1,17},{17,33},{33,49},{49,1},{2,18}... | collective-permute-start | bytes 712712 | tf_op jit(solution)/shard_map/ppermute | solution.py:21
  146.6 10.7 %collective-permute-start.11 = (bf16[4,2,464,128]{3,2,1,0:T(8,128)(2,1)S(1)}, bf16[4,2,464,128]{3,2,1,0:T(8,128)(2,1)S(1)}, u32[]{:S(2)}, u32[]{:S(2)}) collective-permute-start(bf16[4,2,464,128]{3,2,1,0:T(8,128)(2,1)S(1)} %all-to-all-done), channel_id=1, source_target_pairs={{0,64},{64,0},{1,65},{65,1},{2,66},{66,2},{3,67},{67,3},{4,68},{68... | collective-permute-start | bytes 2850824 | tf_op jit(solution)/shard_map/ppermute | solution.py:21
